TPU v7x, 512 devices: a whole 4x8x8 slice. The times are simulated.
512 devices in a mesh: rep: 8 (over z), mp: 64 (over y, x, core).
Axes of the slice: x: 4, y: 8, z: 8, core: 2. Of those that a mesh axis runs over, the one named last changes fastest.
Arguments:
- pooled_grad: bfloat16 [65536, 8, 256], P(('rep', 'mp')), may hold values from -6 to 6
- owner_ids: int32 [65536, 8, 2, 1], P(('rep', 'mp')), may hold values from 0 to 63; in each aligned block of 2048 rows (0 to 2047, 2048 to 4095, ..., all dimensions but the last counted through in order) at most 48 rows name the same one
- local_ids: int32 [65536, 8, 2], P(('rep', 'mp')), may hold values from 0 to 1023
- feature_table: int32 [8], replicated, may hold values from 0 to 1
- table_rows: bfloat16 [2, 65536, 256], P(None, 'mp'), may hold values from -6 to 6
- adagrad_state: float32 [2, 65536], P(None, 'mp'), may hold values from 0.01 to 1
Outputs:
- new_tables: bfloat16 [2, 65536, 256], P(None, 'mp')
- new_state: float32 [2, 65536], P(None, 'mp')
Inputs may be any that keep to these rules, and one draw needn't show every extreme that they name: `owner_ids`: among the lookups of one device, at most 48 name any one owner, and in every draw some owner is named by exactly 48 of them.
All inputs are finite; a program needn't handle non-finite values.
Results may differ from a plain program's by a relative error of at most 0.0034.
Values may be sent and summed in bfloat16 or wider, within the bound.
No kernel may reach another device: no remote copies, remote signals or barrier semaphores. Data moves between devices by JAX's collectives and lax.ppermute only.
A program may use at most 64 MiB of HBM per device.

v0:
```python
import jax
import jax.numpy as jnp
from jax import lax
from jax.sharding import PartitionSpec as P


def shards(pooled_grad, owner_ids, local_ids, feature_table, table_rows, adagrad_state):
    samples, features, embed = pooled_grad.shape
    pool = local_ids.shape[2]
    tables, rows_dev = adagrad_state.shape
    owners = lax.axis_size("mp")
    replicas = lax.axis_size("rep")
    slots = tables * rows_dev
    count = samples * features * pool
    capacity = 3 * count // (2 * owners)
    owner_list = owner_ids[..., 0].reshape(-1)
    target = (feature_table[None, :, None] * rows_dev + local_ids).reshape(-1)
    owner_hot = owner_list[:, None] == jnp.arange(owners, dtype=jnp.int32)[None, :]
    lookup_pos = jnp.arange(count, dtype=jnp.int32)
    lower = (lookup_pos[:, None] >= lookup_pos[None, :]).astype(jnp.bfloat16)
    running = jnp.dot(lower, owner_hot.astype(jnp.bfloat16), preferred_element_type=jnp.float32)
    position = jnp.sum(jnp.where(owner_hot, running, 0.0), axis=1).astype(jnp.int32) - 1
    slot_of = owner_list * capacity + position
    slot_pos = jnp.arange(owners * capacity, dtype=jnp.int32)
    chosen = slot_pos[:, None] == slot_of[None, :]
    valid = jnp.any(chosen, axis=1)
    send_ids = jnp.where(valid, jnp.sum(jnp.where(chosen, target[None, :], 0), axis=1), slots)
    pick_rows = jnp.sum(
        chosen.reshape(owners * capacity, count // pool, pool).astype(jnp.bfloat16), axis=2
    )
    send_rows = jnp.dot(
        pick_rows, pooled_grad.reshape(-1, embed), preferred_element_type=jnp.float32
    ).astype(jnp.bfloat16)
    received, received_ids = (
        lax.all_to_all(
            send_rows.reshape(owners, capacity, embed),
            "mp",
            split_axis=0,
            concat_axis=0,
            tiled=True,
        ),
        lax.all_to_all(
            send_ids.reshape(owners, capacity), "mp", split_axis=0, concat_axis=0, tiled=True
        ),
    )
    row_hot = (jnp.arange(slots, dtype=jnp.int32)[:, None] == received_ids.reshape(1, -1)).astype(
        jnp.bfloat16
    )
    row_grad = jnp.dot(row_hot, received.reshape(-1, embed), preferred_element_type=jnp.float32)
    row_grad = row_grad.reshape(tables, rows_dev, embed)
    state = adagrad_state + jnp.mean(row_grad * row_grad, axis=2)
    updated = (
        table_rows.astype(jnp.float32) - 0.3 * row_grad / jnp.sqrt(state)[:, :, None]
    ).astype(jnp.bfloat16)
    widened = lax.optimization_barrier(updated).astype(jnp.float32)
    table_sum, state_sum = lax.psum((widened, state), "rep")
    return ((table_sum / replicas).astype(jnp.bfloat16), state_sum / replicas)


def solution(mesh):
    placed = (
        P(("rep", "mp"), None, None),
        P(("rep", "mp"), None, None, None),
        P(("rep", "mp"), None, None),
        P(),
        P(None, "mp", None),
        P(None, "mp"),
    )
    return jax.shard_map(
        shards,
        mesh=mesh,
        in_specs=placed,
        out_specs=(P(None, "mp", None), P(None, "mp")),
        check_vma=False,
    )
```

profile of v0, /device:TPU:6, one launch (start us, length us, event | category | flops | bytes accessed | tf_op | source)
XLA Modules:
  0.0 169.7 jit_solution(17874390085583121371)
XLA Ops:
  0.7 1.0 copy.29
  1.7 0.3 reshape_squeeze.3
  1.9 1.7 fusion.9
  3.6 3.1 %fusion = pred[3072]{0:T(1024)(128)(4,1)S(1)} fusion(s32[2048]{0:T(1024)S(1)} %get-tuple-element.14), kind=kLoop, calls=%fused_computation.3 | loop fusion | flops 12579840 | bytes 11264 | tf_op jit(solution)/shard_map/reduce_or | solution.py:26
  6.8 0.3 copy.30
  7.1 0.3 broadcast_in_dim.31
  7.4 2.6 %select_reduce_fusion = s32[3072]{0:T(1024)S(1)} fusion(s32[2048]{0:T(1024)S(1)} %broadcast_in_dim.31, s32[2048]{0:T(1024)S(1)} %get-tuple-element.14), kind=kLoop, calls=%fused_computation.1 | loop fusion | flops 18871296 | bytes 28672 | tf_op jit(solution)/shard_map/reduce_sum | solution.py:27
  10.0 0.7 select_n.26
  10.7 10.6 %all-to-all-start = ((s32[64,1,48]{2,1,0:T(1,128)}), s32[64,1,48]{2,1,0:T(1,128)S(1)}, u32[]{:S(2)}, u32[]{:S(2)}) async-start(s32[64,1,48]{2,1,0:T(1,128)} %bitcast), calls=%async_computation | async-start | bytes 65536 | tf_op jit(solution)/shard_map/all_to_all | solution.py:42
  21.6 0.5 sub.10
  22.0 0.2 copy.33
  22.2 9.3 %fusion.5 = bf16[3072,1024]{1,0:T(8,128)(2,1)} fusion(s32[1024,2]{0,1:T(2,128)S(1)} %add.39), kind=kLoop, calls=%fused_computation.9 | loop fusion | flops 15728640 | bytes 6299648 | tf_op jit(solution)/shard_map/reduce_sum | solution.py:28
  31.5 5.7 %convolution_convert_fusion = bf16[3072,256]{1,0:T(8,128)(2,1)} fusion(bf16[3072,1024]{1,0:T(8,128)(2,1)} %fusion.5, bf16[128,8,256]{2,1,0:T(8,128)(2,1)S(1)} %copy-done), kind=kOutput, calls=%fused_computation.12 | convolution fusion | flops 1611399168 | bytes 8388608 | tf_op jit(solution)/shard_map/dot_general | solution.py:31
  37.3 10.3 %all-to-all-start.1 = ((bf16[64,48,256]{2,1,0:T(8,128)(2,1)}), bf16[64,48,256]{2,1,0:T(8,128)(2,1)S(1)}, u32[]{:S(2)}, u32[]{:S(2)}) async-start(bf16[64,48,256]{2,1,0:T(8,128)(2,1)} %bitcast.19), calls=%async_computation.1 | async-start | bytes 3145728 | tf_op jit(solution)/shard_map/all_to_all | solution.py:35
  47.6 1.5 copy.28
  49.1 0.5 broadcast.68
  49.6 0.7 reduce.4
  50.4 37.2 %all-to-all-done.1 = bf16[64,48,256]{2,1,0:T(8,128)(2,1)S(1)} async-done(((bf16[64,48,256]{2,1,0:T(8,128)(2,1)}), bf16[64,48,256]{2,1,0:T(8,128)(2,1)S(1)}, u32[]{:S(2)}, u32[]{:S(2)}) %all-to-all-start.1) | async-done | bytes 1572896 | tf_op jit(solution)/shard_map/all_to_all | solution.py:35
  87.6 5.0 %multiply_reduce_fusion = (f32[2,1024]{1,0:T(2,128)S(1)}, f32[2,1024,256]{1,2,0:T(8,128)S(1)}) fusion(bf16[3072,256,1]{1,0,2:T(8,128)(2,1)S(1)} %bitcast.18, s32[3072]{0:T(1024)S(1)} %eq.69, s32[2,1024]{1,0:T(2,128)S(1)} %multiply_add_fusion.2), kind=kOutput, calls=%fused_computation.16 | convolution fusion | flops 3228563456 | bytes 3698688 | tf_op jit(solution)/shard_map/dot_general | solution.py:49
  92.7 0.4 subtract_convert_fusion
  93.1 72.9 %all-reduce.2 = (f32[2,1024,256]{1,2,0:T(8,128)}, f32[2,1024]{1,0:T(2,128)S(1)}) all-reduce(bf16[2,1024,256]{1,2,0:T(8,128)(2,1)S(1)} %subtract_convert_fusion, f32[2,1024]{1,0:T(2,128)S(1)} %get-tuple-element.13), channel_id=1, replica_groups=mesh['rep'=8,'mp'=64] {'rep'}, use_global_device_ids=true, to_apply=%region_5.6 | all-reduce | flops 526336 | bytes 3162112 | tf_op jit(solution)/shard_map/psum | solution.py:56
  166.0 1.8 %multiply_convert_fusion = bf16[2,1024,256]{1,2,0:T(8,128)(2,1)S(1)} fusion(f32[2,1024,256]{1,2,0:T(8,128)} %get-tuple-element.10), kind=kLoop, calls=%fused_computation.14 | loop fusion | flops 1048576 | bytes 3145728 | tf_op jit(solution)/shard_map/convert_element_type | solution.py:57
  167.8 1.3 copy.35
  169.1 0.6 broadcast_multiply_fusion
  (22 shorter events, 0.5 us)
Async XLA Ops:
  0.6 30.9 %copy-start = (bf16[128,8,256]{2,1,0:T(8,128)(2,1)S(1)}, bf16[128,8,256]{2,1,0:T(8,128)(2,1)}, u32[]{:S(2)}) copy-start(bf16[128,8,256]{2,1,0:T(8,128)(2,1)} %param.6) | copy-start | bytes 1572868
  0.6 20.6 %copy-start.1 = (s32[128,8,2,1]{0,3,2,1:T(1,128)S(1)}, s32[128,8,2,1]{0,3,2,1:T(1,128)}, u32[]{:S(2)}) copy-start(s32[128,8,2,1]{0,3,2,1:T(1,128)} %param.7) | copy-start | bytes 24580
  0.7 6.1 %copy-start.4 = (s32[8]{0:T(128)S(1)}, s32[8]{0:T(128)}, u32[]{:S(2)}) copy-start(s32[8]{0:T(128)} %param.9) | copy-start | bytes 100
  0.7 6.1 %copy-start.2 = (s32[128,8,2]{0,2,1:T(2,128)S(1)}, s32[128,8,2]{0,2,1:T(2,128)}, u32[]{:S(2)}) copy-start(s32[128,8,2]{0,2,1:T(2,128)} %param.8) | copy-start | bytes 24580
  10.7 26.6 %all-to-all-start = ((s32[64,1,48]{2,1,0:T(1,128)}), s32[64,1,48]{2,1,0:T(1,128)S(1)}, u32[]{:S(2)}, u32[]{:S(2)}) async-start(s32[64,1,48]{2,1,0:T(1,128)} %bitcast), calls=%async_computation | async-start | bytes 65536 | tf_op jit(solution)/shard_map/all_to_all | solution.py:42
  37.3 50.4 %all-to-all-start.1 = ((bf16[64,48,256]{2,1,0:T(8,128)(2,1)}), bf16[64,48,256]{2,1,0:T(8,128)(2,1)S(1)}, u32[]{:S(2)}, u32[]{:S(2)}) async-start(bf16[64,48,256]{2,1,0:T(8,128)(2,1)} %bitcast.19), calls=%async_computation.1 | async-start | bytes 3145728 | tf_op jit(solution)/shard_map/all_to_all | solution.py:35
  87.6 5.0 %copy-start.3 = (f32[2,1024]{1,0:T(2,128)S(1)}, f32[2,1024]{1,0:T(2,128)}, u32[]{:S(2)}) copy-start(f32[2,1024]{1,0:T(2,128)} %param.11) | copy-start | bytes 24580
where the time goes:
time: 170 us
  blocking collectives  72.9 us (43%)
  waiting for transfers between devices  37.2 us (22%)
  starting transfers between devices  20.9 us (12%)
  other arithmetic  18.7 us (11%)
  matrix products  12.4 us (7%)
  local copies, waits for them, and re-layouts  6.79 us (4%)
    psum x1, blocking collectives, shards(): table_sum, state_sum = lax.psum((widened, state), 'rep')  72.9 us
    all_to_all x1, waiting for transfers between devices, shards(): lax.all_to_all(send_rows.reshape(owners, capacity, embed), 'mp', split_ax...  37.2 us
    all_to_all x1, starting transfers between devices, shards(): lax.all_to_all(send_ids.reshape(owners, capacity), 'mp', split_axis=0, co...  10.6 us
    all_to_all x1, starting transfers between devices, shards(): lax.all_to_all(send_rows.reshape(owners, capacity, embed), 'mp', split_ax...  10.3 us
    reduce_sum x1, other arithmetic, shards(): jnp.sum(chosen.reshape(owners * capacity, count // pool, pool).astype(jnp...  9.31 us
    dot_general x1, matrix products, shards(): jnp.dot(pick_rows, pooled_grad.reshape(-1, embed), preferred_element_type...  5.73 us
    dot_general x1, matrix products, shards(): jnp.dot(row_hot, received.reshape(-1, embed), preferred_element_type=jnp....  4.99 us
    unnamed x13, local copies, waits for them, and re-layouts  3.81 us
  transfers between devices with their start and end apart: 2, of which 1 were waited for; matrix products, arithmetic and copies ran while one was open for 11% of the time, Pallas kernels for 0%

commit v1 on v0

v1 whole, which is shorter than its diff:
```python
import jax
import jax.numpy as jnp
from jax import lax
from jax.experimental import pallas as pl
from jax.experimental.pallas import tpu as pltpu
from jax.sharding import PartitionSpec as P

BF = jnp.bfloat16
F32 = jnp.float32
LANES = 128
IDS = 8


def iota(shape, dim):
    return lax.broadcasted_iota(jnp.int32, shape, dim)


def split3(x):
    hi = x.astype(BF).astype(F32)
    mid = (x - hi).astype(BF).astype(F32)
    return hi, mid, x - hi - mid


def pack_kernel(owners, cap, rows_dev, mine, tables_ref, owner_ref, local_ref, grad_ref, out_ref):
    lists, samples = owner_ref.shape
    features = tables_ref.shape[0]
    pool = lists // features
    count = grad_ref.shape[0]
    owner = owner_ref[...]
    table = jnp.zeros((lists, samples), jnp.int32)
    for f in range(features):
        table = jnp.where(iota((lists, samples), 0) // pool == f, tables_ref[f], table)
    target = table * rows_dev + local_ref[...]

    low = iota((samples, 2 * samples), 0)
    col = iota((samples, 2 * samples), 1)
    tri = jnp.where((low <= col), 1.0, 0.0).astype(BF)
    hot = [iota((owners, samples), 0) == owner[r : r + 1, :] for r in range(lists)]
    stacked = jnp.concatenate([jnp.where(h, 1.0, 0.0) for h in hot], axis=0).astype(BF)
    counts = jnp.dot(stacked, tri, preferred_element_type=F32)
    carry = jnp.zeros((owners, samples), F32)
    places = []
    for r in range(lists):
        block = counts[r * owners : (r + 1) * owners]
        running = block[:, :samples] + carry
        places.append(jnp.sum(jnp.where(hot[r], running, 0.0), axis=0, keepdims=True) - 1.0)
        carry = carry + block[:, samples:]
    place = jnp.concatenate(places, axis=0)

    spread = (iota((samples, count), 1) // features == iota((samples, count), 0))
    spread = jnp.where(spread, 1.0, 0.0).astype(BF)
    both = jnp.concatenate([owner.astype(F32), place], axis=0).astype(BF)
    wide = jnp.dot(both, spread, preferred_element_type=F32)
    slots = []
    lane_f = iota((lists, count), 1) % features
    for p in range(pool):
        keep = iota((lists, count), 0) == lane_f * pool + p
        slot = wide[:lists] * cap + wide[lists:]
        slots.append(jnp.sum(jnp.where(keep, slot, 0.0), axis=0, keepdims=True).astype(jnp.int32))

    grad = grad_ref[...]
    group = 8
    for g in range(owners // group):
        rows = group * cap
        index = iota((rows, count), 0) + g * rows
        chosen = index == slots[0]
        for p in range(1, pool):
            chosen = chosen | (index == slots[p])
        picked = jnp.dot(jnp.where(chosen, 1.0, 0.0).astype(BF), grad, preferred_element_type=F32)
        picked = picked.astype(BF)
        for k in range(group):
            part = picked[k * cap : (k + 1) * cap]
            out_ref[g * group + k, 0:cap, :] = part[:, :LANES]
            out_ref[g * group + k, cap : 2 * cap, :] = part[:, LANES:]

    shift = (lax.axis_index("mp") % 8) * cap
    lane = place.astype(jnp.int32) + shift
    chunk = lane // LANES
    low_id = (target % 64).astype(F32)
    high_id = (target // 64).astype(F32)
    left, right = [], []
    kind = iota((IDS, samples), 0)
    for r in range(lists):
        row = slice(r, r + 1)
        value = jnp.where(kind < 3, low_id[row], high_id[row])
        value = jnp.where((kind % 3 == chunk[row]) & (kind < 6), value, 0.0)
        blocks = [jnp.where(owner[row] == o, value, 0.0) for o in range(owners)]
        left.append(jnp.concatenate(blocks, axis=0).astype(BF))
        right.append(jnp.where(lane[row] % LANES == iota((LANES, samples), 0), 1.0, 0.0).astype(BF))
    ids = lax.dot_general(
        jnp.concatenate(left, axis=1),
        jnp.concatenate(right, axis=1),
        (((1,), (1,)), ((), ())),
        preferred_element_type=F32,
    )
    out_ref[:, 2 * cap : 2 * cap + IDS, :] = ids.reshape(owners, IDS, LANES).astype(BF)


def update_kernel(cap, shards, recv_ref, table_ref, state_ref, out_ref):
    senders = recv_ref.shape[0]
    rows = table_ref.shape[0]
    part = rows // shards
    ids = recv_ref[:, 2 * cap : 2 * cap + IDS, :].astype(F32)
    ids = jnp.sum(ids.reshape(senders // 8, 8, IDS, LANES), axis=1)
    group = 16
    where, data = [], []
    for g in range(senders // group):
        lanes = []
        for h in range(group // 8):
            x = ids[g * (group // 8) + h]
            lanes += [x[j : j + 1] + 64.0 * x[j + 3 : j + 4] for j in range(3)]
        where.append(jnp.concatenate(lanes, axis=1).astype(jnp.int32))
        block = recv_ref[g * group : (g + 1) * group, 0 : 2 * cap, :]
        halves = [
            block[:, h * cap : (h + 1) * cap, :].reshape(group * cap, LANES) for h in range(2)
        ]
        data.append(jnp.concatenate(halves, axis=1))
    state = jnp.transpose(state_ref[...])
    for k in range(shards):
        total = jnp.zeros((part, 2 * LANES), F32)
        for g in range(senders // group):
            hot = iota((part, group * cap), 0) + k * part == where[g]
            hot = jnp.where(hot, 1.0, 0.0).astype(BF)
            total = total + jnp.dot(hot, data[g], preferred_element_type=F32)
        square = jnp.sum(total * total, axis=1, keepdims=True) * (1.0 / (2 * LANES))
        columns = []
        for b in range(part // LANES):
            at = k * (part // LANES) + b
            columns.append(state[:, at : at + 1] + square[b * LANES : (b + 1) * LANES])
        new = jnp.concatenate(columns, axis=0)
        old = table_ref[k * part : (k + 1) * part, :].astype(F32)
        out_ref[k, 0:part, :] = (old - 0.3 * total / jnp.sqrt(new)).astype(BF)
        wide = [jnp.transpose(jnp.broadcast_to(c, (LANES, LANES)))[0:IDS] for c in columns]
        wide = jnp.concatenate(wide, axis=1)
        hi, mid, lo = split3(wide)
        kind = iota((IDS, 2 * LANES), 0)
        parts = jnp.where(kind == 0, hi, jnp.where(kind == 1, mid, jnp.where(kind == 2, lo, 0.0)))
        out_ref[k, part : part + IDS, :] = parts.astype(BF)


def average_kernel(got_ref, out_ref):
    replicas, rows, embed = got_ref.shape
    part = rows - IDS
    total = got_ref[0].astype(F32)
    for r in range(1, replicas):
        total = total + got_ref[r].astype(F32)
    total = total * (1.0 / replicas)
    table = total[:part].astype(BF)
    state = total[part : part + 1] + total[part + 1 : part + 2] + total[part + 2 : part + 3]
    hi, mid, lo = split3(jnp.broadcast_to(state, (IDS, embed)))
    kind = iota((IDS, embed), 0)
    parts = jnp.where(kind == 0, hi, jnp.where(kind == 1, mid, jnp.where(kind == 2, lo, 0.0)))
    parts = parts.astype(BF)
    for r in range(replicas):
        out_ref[r, 0:part, :] = table
        out_ref[r, part:rows, :] = parts


def unpack_kernel(got_ref, table_ref, state_ref):
    shards, rows, embed = got_ref.shape
    part = rows - IDS
    for k in range(shards):
        table_ref[k * part : (k + 1) * part, :] = got_ref[k, 0:part, :]
        parts = got_ref[k, part:rows, :].astype(F32)
        state = parts[0:1] + parts[1:2] + parts[2:3]
        state_ref[k : k + 1, :] = state


PARAMS = pltpu.CompilerParams(vmem_limit_bytes=40 * 2**20)
VMEM = pl.BlockSpec(memory_space=pltpu.VMEM)
SMEM = pl.BlockSpec(memory_space=pltpu.SMEM)


def shards_fn(pooled_grad, owner_ids, local_ids, feature_table, table_rows, adagrad_state):
    samples, features, embed = pooled_grad.shape
    pool = local_ids.shape[2]
    tables, rows_dev = adagrad_state.shape
    owners = lax.axis_size("mp")
    replicas = lax.axis_size("rep")
    slots = tables * rows_dev
    count = samples * features * pool
    cap = 3 * count // (2 * owners)
    part = slots // replicas
    owner = jnp.transpose(owner_ids[..., 0], (1, 2, 0)).reshape(features * pool, samples)
    local = jnp.transpose(local_ids, (1, 2, 0)).reshape(features * pool, samples)
    send = pl.pallas_call(
        lambda *refs: pack_kernel(owners, cap, rows_dev, None, *refs),
        out_shape=jax.ShapeDtypeStruct((owners, 2 * cap + IDS, LANES), BF),
        in_specs=[SMEM, VMEM, VMEM, VMEM],
        out_specs=VMEM,
        compiler_params=PARAMS,
        name="pack",
    )(feature_table, owner, local, pooled_grad.reshape(samples * features, embed))
    received = lax.all_to_all(send, "mp", split_axis=0, concat_axis=0, tiled=True)
    updated = pl.pallas_call(
        lambda *refs: update_kernel(cap, replicas, *refs),
        out_shape=jax.ShapeDtypeStruct((replicas, part + IDS, embed), BF),
        in_specs=[VMEM, VMEM, VMEM],
        out_specs=VMEM,
        compiler_params=PARAMS,
        name="update",
    )(received, table_rows.reshape(slots, embed), adagrad_state.reshape(slots // LANES, LANES))
    mine = lax.all_to_all(updated, "rep", split_axis=0, concat_axis=0, tiled=True)
    copies = pl.pallas_call(
        average_kernel,
        out_shape=jax.ShapeDtypeStruct((replicas, part + IDS, embed), BF),
        in_specs=[VMEM],
        out_specs=VMEM,
        compiler_params=PARAMS,
        name="average",
    )(mine)
    full = lax.all_to_all(copies, "rep", split_axis=0, concat_axis=0, tiled=True)
    table, state = pl.pallas_call(
        unpack_kernel,
        out_shape=(
            jax.ShapeDtypeStruct((slots, embed), BF),
            jax.ShapeDtypeStruct((replicas, part), F32),
        ),
        in_specs=[VMEM],
        out_specs=(VMEM, VMEM),
        compiler_params=PARAMS,
        name="unpack",
    )(full)
    return table.reshape(tables, rows_dev, embed), state.reshape(tables, rows_dev)


def solution(mesh):
    placed = (
        P(("rep", "mp"), None, None),
        P(("rep", "mp"), None, None, None),
        P(("rep", "mp"), None, None),
        P(),
        P(None, "mp", None),
        P(None, "mp"),
    )
    return jax.shard_map(
        shards_fn,
        mesh=mesh,
        in_specs=placed,
        out_specs=(P(None, "mp", None), P(None, "mp")),
        check_vma=False,
    )
```

time: 170 us -> 139 us (0.82)
  the two profiles are of different devices: /device:TPU:6 before, /device:TPU:18 now
where the time goes in v1:
time: 139 us
  blocking collectives  72.4 us (52%)
  waiting for transfers between devices  40.8 us (29%)
  Pallas kernels  10.9 us (8%)
  starting transfers between devices  10.6 us (8%)
  local copies, waits for them, and re-layouts  3.71 us (3%)
    all_to_all x1, waiting for transfers between devices, shards_fn(): lax.all_to_all(send, 'mp', split_axis=0, concat_axis=0, tiled=True)  40.8 us
    all_to_all x1, blocking collectives, shards_fn(): lax.all_to_all(updated, 'rep', split_axis=0, concat_axis=0, tiled=True)  40.5 us
    all_to_all x1, blocking collectives, shards_fn(): lax.all_to_all(copies, 'rep', split_axis=0, concat_axis=0, tiled=True)  31.9 us
    all_to_all x1, starting transfers between devices, shards_fn(): lax.all_to_all(send, 'mp', split_axis=0, concat_axis=0, tiled=True)  10.6 us
    pallas_call x1, Pallas kernels, shards_fn(): pl.pallas_call(lambda *refs: pack_kernel(owners, cap, rows_dev, None, *re...  5.55 us
    pallas_call x1, Pallas kernels, shards_fn(): pl.pallas_call(lambda *refs: update_kernel(cap, replicas, *refs), out_sha...  4.13 us
    unnamed x12, local copies, waits for them, and re-layouts  3.09 us
  transfers between devices with their start and end apart: 1, of which 1 were waited for; matrix products, arithmetic and copies ran while one was open for 0% of the time, Pallas kernels for 0%

profile of v1, /device:TPU:18, one launch (start us, length us, event | category | flops | bytes accessed | tf_op | source)
XLA Modules:
  0.0 139.0 jit_solution(7065488665777616840)
XLA Ops:
  0.6 0.0 copy-start.1
  0.6 1.0 copy-done.1
  1.7 0.0 copy-start.2
  1.7 0.7 copy-done.2
  2.4 0.0 copy-start.3
  2.4 0.7 copy-done.3
  3.1 0.0 copy-start.4
  3.1 0.7 copy-done.4
  3.7 5.5 %pack.1 = bf16[64,104,128]{2,1,0:T(8,128)(2,1)} custom-call(s32[8]{0:T(128)S(1)} %copy-done.4, s32[16,128]{1,0:T(8,128)S(1)} %bitcast.13, s32[16,128]{1,0:T(8,128)S(1)} %bitcast.14, bf16[1024,256]{1,0:T(8,128)(2,1)S(1)} %bitcast.12), custom_call_target="tpu_custom_call" | custom-call | tf_op jit(solution)/shard_map/pack/pallas_call | solution.py:186
  9.3 0.0 copy-start.5
  9.3 0.0 copy-start
  9.3 10.6 %all-to-all-start = ((bf16[64,104,128]{2,1,0:T(8,128)(2,1)}), bf16[64,104,128]{2,1,0:T(8,128)(2,1)S(1)}, u32[]{:S(2)}, u32[]{:S(2)}) async-start(bf16[64,104,128]{2,1,0:T(8,128)(2,1)} %pack.1), calls=%async_computation | async-start | bytes 3407872 | tf_op jit(solution)/shard_map/all_to_all | solution.py:194
  19.8 0.0 copy-done.5
  19.9 40.8 %all-to-all-done.refs_0_ = bf16[64,104,128]{2,1,0:T(8,128)(2,1)S(1)} async-done(((bf16[64,104,128]{2,1,0:T(8,128)(2,1)}), bf16[64,104,128]{2,1,0:T(8,128)(2,1)S(1)}, u32[]{:S(2)}, u32[]{:S(2)}) %all-to-all-start) | async-done | bytes 1703968 | tf_op jit(solution)/shard_map/all_to_all | solution.py:194
  60.6 0.0 copy-done
  60.6 4.1 %update.1 = bf16[8,264,256]{2,1,0:T(8,128)(2,1)S(1)} custom-call(bf16[64,104,128]{2,1,0:T(8,128)(2,1)S(1)} %all-to-all-done.refs_0_, bf16[2048,256]{1,0:T(8,128)(2,1)S(1)} %bitcast.11, f32[16,128]{1,0:T(8,128)S(1)} %reshape.29.refs_2_), custom_call_target="tpu_custom_call" | custom-call | tf_op jit(solution)/shard_map/update/pallas_call | solution.py:195
  64.8 40.5 %all_to_all.15.got_ref = bf16[8,264,256]{2,1,0:T(8,128)(2,1)S(1)} all-to-all(bf16[8,264,256]{2,1,0:T(8,128)(2,1)S(1)} %update.1), channel_id=1, replica_groups=mesh['rep'=8,'mp'=64] {'rep'}, dimensions={0} | all-to-all | bytes 2162688 | tf_op jit(solution)/shard_map/all_to_all | solution.py:203
  105.2 0.2 average.1
  105.4 31.9 %all_to_all.16.got_ref = bf16[8,264,256]{2,1,0:T(8,128)(2,1)S(1)} all-to-all(bf16[8,264,256]{2,1,0:T(8,128)(2,1)S(1)} %average.1), channel_id=1, replica_groups=mesh['rep'=8,'mp'=64] {'rep'}, dimensions={0} | all-to-all | bytes 2162688 | tf_op jit(solution)/shard_map/all_to_all | solution.py:212
  137.4 1.0 unpack.1
  138.4 0.6 reshape.31
  (1 shorter events, 0.0 us)
Async XLA Ops:
  0.6 1.0 copy-start.1
  1.7 0.7 copy-start.2
  2.4 0.7 copy-start.3
  3.1 0.7 copy-start.4
  9.3 10.6 %copy-start.5 = (f32[2,1024]{1,0:T(2,128)S(1)}, f32[2,1024]{1,0:T(2,128)}, u32[]{:S(2)}) copy-start(f32[2,1024]{1,0:T(2,128)} %param.11) | copy-start | bytes 24580
  9.3 51.4 %copy-start = (bf16[2,1024,256]{2,1,0:T(8,128)(2,1)S(1)}, bf16[2,1024,256]{2,1,0:T(8,128)(2,1)}, u32[]{:S(2)}) copy-start(bf16[2,1024,256]{2,1,0:T(8,128)(2,1)} %param.10) | copy-start | bytes 3145732
  9.3 51.4 %all-to-all-start = ((bf16[64,104,128]{2,1,0:T(8,128)(2,1)}), bf16[64,104,128]{2,1,0:T(8,128)(2,1)S(1)}, u32[]{:S(2)}, u32[]{:S(2)}) async-start(bf16[64,104,128]{2,1,0:T(8,128)(2,1)} %pack.1), calls=%async_computation | async-start | bytes 3407872 | tf_op jit(solution)/shard_map/all_to_all | solution.py:194

commit v2 on v1

v2 whole, which is shorter than its diff:
```python
import jax
import jax.numpy as jnp
from jax import lax
from jax.experimental import pallas as pl
from jax.experimental.pallas import tpu as pltpu
from jax.sharding import PartitionSpec as P

BF = jnp.bfloat16
F32 = jnp.float32
LANES = 128
IDS = 8


def iota(shape, dim):
    return lax.broadcasted_iota(jnp.int32, shape, dim)


def hot16(index, *rows):
    found = index == rows[0]
    for row in rows[1:]:
        found = found | (index == row)
    return jnp.where(found, jnp.ones((), BF), jnp.zeros((), BF))


def pack_kernel(owners, cap, rows_dev, tables_hbm, owner_hbm, local_hbm, grad_hbm, out_ref,
                tables_ref, owner_ref, local_ref, grad_ref, sems):
    pairs = (
        (owner_hbm, owner_ref),
        (tables_hbm, tables_ref),
        (local_hbm, local_ref),
        (grad_hbm, grad_ref),
    )
    copies = [pltpu.make_async_copy(a, b, sems.at[i]) for i, (a, b) in enumerate(pairs)]
    for copy in copies:
        copy.start()
    lists, samples = owner_ref.shape
    features = tables_ref.shape[0]
    pool = lists // features
    count = grad_ref.shape[0]
    copies[0].wait()
    owner = owner_ref[...]

    low = iota((samples, 2 * samples), 0)
    col = iota((samples, 2 * samples), 1)
    tri = jnp.where((low <= col), 1.0, 0.0).astype(BF)
    hot = [iota((owners, samples), 0) == owner[r : r + 1, :] for r in range(lists)]
    stacked = jnp.concatenate([jnp.where(h, 1.0, 0.0) for h in hot], axis=0).astype(BF)
    counts = jnp.dot(stacked, tri, preferred_element_type=F32)
    carry = jnp.zeros((owners, samples), F32)
    places = []
    for r in range(lists):
        block = counts[r * owners : (r + 1) * owners]
        running = block[:, :samples] + carry
        places.append(jnp.sum(jnp.where(hot[r], running, 0.0), axis=0, keepdims=True) - 1.0)
        carry = carry + block[:, samples:]
    place = jnp.concatenate(places, axis=0)

    spread = (iota((samples, count), 1) // features == iota((samples, count), 0))
    spread = jnp.where(spread, 1.0, 0.0).astype(BF)
    both = jnp.concatenate([owner.astype(F32), place], axis=0).astype(BF)
    wide = jnp.dot(both, spread, preferred_element_type=F32)
    slots = []
    lane_f = iota((lists, count), 1) % features
    slot = wide[:lists] * cap + wide[lists:]
    for p in range(pool):
        keep = iota((lists, count), 0) == lane_f * pool + p
        one = jnp.sum(jnp.where(keep, slot, 0.0), axis=0, keepdims=True)
        slots.append(jnp.broadcast_to(one, (16, count)).astype(jnp.int32).astype(jnp.int16)[0:1])

    group = 8
    rows = group * cap
    index = iota((rows, count), 0).astype(jnp.int16)
    copies[3].wait()
    grad = grad_ref[...]
    for g in range(owners // group):
        chosen = hot16(index, *[s - jnp.int16(g * rows) for s in slots])
        picked = jnp.dot(chosen, grad, preferred_element_type=F32)
        picked = picked.astype(BF)
        for k in range(group):
            part = picked[k * cap : (k + 1) * cap]
            out_ref[g * group + k, 0:cap, :] = part[:, :LANES]
            out_ref[g * group + k, cap : 2 * cap, :] = part[:, LANES:]

    copies[1].wait()
    copies[2].wait()
    table = jnp.zeros((lists, samples), jnp.int32)
    for f in range(features):
        table = jnp.where(iota((lists, samples), 0) // pool == f, tables_ref[f], table)
    target = table * rows_dev + local_ref[...]
    shift = (lax.axis_index("mp") % 8) * cap
    lane = place.astype(jnp.int32) + shift
    chunk = lane // LANES
    low_id = (target % 64).astype(F32)
    high_id = (target // 64).astype(F32)
    left, right = [], []
    kind = iota((IDS, samples), 0)
    for r in range(lists):
        row = slice(r, r + 1)
        value = jnp.where(kind < 3, low_id[row], high_id[row])
        value = jnp.where((kind % 3 == chunk[row]) & (kind < 6), value, 0.0)
        blocks = [jnp.where(owner[row] == o, value, 0.0) for o in range(owners)]
        left.append(jnp.concatenate(blocks, axis=0).astype(BF))
        right.append(jnp.where(lane[row] % LANES == iota((LANES, samples), 0), 1.0, 0.0).astype(BF))
    ids = lax.dot_general(
        jnp.concatenate(left, axis=1),
        jnp.concatenate(right, axis=1),
        (((1,), (1,)), ((), ())),
        preferred_element_type=F32,
    )
    out_ref[:, 2 * cap : 2 * cap + IDS, :] = ids.reshape(owners, IDS, LANES).astype(BF)


def update_kernel(cap, shards, recv_ref, table_ref, state_ref, out_ref):
    senders = recv_ref.shape[0]
    rows = table_ref.shape[0]
    part = rows // shards
    ids = recv_ref[:, 2 * cap : 2 * cap + IDS, :].astype(F32)
    ids = jnp.sum(ids.reshape(senders // 8, 8, IDS, LANES), axis=1)
    group = 16
    where, data = [], []
    for g in range(senders // group):
        lanes = []
        for h in range(group // 8):
            x = ids[g * (group // 8) + h]
            lanes += [x[j : j + 1] + 64.0 * x[j + 3 : j + 4] for j in range(3)]
        one = jnp.concatenate(lanes, axis=1)
        one = jnp.broadcast_to(one, (16, group * cap)).astype(jnp.int32).astype(jnp.int16)
        where.append(one[0:1])
        block = recv_ref[g * group : (g + 1) * group, 0 : 2 * cap, :]
        halves = [
            block[:, h * cap : (h + 1) * cap, :].reshape(group * cap, LANES) for h in range(2)
        ]
        data.append(jnp.concatenate(halves, axis=1))
    state = jnp.transpose(state_ref[...])
    index = iota((part, group * cap), 0).astype(jnp.int16)
    spread = []
    for k in range(shards):
        total = jnp.zeros((part, 2 * LANES), F32)
        for g in range(senders // group):
            hot = hot16(index, where[g] - jnp.int16(k * part))
            total = total + jnp.dot(hot, data[g], preferred_element_type=F32)
        square = jnp.sum(total * total, axis=1, keepdims=True) * (1.0 / (2 * LANES))
        columns = []
        for b in range(part // LANES):
            at = k * (part // LANES) + b
            columns.append(state[:, at : at + 1] + square[b * LANES : (b + 1) * LANES])
        new = jnp.concatenate(columns, axis=0)
        old = table_ref[k * part : (k + 1) * part, :].astype(F32)
        out_ref[k, 0:part, :] = (old - 0.3 * total / jnp.sqrt(new)).astype(BF)
        wide = [jnp.transpose(jnp.broadcast_to(c, (LANES, LANES)))[0:1] for c in columns]
        spread.append(jnp.concatenate(wide, axis=1))
    whole = jnp.concatenate(spread, axis=0)
    high = whole.astype(BF).astype(F32)
    both = jnp.concatenate([high, whole - high], axis=0).astype(BF)
    for k in range(shards):
        out_ref[k, part : part + 2 * shards, :] = both


def average_kernel(got_ref, out_ref, state_ref):
    replicas, rows, embed = got_ref.shape
    part = rows - 2 * replicas
    total = got_ref[0].astype(F32)
    for r in range(1, replicas):
        total = total + got_ref[r].astype(F32)
    total = total * (1.0 / replicas)
    table = total[:part].astype(BF)
    for r in range(replicas):
        out_ref[r, :, :] = table
    state = total[part : part + replicas] + total[part + replicas :]
    wide = state_ref.shape[1] // embed
    for k in range(replicas):
        at = (k % wide) * embed
        state_ref[k // wide : k // wide + 1, at : at + embed] = state[k : k + 1]


ALL_VMEM = pltpu.CompilerParams(vmem_limit_bytes=60 * 2**20)
PARAMS = pltpu.CompilerParams(vmem_limit_bytes=32 * 2**20)
VMEM = pl.BlockSpec(memory_space=pltpu.VMEM)
ANY = pl.BlockSpec(memory_space=pl.ANY)


def shards_fn(pooled_grad, owner_ids, local_ids, feature_table, table_rows, adagrad_state):
    samples, features, embed = pooled_grad.shape
    pool = local_ids.shape[2]
    tables, rows_dev = adagrad_state.shape
    owners = lax.axis_size("mp")
    replicas = lax.axis_size("rep")
    slots = tables * rows_dev
    count = samples * features * pool
    cap = 3 * count // (2 * owners)
    part = slots // replicas
    owner = jnp.transpose(owner_ids[..., 0], (1, 2, 0)).reshape(features * pool, samples)
    local = jnp.transpose(local_ids, (1, 2, 0)).reshape(features * pool, samples)
    send = pl.pallas_call(
        lambda *refs: pack_kernel(owners, cap, rows_dev, *refs),
        out_shape=jax.ShapeDtypeStruct((owners, 2 * cap + IDS, LANES), BF),
        in_specs=[ANY, ANY, ANY, ANY],
        out_specs=VMEM,
        scratch_shapes=[
            pltpu.SMEM((features,), jnp.int32),
            pltpu.VMEM((features * pool, samples), jnp.int32),
            pltpu.VMEM((features * pool, samples), jnp.int32),
            pltpu.VMEM((samples * features, embed), BF),
            pltpu.SemaphoreType.DMA((4,)),
        ],
        compiler_params=ALL_VMEM,
        name="pack",
    )(feature_table, owner, local, pooled_grad.reshape(samples * features, embed))
    received = lax.all_to_all(send, "mp", split_axis=0, concat_axis=0, tiled=True)
    updated = pl.pallas_call(
        lambda *refs: update_kernel(cap, replicas, *refs),
        out_shape=jax.ShapeDtypeStruct((replicas, part + 2 * replicas, embed), BF),
        in_specs=[VMEM, VMEM, VMEM],
        out_specs=VMEM,
        compiler_params=PARAMS,
        name="update",
    )(received, table_rows.reshape(slots, embed), adagrad_state.reshape(slots // LANES, LANES))
    mine = lax.all_to_all(updated, "rep", split_axis=0, concat_axis=0, tiled=True)
    copies, state = pl.pallas_call(
        average_kernel,
        out_shape=(
            jax.ShapeDtypeStruct((replicas, part, embed), BF),
            jax.ShapeDtypeStruct((tables, rows_dev), F32),
        ),
        in_specs=[VMEM],
        out_specs=(VMEM, VMEM),
        compiler_params=PARAMS,
        name="average",
    )(mine)
    full = lax.all_to_all(copies, "rep", split_axis=0, concat_axis=0, tiled=True)
    return full.reshape(tables, rows_dev, embed), state


def solution(mesh):
    placed = (
        P(("rep", "mp"), None, None),
        P(("rep", "mp"), None, None, None),
        P(("rep", "mp"), None, None),
        P(),
        P(None, "mp", None),
        P(None, "mp"),
    )
    return jax.shard_map(
        shards_fn,
        mesh=mesh,
        in_specs=placed,
        out_specs=(P(None, "mp", None), P(None, "mp")),
        check_vma=False,
    )
```

time: 139 us -> 136 us (0.978)
  the two profiles are of different devices: /device:TPU:18 before, /device:TPU:19 now
where the time goes in v2:
time: 136 us
  blocking collectives  72 us (53%)
  waiting for transfers between devices  41.4 us (30%)
  starting transfers between devices  10.9 us (8%)
  Pallas kernels  10 us (7%)
    all_to_all x1, waiting for transfers between devices, shards_fn(): lax.all_to_all(send, 'mp', split_axis=0, concat_axis=0, tiled=True)  41.4 us
    all_to_all x1, blocking collectives, shards_fn(): lax.all_to_all(updated, 'rep', split_axis=0, concat_axis=0, tiled=True)  40.5 us
    all_to_all x1, blocking collectives, shards_fn(): lax.all_to_all(copies, 'rep', split_axis=0, concat_axis=0, tiled=True)  31.5 us
    all_to_all x1, starting transfers between devices, shards_fn(): lax.all_to_all(send, 'mp', split_axis=0, concat_axis=0, tiled=True)  10.9 us
    pallas_call x1, Pallas kernels, shards_fn(): pl.pallas_call(lambda *refs: pack_kernel(owners, cap, rows_dev, *refs), o...  5.25 us
    pallas_call x1, Pallas kernels, shards_fn(): pl.pallas_call(lambda *refs: update_kernel(cap, replicas, *refs), out_sha...  4.13 us
  transfers between devices with their start and end apart: 1, of which 1 were waited for; matrix products, arithmetic and copies ran while one was open for 0% of the time, Pallas kernels for 0%

profile of v2, /device:TPU:19, one launch (start us, length us, event | category | flops | bytes accessed | tf_op | source)
XLA Modules:
  0.0 136.0 jit_solution(14759139679657001706)
XLA Ops:
  0.6 5.3 %pack.1 = bf16[64,104,128]{2,1,0:T(8,128)(2,1)} custom-call(s32[8]{0:T(128)} %refs_0_.1, s32[16,128]{1,0:T(8,128)} %bitcast.14, s32[16,128]{1,0:T(8,128)} %bitcast.15, bf16[1024,256]{1,0:T(8,128)(2,1)} %bitcast.13), custom_call_target="tpu_custom_call" | custom-call | tf_op jit(solution)/shard_map/pack/pallas_call | solution.py:194
  5.9 0.0 copy-start.1
  5.9 0.0 copy-start
  5.9 10.9 %all-to-all-start = ((bf16[64,104,128]{2,1,0:T(8,128)(2,1)}), bf16[64,104,128]{2,1,0:T(8,128)(2,1)S(1)}, u32[]{:S(2)}, u32[]{:S(2)}) async-start(bf16[64,104,128]{2,1,0:T(8,128)(2,1)} %pack.1), calls=%async_computation | async-start | bytes 3407872 | tf_op jit(solution)/shard_map/all_to_all | solution.py:209
  16.8 0.0 copy-done.1
  16.8 41.4 %all-to-all-done.refs_0_ = bf16[64,104,128]{2,1,0:T(8,128)(2,1)S(1)} async-done(((bf16[64,104,128]{2,1,0:T(8,128)(2,1)}), bf16[64,104,128]{2,1,0:T(8,128)(2,1)S(1)}, u32[]{:S(2)}, u32[]{:S(2)}) %all-to-all-start) | async-done | bytes 1703968 | tf_op jit(solution)/shard_map/all_to_all | solution.py:209
  58.2 0.0 copy-done
  58.2 4.1 %update.1 = bf16[8,272,256]{2,1,0:T(8,128)(2,1)S(1)} custom-call(bf16[64,104,128]{2,1,0:T(8,128)(2,1)S(1)} %all-to-all-done.refs_0_, bf16[2048,256]{1,0:T(8,128)(2,1)S(1)} %bitcast.11, f32[16,128]{1,0:T(8,128)S(1)} %reshape.26.refs_2_), custom_call_target="tpu_custom_call" | custom-call | tf_op jit(solution)/shard_map/update/pallas_call | solution.py:210
  62.4 40.5 %all_to_all.15.got_ref = bf16[8,272,256]{2,1,0:T(8,128)(2,1)S(1)} all-to-all(bf16[8,272,256]{2,1,0:T(8,128)(2,1)S(1)} %update.1), channel_id=1, replica_groups=mesh['rep'=8,'mp'=64] {'rep'}, dimensions={0} | all-to-all | bytes 2228224 | tf_op jit(solution)/shard_map/all_to_all | solution.py:218
  102.8 0.6 average.1
  103.5 31.5 %all_to_all.16 = bf16[8,256,256]{2,1,0:T(8,128)(2,1)S(1)} all-to-all(bf16[8,256,256]{2,1,0:T(8,128)(2,1)S(1)} %get-tuple-element.4), channel_id=1, replica_groups=mesh['rep'=8,'mp'=64] {'rep'}, dimensions={0} | all-to-all | bytes 2097152 | tf_op jit(solution)/shard_map/all_to_all | solution.py:230
  135.0 1.0 copy.9
  (1 shorter events, 0.0 us)
Async XLA Ops:
  5.9 10.9 %copy-start.1 = (f32[2,1024]{1,0:T(2,128)S(1)}, f32[2,1024]{1,0:T(2,128)}, u32[]{:S(2)}) copy-start(f32[2,1024]{1,0:T(2,128)} %param.11) | copy-start | bytes 24580
  5.9 52.3 %copy-start = (bf16[2,1024,256]{2,1,0:T(8,128)(2,1)S(1)}, bf16[2,1024,256]{2,1,0:T(8,128)(2,1)}, u32[]{:S(2)}) copy-start(bf16[2,1024,256]{2,1,0:T(8,128)(2,1)} %param.10) | copy-start | bytes 3145732
  5.9 52.3 %all-to-all-start = ((bf16[64,104,128]{2,1,0:T(8,128)(2,1)}), bf16[64,104,128]{2,1,0:T(8,128)(2,1)S(1)}, u32[]{:S(2)}, u32[]{:S(2)}) async-start(bf16[64,104,128]{2,1,0:T(8,128)(2,1)} %pack.1), calls=%async_computation | async-start | bytes 3407872 | tf_op jit(solution)/shard_map/all_to_all | solution.py:209

commit v3 on v2

--- a/solution.py
+++ b/solution.py
@@ -8,6 +8,7 @@
 BF = jnp.bfloat16
 F32 = jnp.float32
 LANES = 128
+TURNS = 2
 IDS = 8
 
 
@@ -22,8 +23,9 @@
     return jnp.where(found, jnp.ones((), BF), jnp.zeros((), BF))
 
 
-def pack_kernel(owners, cap, rows_dev, tables_hbm, owner_hbm, local_hbm, grad_hbm, out_ref,
-                tables_ref, owner_ref, local_ref, grad_ref, sems):
+def pack_kernel(owners, cap, rows_dev, tables_hbm, owner_hbm, local_hbm, grad_hbm, own_ref,
+                other_ref, tables_ref, owner_ref, local_ref, grad_ref, sems):
+    chips = owners // 2
     pairs = (
         (owner_hbm, owner_ref),
         (tables_hbm, tables_ref),
@@ -39,6 +41,8 @@
     count = grad_ref.shape[0]
     copies[0].wait()
     owner = owner_ref[...]
+    core = lax.axis_index("core")
+    owner = owner // 2 + chips * ((owner + core) % 2)
 
     low = iota((samples, 2 * samples), 0)
     col = iota((samples, 2 * samples), 1)
@@ -78,8 +82,9 @@
         picked = picked.astype(BF)
         for k in range(group):
             part = picked[k * cap : (k + 1) * cap]
-            out_ref[g * group + k, 0:cap, :] = part[:, :LANES]
-            out_ref[g * group + k, cap : 2 * cap, :] = part[:, LANES:]
+            out_ref, at = (own_ref, other_ref)[(g * group + k) // chips], (g * group + k) % chips
+            out_ref[at, 0:cap, :] = part[:, :LANES]
+            out_ref[at, cap : 2 * cap, :] = part[:, LANES:]
 
     copies[1].wait()
     copies[2].wait()
@@ -87,7 +92,7 @@
     for f in range(features):
         table = jnp.where(iota((lists, samples), 0) // pool == f, tables_ref[f], table)
     target = table * rows_dev + local_ref[...]
-    shift = (lax.axis_index("mp") % 8) * cap
+    shift = ((lax.axis_index("yx") % 4) * 2 + core) * cap
     lane = place.astype(jnp.int32) + shift
     chunk = lane // LANES
     low_id = (target % 64).astype(F32)
@@ -107,15 +112,38 @@
         (((1,), (1,)), ((), ())),
         preferred_element_type=F32,
     )
-    out_ref[:, 2 * cap : 2 * cap + IDS, :] = ids.reshape(owners, IDS, LANES).astype(BF)
+    ids = ids.reshape(owners, IDS, LANES).astype(BF)
+    own_ref[:, 2 * cap : 2 * cap + IDS, :] = ids[:chips]
+    other_ref[:, 2 * cap : 2 * cap + IDS, :] = ids[chips:]
+
+
+def merge_kernel(own_ref, got_ref, turn_ref, out_ref):
+    rows = own_ref.shape[1] - IDS
+    first = lax.axis_index("core") == 0
+
+    @pl.when(first)
+    def _():
+        out_ref[:, 0:rows, :] = own_ref[:, 0:rows, :]
+        out_ref[:, rows : 2 * rows, :] = got_ref[:, 0:rows, :]
+
+    @pl.when(jnp.logical_not(first))
+    def _():
+        out_ref[:, 0:rows, :] = got_ref[:, 0:rows, :]
+        out_ref[:, rows : 2 * rows, :] = own_ref[:, 0:rows, :]
+
+    ids = own_ref[:, rows:, :].astype(F32) + got_ref[:, rows:, :].astype(F32)
+    out_ref[:, 2 * rows :, :] = ids.astype(BF)
+    turn = jnp.where(iota((IDS, LANES), 0) < 6, ids[0], turn_ref[...].astype(F32))
+    out_ref[0, 2 * rows :, :] = turn.astype(BF)
 
 
 def update_kernel(cap, shards, recv_ref, table_ref, state_ref, out_ref):
-    senders = recv_ref.shape[0]
+    chips = recv_ref.shape[0]
+    senders = 2 * chips
     rows = table_ref.shape[0]
     part = rows // shards
-    ids = recv_ref[:, 2 * cap : 2 * cap + IDS, :].astype(F32)
-    ids = jnp.sum(ids.reshape(senders // 8, 8, IDS, LANES), axis=1)
+    ids = recv_ref[:, 4 * cap : 4 * cap + IDS, :].astype(F32)
+    ids = jnp.sum(ids.reshape(chips // 4, 4, IDS, LANES), axis=1)
     group = 16
     where, data = [], []
     for g in range(senders // group):
@@ -126,7 +154,8 @@
         one = jnp.concatenate(lanes, axis=1)
         one = jnp.broadcast_to(one, (16, group * cap)).astype(jnp.int32).astype(jnp.int16)
         where.append(one[0:1])
-        block = recv_ref[g * group : (g + 1) * group, 0 : 2 * cap, :]
+        block = recv_ref[g * group // 2 : (g + 1) * group // 2, 0 : 4 * cap, :]
+        block = block.reshape(group, 2 * cap, LANES)
         halves = [
             block[:, h * cap : (h + 1) * cap, :].reshape(group * cap, LANES) for h in range(2)
         ]
@@ -183,7 +212,8 @@
     samples, features, embed = pooled_grad.shape
     pool = local_ids.shape[2]
     tables, rows_dev = adagrad_state.shape
-    owners = lax.axis_size("mp")
+    chips = lax.axis_size("yx")
+    owners = 2 * chips
     replicas = lax.axis_size("rep")
     slots = tables * rows_dev
     count = samples * features * pool
@@ -191,11 +221,11 @@
     part = slots // replicas
     owner = jnp.transpose(owner_ids[..., 0], (1, 2, 0)).reshape(features * pool, samples)
     local = jnp.transpose(local_ids, (1, 2, 0)).reshape(features * pool, samples)
-    send = pl.pallas_call(
+    own, other = pl.pallas_call(
         lambda *refs: pack_kernel(owners, cap, rows_dev, *refs),
-        out_shape=jax.ShapeDtypeStruct((owners, 2 * cap + IDS, LANES), BF),
+        out_shape=(jax.ShapeDtypeStruct((chips, 2 * cap + IDS, LANES), BF),) * 2,
         in_specs=[ANY, ANY, ANY, ANY],
-        out_specs=VMEM,
+        out_specs=(VMEM, VMEM),
         scratch_shapes=[
             pltpu.SMEM((features,), jnp.int32),
             pltpu.VMEM((features * pool, samples), jnp.int32),
@@ -206,7 +236,20 @@
         compiler_params=ALL_VMEM,
         name="pack",
     )(feature_table, owner, local, pooled_grad.reshape(samples * features, embed))
-    received = lax.all_to_all(send, "mp", split_axis=0, concat_axis=0, tiled=True)
+    got = lax.ppermute(other, "core", [(0, 1), (1, 0)])
+    turn = got[0, 2 * cap :, :]
+    for _ in range(TURNS):
+        ring = [(2 * i + 1, 2 * ((i + 1) % chips) + 1) for i in range(chips)]
+        turn = lax.ppermute(turn, ("yx", "core"), ring)
+    send = pl.pallas_call(
+        merge_kernel,
+        out_shape=jax.ShapeDtypeStruct((chips, 4 * cap + IDS, LANES), BF),
+        in_specs=[VMEM, VMEM, VMEM],
+        out_specs=VMEM,
+        compiler_params=PARAMS,
+        name="merge",
+    )(own, got, turn)
+    received = lax.all_to_all(send, "yx", split_axis=0, concat_axis=0, tiled=True)
     updated = pl.pallas_call(
         lambda *refs: update_kernel(cap, replicas, *refs),
         out_shape=jax.ShapeDtypeStruct((replicas, part + 2 * replicas, embed), BF),
@@ -232,18 +275,22 @@
 
 
 def solution(mesh):
+    replicas, owners = mesh.devices.shape
+    cores = mesh.devices.reshape(replicas, owners // 2, 2)
+    by_core = jax.sharding.Mesh(cores, ("rep", "yx", "core"))
+    every, mine = ("rep", "yx", "core"), ("yx", "core")
     placed = (
-        P(("rep", "mp"), None, None),
-        P(("rep", "mp"), None, None, None),
-        P(("rep", "mp"), None, None),
+        P(every, None, None),
+        P(every, None, None, None),
+        P(every, None, None),
         P(),
-        P(None, "mp", None),
-        P(None, "mp"),
+        P(None, mine, None),
+        P(None, mine),
     )
     return jax.shard_map(
         shards_fn,
-        mesh=mesh,
+        mesh=by_core,
         in_specs=placed,
-        out_specs=(P(None, "mp", None), P(None, "mp")),
+        out_specs=(P(None, mine, None), P(None, mine)),
         check_vma=False,
     )

time: 136 us -> 130 us (0.956)
  the two profiles are of different devices: /device:TPU:19 before, /device:TPU:3 now
where the time goes in v3:
time: 130 us
  blocking collectives  57.9 us (45%)
  waiting for transfers between devices  41.9 us (32%)
  starting transfers between devices  15.8 us (12%)
  Pallas kernels  11.2 us (9%)
  local copies, waits for them, and re-layouts  2.15 us (2%)
    all_to_all x1, blocking collectives, shards_fn(): lax.all_to_all(updated, 'rep', split_axis=0, concat_axis=0, tiled=True)  32.8 us
    all_to_all x1, waiting for transfers between devices, shards_fn(): lax.all_to_all(send, 'yx', split_axis=0, concat_axis=0, tiled=True)  28.3 us
    all_to_all x1, blocking collectives, shards_fn(): lax.all_to_all(copies, 'rep', split_axis=0, concat_axis=0, tiled=True)  25.2 us
    ppermute x2, waiting for transfers between devices, shards_fn(): turn = lax.ppermute(turn, ('yx', 'core'), ring)  11.4 us
    all_to_all x1, starting transfers between devices, shards_fn(): lax.all_to_all(send, 'yx', split_axis=0, concat_axis=0, tiled=True)  8.25 us
    pallas_call x1, Pallas kernels, shards_fn(): pl.pallas_call(lambda *refs: pack_kernel(owners, cap, rows_dev, *refs), o...  5.18 us
    ppermute x2, starting transfers between devices, shards_fn(): turn = lax.ppermute(turn, ('yx', 'core'), ring)  5.01 us
    pallas_call x1, Pallas kernels, shards_fn(): pl.pallas_call(lambda *refs: update_kernel(cap, replicas, *refs), out_sha...  4.13 us
  transfers between devices with their start and end apart: 4, of which 4 were waited for; matrix products, arithmetic and copies ran while one was open for 0% of the time, Pallas kernels for 0%

profile of v3, /device:TPU:3, one launch (start us, length us, event | category | flops | bytes accessed | tf_op | source)
XLA Modules:
  0.0 129.8 jit_solution(7468054457984470195)
XLA Ops:
  0.6 5.2 %pack.1 = (bf16[32,104,128]{2,1,0:T(8,128)(2,1)}, bf16[32,104,128]{2,1,0:T(8,128)(2,1)}) custom-call(s32[8]{0:T(128)} %refs_0_.1, s32[16,128]{1,0:T(8,128)} %bitcast.16, s32[16,128]{1,0:T(8,128)} %bitcast.17, bf16[1024,256]{1,0:T(8,128)(2,1)} %bitcast.15), custom_call_target="tpu_custom_call" | custom-call | tf_op jit(solution)/shard_map/pack/pallas_call | solution.py:224
  5.8 2.6 %collective-permute-start = (bf16[32,104,128]{2,1,0:T(8,128)(2,1)}, bf16[32,104,128]{2,1,0:T(8,128)(2,1)S(1)}, u32[]{:S(2)}, u32[]{:S(2)}) collective-permute-start(bf16[32,104,128]{2,1,0:T(8,128)(2,1)} %get-tuple-element.7), channel_id=1, source_target_pairs={{0,1},{1,0},{2,3},{3,2},{4,5},{5,4},{6,7},{7,6},{8,9},{9,8},{10,11... | collective-permute-start | bytes 2555912 | tf_op jit(solution)/shard_map/ppermute | solution.py:239
  8.4 2.2 %collective-permute-done.got_ref = bf16[32,104,128]{2,1,0:T(8,128)(2,1)S(1)} collective-permute-done((bf16[32,104,128]{2,1,0:T(8,128)(2,1)}, bf16[32,104,128]{2,1,0:T(8,128)(2,1)S(1)}, u32[]{:S(2)}, u32[]{:S(2)}) %collective-permute-start) | collective-permute-done | bytes 852000 | tf_op jit(solution)/shard_map/ppermute | solution.py:239
  10.6 3.1 %collective-permute-start.1 = (bf16[8,128]{1,0:T(8,128)(2,1)S(1)}, bf16[8,128]{1,0:T(8,128)(2,1)S(1)}, u32[]{:S(2)}, u32[]{:S(2)}) collective-permute-start(bf16[8,128]{1,0:T(8,128)(2,1)S(1)} %slice_bitcast_fusion), channel_id=1, source_target_pairs={{1,3},{3,5},{5,7},{7,9},{9,11},{11,13},{13,15},{15,17},{17,19},{19... | collective-permute-start | bytes 6152 | tf_op jit(solution)/shard_map/ppermute | solution.py:243
  13.7 5.4 %collective-permute-done.1 = bf16[8,128]{1,0:T(8,128)(2,1)S(1)} collective-permute-done((bf16[8,128]{1,0:T(8,128)(2,1)S(1)}, bf16[8,128]{1,0:T(8,128)(2,1)S(1)}, u32[]{:S(2)}, u32[]{:S(2)}) %collective-permute-start.1) | collective-permute-done | bytes 2080 | tf_op jit(solution)/shard_map/ppermute | solution.py:243
  19.1 1.9 %collective-permute-start.2 = (bf16[8,128]{1,0:T(8,128)(2,1)S(1)}, bf16[8,128]{1,0:T(8,128)(2,1)S(1)}, u32[]{:S(2)}, u32[]{:S(2)}) collective-permute-start(bf16[8,128]{1,0:T(8,128)(2,1)S(1)} %collective-permute-done.1), channel_id=1, source_target_pairs={{1,3},{3,5},{5,7},{7,9},{9,11},{11,13},{13,15},{15,17},{17,19},{19... | collective-permute-start | bytes 6152 | tf_op jit(solution)/shard_map/ppermute | solution.py:243
  21.0 6.0 %collective-permute-done.2.turn_ref = bf16[8,128]{1,0:T(8,128)(2,1)S(1)} collective-permute-done((bf16[8,128]{1,0:T(8,128)(2,1)S(1)}, bf16[8,128]{1,0:T(8,128)(2,1)S(1)}, u32[]{:S(2)}, u32[]{:S(2)}) %collective-permute-start.2) | collective-permute-done | bytes 2080 | tf_op jit(solution)/shard_map/ppermute | solution.py:243
  27.0 0.0 copy-start.1
  27.0 1.2 copy-done.1
  28.2 1.3 %merge.1 = bf16[32,200,128]{2,1,0:T(8,128)(2,1)} custom-call(bf16[32,104,128]{2,1,0:T(8,128)(2,1)S(1)} %copy-done.1, bf16[32,104,128]{2,1,0:T(8,128)(2,1)S(1)} %collective-permute-done.got_ref, bf16[8,128]{1,0:T(8,128)(2,1)S(1)} %collective-permute-done.2.turn_ref), custom_call_target="tpu_custom_call" | custom-call | tf_op jit(solution)/shard_map/merge/pallas_call | solution.py:244
  29.5 0.0 copy-start.2
  29.5 0.0 copy-start
  29.5 8.3 %all-to-all-start = ((bf16[32,200,128]{2,1,0:T(8,128)(2,1)}), bf16[32,200,128]{2,1,0:T(8,128)(2,1)S(1)}, u32[]{:S(2)}, u32[]{:S(2)}) async-start(bf16[32,200,128]{2,1,0:T(8,128)(2,1)} %merge.1), calls=%async_computation | async-start | bytes 3276800 | tf_op jit(solution)/shard_map/all_to_all | solution.py:252
  37.8 0.0 copy-done.2
  37.8 28.3 %all-to-all-done.refs_0_ = bf16[32,200,128]{2,1,0:T(8,128)(2,1)S(1)} async-done(((bf16[32,200,128]{2,1,0:T(8,128)(2,1)}), bf16[32,200,128]{2,1,0:T(8,128)(2,1)S(1)}, u32[]{:S(2)}, u32[]{:S(2)}) %all-to-all-start) | async-done | bytes 1638432 | tf_op jit(solution)/shard_map/all_to_all | solution.py:252
  66.1 0.0 copy-done
  66.1 4.1 %update.1 = bf16[8,272,256]{2,1,0:T(8,128)(2,1)S(1)} custom-call(bf16[32,200,128]{2,1,0:T(8,128)(2,1)S(1)} %all-to-all-done.refs_0_, bf16[2048,256]{1,0:T(8,128)(2,1)S(1)} %bitcast.13, f32[16,128]{1,0:T(8,128)S(1)} %reshape.26.refs_2_), custom_call_target="tpu_custom_call" | custom-call | tf_op jit(solution)/shard_map/update/pallas_call | solution.py:253
  70.2 32.8 %all_to_all.15.got_ref = bf16[8,272,256]{2,1,0:T(8,128)(2,1)S(1)} all-to-all(bf16[8,272,256]{2,1,0:T(8,128)(2,1)S(1)} %update.1), channel_id=1, replica_groups=mesh['rep'=8,'yx'=32,'core'=2] {'rep'}, dimensions={0} | all-to-all | bytes 2228224 | tf_op jit(solution)/shard_map/all_to_all | solution.py:261
  103.0 0.6 average.1
  103.6 25.2 %all_to_all.16 = bf16[8,256,256]{2,1,0:T(8,128)(2,1)S(1)} all-to-all(bf16[8,256,256]{2,1,0:T(8,128)(2,1)S(1)} %get-tuple-element.8), channel_id=1, replica_groups=mesh['rep'=8,'yx'=32,'core'=2] {'rep'}, dimensions={0} | all-to-all | bytes 2097152 | tf_op jit(solution)/shard_map/all_to_all | solution.py:273
  128.8 1.0 copy.9
  (2 shorter events, 0.0 us)
Async XLA Ops:
  5.8 4.8 %collective-permute-start = (bf16[32,104,128]{2,1,0:T(8,128)(2,1)}, bf16[32,104,128]{2,1,0:T(8,128)(2,1)S(1)}, u32[]{:S(2)}, u32[]{:S(2)}) collective-permute-start(bf16[32,104,128]{2,1,0:T(8,128)(2,1)} %get-tuple-element.7), channel_id=1, source_target_pairs={{0,1},{1,0},{2,3},{3,2},{4,5},{5,4},{6,7},{7,6},{8,9},{9,8},{10,11... | collective-permute-start | bytes 2555912 | tf_op jit(solution)/shard_map/ppermute | solution.py:239
  10.6 8.5 %collective-permute-start.1 = (bf16[8,128]{1,0:T(8,128)(2,1)S(1)}, bf16[8,128]{1,0:T(8,128)(2,1)S(1)}, u32[]{:S(2)}, u32[]{:S(2)}) collective-permute-start(bf16[8,128]{1,0:T(8,128)(2,1)S(1)} %slice_bitcast_fusion), channel_id=1, source_target_pairs={{1,3},{3,5},{5,7},{7,9},{9,11},{11,13},{13,15},{15,17},{17,19},{19... | collective-permute-start | bytes 6152 | tf_op jit(solution)/shard_map/ppermute | solution.py:243
  19.1 7.9 %collective-permute-start.2 = (bf16[8,128]{1,0:T(8,128)(2,1)S(1)}, bf16[8,128]{1,0:T(8,128)(2,1)S(1)}, u32[]{:S(2)}, u32[]{:S(2)}) collective-permute-start(bf16[8,128]{1,0:T(8,128)(2,1)S(1)} %collective-permute-done.1), channel_id=1, source_target_pairs={{1,3},{3,5},{5,7},{7,9},{9,11},{11,13},{13,15},{15,17},{17,19},{19... | collective-permute-start | bytes 6152 | tf_op jit(solution)/shard_map/ppermute | solution.py:243
  27.0 1.2 copy-start.1
  29.5 8.3 %copy-start.2 = (f32[2,1024]{1,0:T(2,128)S(1)}, f32[2,1024]{1,0:T(2,128)}, u32[]{:S(2)}) copy-start(f32[2,1024]{1,0:T(2,128)} %param.11) | copy-start | bytes 24580
  29.5 36.6 %copy-start = (bf16[2,1024,256]{2,1,0:T(8,128)(2,1)S(1)}, bf16[2,1024,256]{2,1,0:T(8,128)(2,1)}, u32[]{:S(2)}) copy-start(bf16[2,1024,256]{2,1,0:T(8,128)(2,1)} %param.10) | copy-start | bytes 3145732
  29.5 36.6 %all-to-all-start = ((bf16[32,200,128]{2,1,0:T(8,128)(2,1)}), bf16[32,200,128]{2,1,0:T(8,128)(2,1)S(1)}, u32[]{:S(2)}, u32[]{:S(2)}) async-start(bf16[32,200,128]{2,1,0:T(8,128)(2,1)} %merge.1), calls=%async_computation | async-start | bytes 3276800 | tf_op jit(solution)/shard_map/all_to_all | solution.py:252

commit v4 on v3

--- a/solution.py
+++ b/solution.py
@@ -8,7 +8,7 @@
 BF = jnp.bfloat16
 F32 = jnp.float32
 LANES = 128
-TURNS = 2
+TURNS = 1
 IDS = 8
 
 

time: 130 us -> 144 us (1.11)
  blocking collectives: 57.9 us -> 72.1 us
  starting transfers between devices: 15.8 us -> 14.2 us
    all_to_all x1, blocking collectives: 32.8 us -> 40.5 us  [shards_fn(): lax.all_to_all(updated, 'rep', split_axis=0, concat_axis=0, tiled=True)]
    all_to_all x1, waiting for transfers between devices: 28.3 us -> 35.3 us  [shards_fn(): lax.all_to_all(send, 'yx', split_axis=0, concat_axis=0, tiled=True)]
    all_to_all x1, blocking collectives: 25.2 us -> 31.6 us  [shards_fn(): lax.all_to_all(copies, 'rep', split_axis=0, concat_axis=0, tiled=True)]
    ppermute x2 -> x1, waiting for transfers between devices: 11.4 us -> 5.38 us  [shards_fn(): turn = lax.ppermute(turn, ('yx', 'core'), ring)]
    ppermute x2 -> x1, starting transfers between devices: 5.01 us -> 3.1 us  [shards_fn(): turn = lax.ppermute(turn, ('yx', 'core'), ring)]
  transfers between devices with their start and end apart: 4 -> 3, of which waited for: 4 -> 3; matrix products, arithmetic and copies ran while one was open for 0% -> 0% of each run, Pallas kernels for 0% -> 0%
where the time goes in v4:
time: 144 us; the launch traced here: 143 us
  blocking collectives  72.1 us (50%)
  waiting for transfers between devices  42.8 us (30%)
  starting transfers between devices  14.2 us (10%)
  Pallas kernels  11.2 us (8%)
  local copies, waits for them, and re-layouts  2.15 us (1%)
    all_to_all x1, blocking collectives, shards_fn(): lax.all_to_all(updated, 'rep', split_axis=0, concat_axis=0, tiled=True)  40.5 us
    all_to_all x1, waiting for transfers between devices, shards_fn(): lax.all_to_all(send, 'yx', split_axis=0, concat_axis=0, tiled=True)  35.3 us
    all_to_all x1, blocking collectives, shards_fn(): lax.all_to_all(copies, 'rep', split_axis=0, concat_axis=0, tiled=True)  31.6 us
    all_to_all x1, starting transfers between devices, shards_fn(): lax.all_to_all(send, 'yx', split_axis=0, concat_axis=0, tiled=True)  8.53 us
    ppermute x1, waiting for transfers between devices, shards_fn(): turn = lax.ppermute(turn, ('yx', 'core'), ring)  5.38 us
    pallas_call x1, Pallas kernels, shards_fn(): pl.pallas_call(lambda *refs: pack_kernel(owners, cap, rows_dev, *refs), o...  5.17 us
    pallas_call x1, Pallas kernels, shards_fn(): pl.pallas_call(lambda *refs: update_kernel(cap, replicas, *refs), out_sha...  4.13 us
    ppermute x1, starting transfers between devices, shards_fn(): turn = lax.ppermute(turn, ('yx', 'core'), ring)  3.1 us
  transfers between devices with their start and end apart: 3, of which 3 were waited for; matrix products, arithmetic and copies ran while one was open for 0% of the time, Pallas kernels for 0%

profile of v4, /device:TPU:3, one launch (start us, length us, event | category | flops | bytes accessed | tf_op | source)
XLA Modules:
  0.0 143.2 jit_solution(2228435659025525399)
XLA Ops:
  0.6 5.2 %pack.1 = (bf16[32,104,128]{2,1,0:T(8,128)(2,1)}, bf16[32,104,128]{2,1,0:T(8,128)(2,1)}) custom-call(s32[8]{0:T(128)} %refs_0_.1, s32[16,128]{1,0:T(8,128)} %bitcast.16, s32[16,128]{1,0:T(8,128)} %bitcast.17, bf16[1024,256]{1,0:T(8,128)(2,1)} %bitcast.15), custom_call_target="tpu_custom_call" | custom-call | tf_op jit(solution)/shard_map/pack/pallas_call | solution.py:224
  5.8 2.6 %collective-permute-start = (bf16[32,104,128]{2,1,0:T(8,128)(2,1)}, bf16[32,104,128]{2,1,0:T(8,128)(2,1)S(1)}, u32[]{:S(2)}, u32[]{:S(2)}) collective-permute-start(bf16[32,104,128]{2,1,0:T(8,128)(2,1)} %get-tuple-element.7), channel_id=1, source_target_pairs={{0,1},{1,0},{2,3},{3,2},{4,5},{5,4},{6,7},{7,6},{8,9},{9,8},{10,11... | collective-permute-start | bytes 2555912 | tf_op jit(solution)/shard_map/ppermute | solution.py:239
  8.4 2.2 %collective-permute-done.got_ref = bf16[32,104,128]{2,1,0:T(8,128)(2,1)S(1)} collective-permute-done((bf16[32,104,128]{2,1,0:T(8,128)(2,1)}, bf16[32,104,128]{2,1,0:T(8,128)(2,1)S(1)}, u32[]{:S(2)}, u32[]{:S(2)}) %collective-permute-start) | collective-permute-done | bytes 852000 | tf_op jit(solution)/shard_map/ppermute | solution.py:239
  10.6 3.1 %collective-permute-start.1 = (bf16[8,128]{1,0:T(8,128)(2,1)S(1)}, bf16[8,128]{1,0:T(8,128)(2,1)S(1)}, u32[]{:S(2)}, u32[]{:S(2)}) collective-permute-start(bf16[8,128]{1,0:T(8,128)(2,1)S(1)} %slice_bitcast_fusion), channel_id=1, source_target_pairs={{1,3},{3,5},{5,7},{7,9},{9,11},{11,13},{13,15},{15,17},{17,19},{19... | collective-permute-start | bytes 6152 | tf_op jit(solution)/shard_map/ppermute | solution.py:243
  13.7 5.4 %collective-permute-done.1.turn_ref = bf16[8,128]{1,0:T(8,128)(2,1)S(1)} collective-permute-done((bf16[8,128]{1,0:T(8,128)(2,1)S(1)}, bf16[8,128]{1,0:T(8,128)(2,1)S(1)}, u32[]{:S(2)}, u32[]{:S(2)}) %collective-permute-start.1) | collective-permute-done | bytes 2080 | tf_op jit(solution)/shard_map/ppermute | solution.py:243
  19.1 0.0 copy-start.1
  19.1 1.2 copy-done.1
  20.2 1.3 merge.1
  21.5 0.0 copy-start.2
  21.6 0.0 copy-start
  21.6 8.5 %all-to-all-start = ((bf16[32,200,128]{2,1,0:T(8,128)(2,1)}), bf16[32,200,128]{2,1,0:T(8,128)(2,1)S(1)}, u32[]{:S(2)}, u32[]{:S(2)}) async-start(bf16[32,200,128]{2,1,0:T(8,128)(2,1)} %merge.1), calls=%async_computation | async-start | bytes 3276800 | tf_op jit(solution)/shard_map/all_to_all | solution.py:252
  30.1 0.0 copy-done.2
  30.1 35.3 %all-to-all-done.refs_0_ = bf16[32,200,128]{2,1,0:T(8,128)(2,1)S(1)} async-done(((bf16[32,200,128]{2,1,0:T(8,128)(2,1)}), bf16[32,200,128]{2,1,0:T(8,128)(2,1)S(1)}, u32[]{:S(2)}, u32[]{:S(2)}) %all-to-all-start) | async-done | bytes 1638432 | tf_op jit(solution)/shard_map/all_to_all | solution.py:252
  65.4 0.0 copy-done
  65.4 4.1 %update.1 = bf16[8,272,256]{2,1,0:T(8,128)(2,1)S(1)} custom-call(bf16[32,200,128]{2,1,0:T(8,128)(2,1)S(1)} %all-to-all-done.refs_0_, bf16[2048,256]{1,0:T(8,128)(2,1)S(1)} %bitcast.13, f32[16,128]{1,0:T(8,128)S(1)} %reshape.26.refs_2_), custom_call_target="tpu_custom_call" | custom-call | tf_op jit(solution)/shard_map/update/pallas_call | solution.py:253
  69.5 40.5 %all_to_all.15.got_ref = bf16[8,272,256]{2,1,0:T(8,128)(2,1)S(1)} all-to-all(bf16[8,272,256]{2,1,0:T(8,128)(2,1)S(1)} %update.1), channel_id=1, replica_groups=mesh['rep'=8,'yx'=32,'core'=2] {'rep'}, dimensions={0} | all-to-all | bytes 2228224 | tf_op jit(solution)/shard_map/all_to_all | solution.py:261
  110.1 0.6 average.1
  110.7 31.6 %all_to_all.16 = bf16[8,256,256]{2,1,0:T(8,128)(2,1)S(1)} all-to-all(bf16[8,256,256]{2,1,0:T(8,128)(2,1)S(1)} %get-tuple-element.8), channel_id=1, replica_groups=mesh['rep'=8,'yx'=32,'core'=2] {'rep'}, dimensions={0} | all-to-all | bytes 2097152 | tf_op jit(solution)/shard_map/all_to_all | solution.py:273
  142.3 1.0 copy.9
  (2 shorter events, 0.0 us)
Async XLA Ops:
  5.8 4.8 %collective-permute-start = (bf16[32,104,128]{2,1,0:T(8,128)(2,1)}, bf16[32,104,128]{2,1,0:T(8,128)(2,1)S(1)}, u32[]{:S(2)}, u32[]{:S(2)}) collective-permute-start(bf16[32,104,128]{2,1,0:T(8,128)(2,1)} %get-tuple-element.7), channel_id=1, source_target_pairs={{0,1},{1,0},{2,3},{3,2},{4,5},{5,4},{6,7},{7,6},{8,9},{9,8},{10,11... | collective-permute-start | bytes 2555912 | tf_op jit(solution)/shard_map/ppermute | solution.py:239
  10.6 8.5 %collective-permute-start.1 = (bf16[8,128]{1,0:T(8,128)(2,1)S(1)}, bf16[8,128]{1,0:T(8,128)(2,1)S(1)}, u32[]{:S(2)}, u32[]{:S(2)}) collective-permute-start(bf16[8,128]{1,0:T(8,128)(2,1)S(1)} %slice_bitcast_fusion), channel_id=1, source_target_pairs={{1,3},{3,5},{5,7},{7,9},{9,11},{11,13},{13,15},{15,17},{17,19},{19... | collective-permute-start | bytes 6152 | tf_op jit(solution)/shard_map/ppermute | solution.py:243
  19.1 1.2 copy-start.1
  21.5 8.5 %copy-start.2 = (f32[2,1024]{1,0:T(2,128)S(1)}, f32[2,1024]{1,0:T(2,128)}, u32[]{:S(2)}) copy-start(f32[2,1024]{1,0:T(2,128)} %param.11) | copy-start | bytes 24580
  21.6 43.8 %copy-start = (bf16[2,1024,256]{2,1,0:T(8,128)(2,1)S(1)}, bf16[2,1024,256]{2,1,0:T(8,128)(2,1)}, u32[]{:S(2)}) copy-start(bf16[2,1024,256]{2,1,0:T(8,128)(2,1)} %param.10) | copy-start | bytes 3145732
  21.6 43.8 %all-to-all-start = ((bf16[32,200,128]{2,1,0:T(8,128)(2,1)}), bf16[32,200,128]{2,1,0:T(8,128)(2,1)S(1)}, u32[]{:S(2)}, u32[]{:S(2)}) async-start(bf16[32,200,128]{2,1,0:T(8,128)(2,1)} %merge.1), calls=%async_computation | async-start | bytes 3276800 | tf_op jit(solution)/shard_map/all_to_all | solution.py:252

commit v5 on v3

--- a/solution.py
+++ b/solution.py
@@ -24,7 +24,7 @@
 
 
 def pack_kernel(owners, cap, rows_dev, tables_hbm, owner_hbm, local_hbm, grad_hbm, own_ref,
-                other_ref, tables_ref, owner_ref, local_ref, grad_ref, sems):
+                other_ref, turn_ref, tables_ref, owner_ref, local_ref, grad_ref, sems):
     chips = owners // 2
     pairs = (
         (owner_hbm, owner_ref),
@@ -115,6 +115,7 @@
     ids = ids.reshape(owners, IDS, LANES).astype(BF)
     own_ref[:, 2 * cap : 2 * cap + IDS, :] = ids[:chips]
     other_ref[:, 2 * cap : 2 * cap + IDS, :] = ids[chips:]
+    turn_ref[...] = jnp.zeros((IDS, LANES), BF)
 
 
 def merge_kernel(own_ref, got_ref, turn_ref, out_ref):
@@ -221,11 +222,15 @@
     part = slots // replicas
     owner = jnp.transpose(owner_ids[..., 0], (1, 2, 0)).reshape(features * pool, samples)
     local = jnp.transpose(local_ids, (1, 2, 0)).reshape(features * pool, samples)
-    own, other = pl.pallas_call(
+    own, other, turn = pl.pallas_call(
         lambda *refs: pack_kernel(owners, cap, rows_dev, *refs),
-        out_shape=(jax.ShapeDtypeStruct((chips, 2 * cap + IDS, LANES), BF),) * 2,
+        out_shape=(
+            jax.ShapeDtypeStruct((chips, 2 * cap + IDS, LANES), BF),
+            jax.ShapeDtypeStruct((chips, 2 * cap + IDS, LANES), BF),
+            jax.ShapeDtypeStruct((IDS, LANES), BF),
+        ),
         in_specs=[ANY, ANY, ANY, ANY],
-        out_specs=(VMEM, VMEM),
+        out_specs=(VMEM, VMEM, VMEM),
         scratch_shapes=[
             pltpu.SMEM((features,), jnp.int32),
             pltpu.VMEM((features * pool, samples), jnp.int32),
@@ -237,7 +242,6 @@
         name="pack",
     )(feature_table, owner, local, pooled_grad.reshape(samples * features, embed))
     got = lax.ppermute(other, "core", [(0, 1), (1, 0)])
-    turn = got[0, 2 * cap :, :]
     for _ in range(TURNS):
         ring = [(2 * i + 1, 2 * ((i + 1) % chips) + 1) for i in range(chips)]
         turn = lax.ppermute(turn, ("yx", "core"), ring)

time: 130 us -> 131 us (level)
  the two profiles are of different devices: /device:TPU:3 before, /device:TPU:15 now
where the time goes in v5:
time: 131 us; the launch traced here: 130 us
  blocking collectives  60.4 us (46%)
  waiting for transfers between devices  30.7 us (23%)
  starting transfers between devices  25.2 us (19%)
  Pallas kernels  11.2 us (9%)
  local copies, waits for them, and re-layouts  2.15 us (2%)
    all_to_all x1, blocking collectives, shards_fn(): lax.all_to_all(updated, 'rep', split_axis=0, concat_axis=0, tiled=True)  33.5 us
    all_to_all x1, waiting for transfers between devices, shards_fn(): lax.all_to_all(send, 'yx', split_axis=0, concat_axis=0, tiled=True)  28.6 us
    all_to_all x1, blocking collectives, shards_fn(): lax.all_to_all(copies, 'rep', split_axis=0, concat_axis=0, tiled=True)  26.8 us
    all_to_all x1, starting transfers between devices, shards_fn(): lax.all_to_all(send, 'yx', split_axis=0, concat_axis=0, tiled=True)  14.3 us
    ppermute x2, starting transfers between devices, shards_fn(): turn = lax.ppermute(turn, ('yx', 'core'), ring)  8.34 us
    pallas_call x1, Pallas kernels, shards_fn(): pl.pallas_call(lambda *refs: pack_kernel(owners, cap, rows_dev, *refs), o...  5.18 us
    pallas_call x1, Pallas kernels, shards_fn(): pl.pallas_call(lambda *refs: update_kernel(cap, replicas, *refs), out_sha...  4.13 us
  transfers between devices with their start and end apart: 4, of which 3 were waited for; matrix products, arithmetic and copies ran while one was open for 0% of the time, Pallas kernels for 0%

profile of v5, /device:TPU:15, one launch (start us, length us, event | category | flops | bytes accessed | tf_op | source)
XLA Modules:
  0.0 130.3 jit_solution(13176209536918553545)
XLA Ops:
  0.6 5.2 %pack.1 = (bf16[32,104,128]{2,1,0:T(8,128)(2,1)}, bf16[32,104,128]{2,1,0:T(8,128)(2,1)}, bf16[8,128]{1,0:T(8,128)(2,1)}) custom-call(s32[8]{0:T(128)} %refs_0_.1, s32[16,128]{1,0:T(8,128)} %bitcast.14, s32[16,128]{1,0:T(8,128)} %bitcast.15, bf16[1024,256]{1,0:T(8,128)(2,1)} %bitcast.13), custom_call_target="tpu_custom_call" | custom-call | tf_op jit(solution)/shard_map/pack/pallas_call | solution.py:225
  5.8 2.6 %collective-permute-start = (bf16[32,104,128]{2,1,0:T(8,128)(2,1)}, bf16[32,104,128]{2,1,0:T(8,128)(2,1)S(1)}, u32[]{:S(2)}, u32[]{:S(2)}) collective-permute-start(bf16[32,104,128]{2,1,0:T(8,128)(2,1)} %get-tuple-element.8), channel_id=1, source_target_pairs={{0,1},{1,0},{2,3},{3,2},{4,5},{5,4},{6,7},{7,6},{8,9},{9,8},{10,11... | collective-permute-start | bytes 2555912 | tf_op jit(solution)/shard_map/ppermute | solution.py:244
  8.4 3.1 %collective-permute-start.1 = (bf16[8,128]{1,0:T(8,128)(2,1)}, bf16[8,128]{1,0:T(8,128)(2,1)S(1)}, u32[]{:S(2)}, u32[]{:S(2)}) collective-permute-start(bf16[8,128]{1,0:T(8,128)(2,1)} %get-tuple-element.9), channel_id=1, source_target_pairs={{1,3},{3,5},{5,7},{7,9},{9,11},{11,13},{13,15},{15,17},{17,19},{19... | collective-permute-start | bytes 6152 | tf_op jit(solution)/shard_map/ppermute | solution.py:247
  11.5 1.4 %collective-permute-done.1 = bf16[8,128]{1,0:T(8,128)(2,1)S(1)} collective-permute-done((bf16[8,128]{1,0:T(8,128)(2,1)}, bf16[8,128]{1,0:T(8,128)(2,1)S(1)}, u32[]{:S(2)}, u32[]{:S(2)}) %collective-permute-start.1) | collective-permute-done | bytes 2080 | tf_op jit(solution)/shard_map/ppermute | solution.py:247
  12.9 5.2 %collective-permute-start.2 = (bf16[8,128]{1,0:T(8,128)(2,1)S(1)}, bf16[8,128]{1,0:T(8,128)(2,1)S(1)}, u32[]{:S(2)}, u32[]{:S(2)}) collective-permute-start(bf16[8,128]{1,0:T(8,128)(2,1)S(1)} %collective-permute-done.1), channel_id=1, source_target_pairs={{1,3},{3,5},{5,7},{7,9},{9,11},{11,13},{13,15},{15,17},{17,19},{19... | collective-permute-start | bytes 6152 | tf_op jit(solution)/shard_map/ppermute | solution.py:247
  18.2 0.7 collective-permute-done.2.turn_ref
  18.9 0.0 collective-permute-done.got_ref
  18.9 0.0 copy-start.1
  18.9 1.2 copy-done.1
  20.0 1.3 merge.1
  21.3 0.0 copy-start.2
  21.3 0.0 copy-start
  21.4 14.3 %all-to-all-start = ((bf16[32,200,128]{2,1,0:T(8,128)(2,1)}), bf16[32,200,128]{2,1,0:T(8,128)(2,1)S(1)}, u32[]{:S(2)}, u32[]{:S(2)}) async-start(bf16[32,200,128]{2,1,0:T(8,128)(2,1)} %merge.1), calls=%async_computation | async-start | bytes 3276800 | tf_op jit(solution)/shard_map/all_to_all | solution.py:256
  35.6 0.0 copy-done.2
  35.7 28.6 %all-to-all-done.refs_0_ = bf16[32,200,128]{2,1,0:T(8,128)(2,1)S(1)} async-done(((bf16[32,200,128]{2,1,0:T(8,128)(2,1)}), bf16[32,200,128]{2,1,0:T(8,128)(2,1)S(1)}, u32[]{:S(2)}, u32[]{:S(2)}) %all-to-all-start) | async-done | bytes 1638432 | tf_op jit(solution)/shard_map/all_to_all | solution.py:256
  64.2 0.0 copy-done
  64.2 4.1 %update.1 = bf16[8,272,256]{2,1,0:T(8,128)(2,1)S(1)} custom-call(bf16[32,200,128]{2,1,0:T(8,128)(2,1)S(1)} %all-to-all-done.refs_0_, bf16[2048,256]{1,0:T(8,128)(2,1)S(1)} %bitcast.11, f32[16,128]{1,0:T(8,128)S(1)} %reshape.26.refs_2_), custom_call_target="tpu_custom_call" | custom-call | tf_op jit(solution)/shard_map/update/pallas_call | solution.py:257
  68.4 33.5 %all_to_all.15.got_ref = bf16[8,272,256]{2,1,0:T(8,128)(2,1)S(1)} all-to-all(bf16[8,272,256]{2,1,0:T(8,128)(2,1)S(1)} %update.1), channel_id=1, replica_groups=mesh['rep'=8,'yx'=32,'core'=2] {'rep'}, dimensions={0} | all-to-all | bytes 2228224 | tf_op jit(solution)/shard_map/all_to_all | solution.py:265
  101.9 0.6 average.1
  102.5 26.8 %all_to_all.16 = bf16[8,256,256]{2,1,0:T(8,128)(2,1)S(1)} all-to-all(bf16[8,256,256]{2,1,0:T(8,128)(2,1)S(1)} %get-tuple-element.10), channel_id=1, replica_groups=mesh['rep'=8,'yx'=32,'core'=2] {'rep'}, dimensions={0} | all-to-all | bytes 2097152 | tf_op jit(solution)/shard_map/all_to_all | solution.py:277
  129.4 1.0 copy.9
  (1 shorter events, 0.0 us)
Async XLA Ops:
  5.8 13.1 %collective-permute-start = (bf16[32,104,128]{2,1,0:T(8,128)(2,1)}, bf16[32,104,128]{2,1,0:T(8,128)(2,1)S(1)}, u32[]{:S(2)}, u32[]{:S(2)}) collective-permute-start(bf16[32,104,128]{2,1,0:T(8,128)(2,1)} %get-tuple-element.8), channel_id=1, source_target_pairs={{0,1},{1,0},{2,3},{3,2},{4,5},{5,4},{6,7},{7,6},{8,9},{9,8},{10,11... | collective-permute-start | bytes 2555912 | tf_op jit(solution)/shard_map/ppermute | solution.py:244
  8.4 4.5 %collective-permute-start.1 = (bf16[8,128]{1,0:T(8,128)(2,1)}, bf16[8,128]{1,0:T(8,128)(2,1)S(1)}, u32[]{:S(2)}, u32[]{:S(2)}) collective-permute-start(bf16[8,128]{1,0:T(8,128)(2,1)} %get-tuple-element.9), channel_id=1, source_target_pairs={{1,3},{3,5},{5,7},{7,9},{9,11},{11,13},{13,15},{15,17},{17,19},{19... | collective-permute-start | bytes 6152 | tf_op jit(solution)/shard_map/ppermute | solution.py:247
  12.9 5.9 %collective-permute-start.2 = (bf16[8,128]{1,0:T(8,128)(2,1)S(1)}, bf16[8,128]{1,0:T(8,128)(2,1)S(1)}, u32[]{:S(2)}, u32[]{:S(2)}) collective-permute-start(bf16[8,128]{1,0:T(8,128)(2,1)S(1)} %collective-permute-done.1), channel_id=1, source_target_pairs={{1,3},{3,5},{5,7},{7,9},{9,11},{11,13},{13,15},{15,17},{17,19},{19... | collective-permute-start | bytes 6152 | tf_op jit(solution)/shard_map/ppermute | solution.py:247
  18.9 1.2 copy-start.1
  21.3 14.3 %copy-start.2 = (f32[2,1024]{1,0:T(2,128)S(1)}, f32[2,1024]{1,0:T(2,128)}, u32[]{:S(2)}) copy-start(f32[2,1024]{1,0:T(2,128)} %param.11) | copy-start | bytes 24580
  21.3 42.9 %copy-start = (bf16[2,1024,256]{2,1,0:T(8,128)(2,1)S(1)}, bf16[2,1024,256]{2,1,0:T(8,128)(2,1)}, u32[]{:S(2)}) copy-start(bf16[2,1024,256]{2,1,0:T(8,128)(2,1)} %param.10) | copy-start | bytes 3145732
  21.4 42.9 %all-to-all-start = ((bf16[32,200,128]{2,1,0:T(8,128)(2,1)}), bf16[32,200,128]{2,1,0:T(8,128)(2,1)S(1)}, u32[]{:S(2)}, u32[]{:S(2)}) async-start(bf16[32,200,128]{2,1,0:T(8,128)(2,1)} %merge.1), calls=%async_computation | async-start | bytes 3276800 | tf_op jit(solution)/shard_map/all_to_all | solution.py:256

commit v6 on v5

--- a/solution.py
+++ b/solution.py
@@ -23,8 +23,9 @@
     return jnp.where(found, jnp.ones((), BF), jnp.zeros((), BF))
 
 
-def pack_kernel(owners, cap, rows_dev, tables_hbm, owner_hbm, local_hbm, grad_hbm, own_ref,
-                other_ref, turn_ref, tables_ref, owner_ref, local_ref, grad_ref, sems):
+def pack_kernel(owners, cap, rows_dev, tables_hbm, owner_hbm, local_hbm, grad_hbm, own_hbm,
+                other_hbm, turn_ref, own_ref, other_ref, tables_ref, owner_ref, local_ref,
+                grad_ref, sems, out_sems):
     chips = owners // 2
     pairs = (
         (owner_hbm, owner_ref),
@@ -70,21 +71,6 @@
         keep = iota((lists, count), 0) == lane_f * pool + p
         one = jnp.sum(jnp.where(keep, slot, 0.0), axis=0, keepdims=True)
         slots.append(jnp.broadcast_to(one, (16, count)).astype(jnp.int32).astype(jnp.int16)[0:1])
-
-    group = 8
-    rows = group * cap
-    index = iota((rows, count), 0).astype(jnp.int16)
-    copies[3].wait()
-    grad = grad_ref[...]
-    for g in range(owners // group):
-        chosen = hot16(index, *[s - jnp.int16(g * rows) for s in slots])
-        picked = jnp.dot(chosen, grad, preferred_element_type=F32)
-        picked = picked.astype(BF)
-        for k in range(group):
-            part = picked[k * cap : (k + 1) * cap]
-            out_ref, at = (own_ref, other_ref)[(g * group + k) // chips], (g * group + k) % chips
-            out_ref[at, 0:cap, :] = part[:, :LANES]
-            out_ref[at, cap : 2 * cap, :] = part[:, LANES:]
 
     copies[1].wait()
     copies[2].wait()
@@ -116,6 +102,35 @@
     own_ref[:, 2 * cap : 2 * cap + IDS, :] = ids[:chips]
     other_ref[:, 2 * cap : 2 * cap + IDS, :] = ids[chips:]
     turn_ref[...] = jnp.zeros((IDS, LANES), BF)
+
+    group = 8
+    rows = group * cap
+    index = iota((rows, count), 0).astype(jnp.int16)
+    copies[3].wait()
+    grad = grad_ref[...]
+    writes = []
+    for g in range(owners // group - 1, -1, -1):
+        chosen = hot16(index, *[s - jnp.int16(g * rows) for s in slots])
+        picked = jnp.dot(chosen, grad, preferred_element_type=F32)
+        picked = picked.astype(BF)
+        for k in range(group):
+            part = picked[k * cap : (k + 1) * cap]
+            out_ref, at = (own_ref, other_ref)[(g * group + k) // chips], (g * group + k) % chips
+            out_ref[at, 0:cap, :] = part[:, :LANES]
+            out_ref[at, cap : 2 * cap, :] = part[:, LANES:]
+        side = g * group // chips
+        some = pl.ds(g * group % chips, group)
+        write = pltpu.make_async_copy(
+            (own_ref, other_ref)[side].at[some], (own_hbm, other_hbm)[side].at[some], out_sems.at[g]
+        )
+        write.start()
+        writes.append(write)
+    for write in writes:
+        write.wait()
+
+
+def place_kernel(own_ref, out_ref):
+    out_ref[...] = own_ref[...]
 
 
 def merge_kernel(own_ref, got_ref, turn_ref, out_ref):
@@ -186,17 +201,23 @@
         out_ref[k, part : part + 2 * shards, :] = both
 
 
-def average_kernel(got_ref, out_ref, state_ref):
+def average_kernel(got_ref, out_ref):
+    replicas, part, _ = out_ref.shape
+    total = got_ref[0, 0:part, :].astype(F32)
+    for r in range(1, replicas):
+        total = total + got_ref[r, 0:part, :].astype(F32)
+    table = (total * (1.0 / replicas)).astype(BF)
+    for r in range(replicas):
+        out_ref[r, :, :] = table
+
+
+def state_kernel(got_ref, state_ref):
     replicas, rows, embed = got_ref.shape
     part = rows - 2 * replicas
-    total = got_ref[0].astype(F32)
+    total = got_ref[0, part:, :].astype(F32)
     for r in range(1, replicas):
-        total = total + got_ref[r].astype(F32)
-    total = total * (1.0 / replicas)
-    table = total[:part].astype(BF)
-    for r in range(replicas):
-        out_ref[r, :, :] = table
-    state = total[part : part + replicas] + total[part + replicas :]
+        total = total + got_ref[r, part:, :].astype(F32)
+    state = (total[:replicas] + total[replicas:]) * (1.0 / replicas)
     wide = state_ref.shape[1] // embed
     for k in range(replicas):
         at = (k % wide) * embed
@@ -230,13 +251,16 @@
             jax.ShapeDtypeStruct((IDS, LANES), BF),
         ),
         in_specs=[ANY, ANY, ANY, ANY],
-        out_specs=(VMEM, VMEM, VMEM),
+        out_specs=(ANY, ANY, VMEM),
         scratch_shapes=[
+            pltpu.VMEM((chips, 2 * cap + IDS, LANES), BF),
+            pltpu.VMEM((chips, 2 * cap + IDS, LANES), BF),
             pltpu.SMEM((features,), jnp.int32),
             pltpu.VMEM((features * pool, samples), jnp.int32),
             pltpu.VMEM((features * pool, samples), jnp.int32),
             pltpu.VMEM((samples * features, embed), BF),
             pltpu.SemaphoreType.DMA((4,)),
+            pltpu.SemaphoreType.DMA((owners // 8,)),
         ],
         compiler_params=ALL_VMEM,
         name="pack",
@@ -245,6 +269,14 @@
     for _ in range(TURNS):
         ring = [(2 * i + 1, 2 * ((i + 1) % chips) + 1) for i in range(chips)]
         turn = lax.ppermute(turn, ("yx", "core"), ring)
+    placed = pl.pallas_call(
+        place_kernel,
+        out_shape=jax.ShapeDtypeStruct((chips, 2 * cap + IDS, LANES), BF),
+        in_specs=[VMEM],
+        out_specs=VMEM,
+        compiler_params=PARAMS,
+        name="place",
+    )(own)
     send = pl.pallas_call(
         merge_kernel,
         out_shape=jax.ShapeDtypeStruct((chips, 4 * cap + IDS, LANES), BF),
@@ -252,7 +284,7 @@
         out_specs=VMEM,
         compiler_params=PARAMS,
         name="merge",
-    )(own, got, turn)
+    )(placed, got, turn)
     received = lax.all_to_all(send, "yx", split_axis=0, concat_axis=0, tiled=True)
     updated = pl.pallas_call(
         lambda *refs: update_kernel(cap, replicas, *refs),
@@ -263,16 +295,21 @@
         name="update",
     )(received, table_rows.reshape(slots, embed), adagrad_state.reshape(slots // LANES, LANES))
     mine = lax.all_to_all(updated, "rep", split_axis=0, concat_axis=0, tiled=True)
-    copies, state = pl.pallas_call(
+    copies = pl.pallas_call(
         average_kernel,
-        out_shape=(
-            jax.ShapeDtypeStruct((replicas, part, embed), BF),
-            jax.ShapeDtypeStruct((tables, rows_dev), F32),
-        ),
+        out_shape=jax.ShapeDtypeStruct((replicas, part, embed), BF),
         in_specs=[VMEM],
-        out_specs=(VMEM, VMEM),
+        out_specs=VMEM,
         compiler_params=PARAMS,
         name="average",
+    )(mine)
+    state = pl.pallas_call(
+        state_kernel,
+        out_shape=jax.ShapeDtypeStruct((tables, rows_dev), F32),
+        in_specs=[VMEM],
+        out_specs=VMEM,
+        compiler_params=PARAMS,
+        name="state",
     )(mine)
     full = lax.all_to_all(copies, "rep", split_axis=0, concat_axis=0, tiled=True)
     return full.reshape(tables, rows_dev, embed), state

time: 131 us -> 132 us (level)
  blocking collectives: 60.4 us -> 33.6 us
  waiting for transfers between devices: 30.7 us -> 53 us
  starting transfers between devices: 25.2 us -> 28.5 us
  Pallas kernels: 11.2 us -> 13.4 us
    all_to_all x1 -> x0, blocking collectives: 26.8 us -> none  [shards_fn(): lax.all_to_all(copies, 'rep', split_axis=0, concat_axis=0, tiled=True)]
    all_to_all x0 -> x1, waiting for transfers between devices: none -> 23.2 us  [shards_fn(): lax.all_to_all(copies, 'rep', split_axis=0, concat_axis=0, tiled=True)]
    all_to_all x0 -> x1, starting transfers between devices: none -> 3.56 us  [shards_fn(): lax.all_to_all(copies, 'rep', split_axis=0, concat_axis=0, tiled=True)]
  transfers between devices with their start and end apart: 4 -> 5, of which waited for: 3 -> 3; matrix products, arithmetic and copies ran while one was open for 0% -> 0% of each run, Pallas kernels for 0% -> 1%
where the time goes in v6:
time: 132 us; the launch traced here: 131 us
  waiting for transfers between devices  53 us (40%)
  blocking collectives  33.6 us (25%)
  starting transfers between devices  28.5 us (22%)
  Pallas kernels  13.4 us (10%)
  local copies, waits for them, and re-layouts  2.14 us (2%)
    all_to_all x1, blocking collectives, shards_fn(): lax.all_to_all(updated, 'rep', split_axis=0, concat_axis=0, tiled=True)  33.6 us
    all_to_all x1, waiting for transfers between devices, shards_fn(): lax.all_to_all(send, 'yx', split_axis=0, concat_axis=0, tiled=True)  28.3 us
    all_to_all x1, waiting for transfers between devices, shards_fn(): lax.all_to_all(copies, 'rep', split_axis=0, concat_axis=0, tiled=True)  23.2 us
    all_to_all x1, starting transfers between devices, shards_fn(): lax.all_to_all(send, 'yx', split_axis=0, concat_axis=0, tiled=True)  14 us
    ppermute x2, starting transfers between devices, shards_fn(): turn = lax.ppermute(turn, ('yx', 'core'), ring)  8.34 us
    pallas_call x1, Pallas kernels, shards_fn(): pl.pallas_call(lambda *refs: pack_kernel(owners, cap, rows_dev, *refs), o...  6.15 us
    pallas_call x1, Pallas kernels, shards_fn(): pl.pallas_call(lambda *refs: update_kernel(cap, replicas, *refs), out_sha...  4.13 us
    all_to_all x1, starting transfers between devices, shards_fn(): lax.all_to_all(copies, 'rep', split_axis=0, concat_axis=0, tiled=True)  3.56 us
  transfers between devices with their start and end apart: 5, of which 3 were waited for; matrix products, arithmetic and copies ran while one was open for 0% of the time, Pallas kernels for 1%

profile of v6, /device:TPU:15, one launch (start us, length us, event | category | flops | bytes accessed | tf_op | source)
XLA Modules:
  0.0 131.3 jit_solution(719630438789867094)
XLA Ops:
  0.6 6.2 %pack.1 = (bf16[32,104,128]{2,1,0:T(8,128)(2,1)}, bf16[32,104,128]{2,1,0:T(8,128)(2,1)}, bf16[8,128]{1,0:T(8,128)(2,1)}) custom-call(s32[8]{0:T(128)} %refs_0_.1, s32[16,128]{1,0:T(8,128)} %bitcast.14, s32[16,128]{1,0:T(8,128)} %bitcast.15, bf16[1024,256]{1,0:T(8,128)(2,1)} %bitcast.13), custom_call_target="tpu_custom_call" | custom-call | tf_op jit(solution)/shard_map/pack/pallas_call | solution.py:246
  6.8 2.6 %collective-permute-start = (bf16[32,104,128]{2,1,0:T(8,128)(2,1)}, bf16[32,104,128]{2,1,0:T(8,128)(2,1)S(1)}, u32[]{:S(2)}, u32[]{:S(2)}) collective-permute-start(bf16[32,104,128]{2,1,0:T(8,128)(2,1)} %get-tuple-element.6), channel_id=1, source_target_pairs={{0,1},{1,0},{2,3},{3,2},{4,5},{5,4},{6,7},{7,6},{8,9},{9,8},{10,11... | collective-permute-start | bytes 2555912 | tf_op jit(solution)/shard_map/ppermute | solution.py:268
  9.4 3.1 %collective-permute-start.1 = (bf16[8,128]{1,0:T(8,128)(2,1)}, bf16[8,128]{1,0:T(8,128)(2,1)S(1)}, u32[]{:S(2)}, u32[]{:S(2)}) collective-permute-start(bf16[8,128]{1,0:T(8,128)(2,1)} %get-tuple-element.7), channel_id=1, source_target_pairs={{1,3},{3,5},{5,7},{7,9},{9,11},{11,13},{13,15},{15,17},{17,19},{19... | collective-permute-start | bytes 6152 | tf_op jit(solution)/shard_map/ppermute | solution.py:271
  12.5 1.4 %collective-permute-done.1 = bf16[8,128]{1,0:T(8,128)(2,1)S(1)} collective-permute-done((bf16[8,128]{1,0:T(8,128)(2,1)}, bf16[8,128]{1,0:T(8,128)(2,1)S(1)}, u32[]{:S(2)}, u32[]{:S(2)}) %collective-permute-start.1) | collective-permute-done | bytes 2080 | tf_op jit(solution)/shard_map/ppermute | solution.py:271
  13.9 5.2 %collective-permute-start.2 = (bf16[8,128]{1,0:T(8,128)(2,1)S(1)}, bf16[8,128]{1,0:T(8,128)(2,1)S(1)}, u32[]{:S(2)}, u32[]{:S(2)}) collective-permute-start(bf16[8,128]{1,0:T(8,128)(2,1)S(1)} %collective-permute-done.1), channel_id=1, source_target_pairs={{1,3},{3,5},{5,7},{7,9},{9,11},{11,13},{13,15},{15,17},{17,19},{19... | collective-permute-start | bytes 6152 | tf_op jit(solution)/shard_map/ppermute | solution.py:271
  19.1 0.0 copy-start.1
  19.2 1.1 copy-done.1
  20.3 0.1 place.1.own_ref
  20.4 0.0 collective-permute-done.2.turn_ref
  20.4 0.0 collective-permute-done.got_ref
  20.4 1.3 %merge.1 = bf16[32,200,128]{2,1,0:T(8,128)(2,1)} custom-call(bf16[32,104,128]{2,1,0:T(8,128)(2,1)S(1)} %place.1.own_ref, bf16[32,104,128]{2,1,0:T(8,128)(2,1)S(1)} %collective-permute-done.got_ref, bf16[8,128]{1,0:T(8,128)(2,1)S(1)} %collective-permute-done.2.turn_ref), custom_call_target="tpu_custom_call" | custom-call | tf_op jit(solution)/shard_map/merge/pallas_call | solution.py:280
  21.7 0.0 copy-start.2
  21.7 0.0 copy-start
  21.7 14.0 %all-to-all-start = ((bf16[32,200,128]{2,1,0:T(8,128)(2,1)}), bf16[32,200,128]{2,1,0:T(8,128)(2,1)S(1)}, u32[]{:S(2)}, u32[]{:S(2)}) async-start(bf16[32,200,128]{2,1,0:T(8,128)(2,1)} %merge.1), calls=%async_computation | async-start | bytes 3276800 | tf_op jit(solution)/shard_map/all_to_all | solution.py:288
  35.8 0.0 copy-done.2
  35.8 28.3 %all-to-all-done.refs_0_ = bf16[32,200,128]{2,1,0:T(8,128)(2,1)S(1)} async-done(((bf16[32,200,128]{2,1,0:T(8,128)(2,1)}), bf16[32,200,128]{2,1,0:T(8,128)(2,1)S(1)}, u32[]{:S(2)}, u32[]{:S(2)}) %all-to-all-start) | async-done | bytes 1638432 | tf_op jit(solution)/shard_map/all_to_all | solution.py:288
  64.1 0.0 copy-done
  64.1 4.1 %update.1 = bf16[8,272,256]{2,1,0:T(8,128)(2,1)S(1)} custom-call(bf16[32,200,128]{2,1,0:T(8,128)(2,1)S(1)} %all-to-all-done.refs_0_, bf16[2048,256]{1,0:T(8,128)(2,1)S(1)} %bitcast.11, f32[16,128]{1,0:T(8,128)S(1)} %reshape.26.refs_2_), custom_call_target="tpu_custom_call" | custom-call | tf_op jit(solution)/shard_map/update/pallas_call | solution.py:289
  68.2 33.6 %all_to_all.15.got_ref = bf16[8,272,256]{2,1,0:T(8,128)(2,1)S(1)} all-to-all(bf16[8,272,256]{2,1,0:T(8,128)(2,1)S(1)} %update.1), channel_id=1, replica_groups=mesh['rep'=8,'yx'=32,'core'=2] {'rep'}, dimensions={0} | all-to-all | bytes 2228224 | tf_op jit(solution)/shard_map/all_to_all | solution.py:297
  101.8 1.1 average.1
  102.9 3.6 %all-to-all-start.2 = ((bf16[8,256,256]{2,1,0:T(8,128)(2,1)}), bf16[8,256,256]{2,1,0:T(8,128)(2,1)S(1)}, u32[]{:S(2)}, u32[]{:S(2)}) async-start(bf16[8,256,256]{2,1,0:T(8,128)(2,1)} %average.1), calls=%async_computation.2 | async-start | bytes 2097152 | tf_op jit(solution)/shard_map/all_to_all | solution.py:314
  106.5 0.6 state.1
  107.1 23.2 %all-to-all-done.2 = bf16[8,256,256]{2,1,0:T(8,128)(2,1)S(1)} async-done(((bf16[8,256,256]{2,1,0:T(8,128)(2,1)}), bf16[8,256,256]{2,1,0:T(8,128)(2,1)S(1)}, u32[]{:S(2)}, u32[]{:S(2)}) %all-to-all-start.2) | async-done | bytes 1048608 | tf_op jit(solution)/shard_map/all_to_all | solution.py:314
  130.4 1.0 copy.9
  (1 shorter events, 0.0 us)
Async XLA Ops:
  6.8 13.6 %collective-permute-start = (bf16[32,104,128]{2,1,0:T(8,128)(2,1)}, bf16[32,104,128]{2,1,0:T(8,128)(2,1)S(1)}, u32[]{:S(2)}, u32[]{:S(2)}) collective-permute-start(bf16[32,104,128]{2,1,0:T(8,128)(2,1)} %get-tuple-element.6), channel_id=1, source_target_pairs={{0,1},{1,0},{2,3},{3,2},{4,5},{5,4},{6,7},{7,6},{8,9},{9,8},{10,11... | collective-permute-start | bytes 2555912 | tf_op jit(solution)/shard_map/ppermute | solution.py:268
  9.4 4.5 %collective-permute-start.1 = (bf16[8,128]{1,0:T(8,128)(2,1)}, bf16[8,128]{1,0:T(8,128)(2,1)S(1)}, u32[]{:S(2)}, u32[]{:S(2)}) collective-permute-start(bf16[8,128]{1,0:T(8,128)(2,1)} %get-tuple-element.7), channel_id=1, source_target_pairs={{1,3},{3,5},{5,7},{7,9},{9,11},{11,13},{13,15},{15,17},{17,19},{19... | collective-permute-start | bytes 6152 | tf_op jit(solution)/shard_map/ppermute | solution.py:271
  13.9 6.4 %collective-permute-start.2 = (bf16[8,128]{1,0:T(8,128)(2,1)S(1)}, bf16[8,128]{1,0:T(8,128)(2,1)S(1)}, u32[]{:S(2)}, u32[]{:S(2)}) collective-permute-start(bf16[8,128]{1,0:T(8,128)(2,1)S(1)} %collective-permute-done.1), channel_id=1, source_target_pairs={{1,3},{3,5},{5,7},{7,9},{9,11},{11,13},{13,15},{15,17},{17,19},{19... | collective-permute-start | bytes 6152 | tf_op jit(solution)/shard_map/ppermute | solution.py:271
  19.1 1.2 copy-start.1
  21.7 14.1 %copy-start.2 = (f32[2,1024]{1,0:T(2,128)S(1)}, f32[2,1024]{1,0:T(2,128)}, u32[]{:S(2)}) copy-start(f32[2,1024]{1,0:T(2,128)} %param.11) | copy-start | bytes 24580
  21.7 42.4 %copy-start = (bf16[2,1024,256]{2,1,0:T(8,128)(2,1)S(1)}, bf16[2,1024,256]{2,1,0:T(8,128)(2,1)}, u32[]{:S(2)}) copy-start(bf16[2,1024,256]{2,1,0:T(8,128)(2,1)} %param.10) | copy-start | bytes 3145732
  21.7 42.4 %all-to-all-start = ((bf16[32,200,128]{2,1,0:T(8,128)(2,1)}), bf16[32,200,128]{2,1,0:T(8,128)(2,1)S(1)}, u32[]{:S(2)}, u32[]{:S(2)}) async-start(bf16[32,200,128]{2,1,0:T(8,128)(2,1)} %merge.1), calls=%async_computation | async-start | bytes 3276800 | tf_op jit(solution)/shard_map/all_to_all | solution.py:288
  102.9 27.4 %all-to-all-start.2 = ((bf16[8,256,256]{2,1,0:T(8,128)(2,1)}), bf16[8,256,256]{2,1,0:T(8,128)(2,1)S(1)}, u32[]{:S(2)}, u32[]{:S(2)}) async-start(bf16[8,256,256]{2,1,0:T(8,128)(2,1)} %average.1), calls=%async_computation.2 | async-start | bytes 2097152 | tf_op jit(solution)/shard_map/all_to_all | solution.py:314

commit v7 on v5

--- a/solution.py
+++ b/solution.py
@@ -118,24 +118,32 @@
     turn_ref[...] = jnp.zeros((IDS, LANES), BF)
 
 
-def merge_kernel(own_ref, got_ref, turn_ref, out_ref):
+def place_kernel(own_ref, out_ref):
+    out_ref[...] = own_ref[...]
+
+
+def merge_kernel(own_ref, got_ref, turn_ref, out_ref, sem):
     rows = own_ref.shape[1] - IDS
-    first = lax.axis_index("core") == 0
-
-    @pl.when(first)
+    core = lax.axis_index("core")
+
+    def merge(own_at, got_at):
+        came = got_ref.at[:, pl.ds(0, rows), :]
+        copy = pltpu.make_async_copy(came, out_ref.at[:, pl.ds(got_at, rows), :], sem)
+        copy.start()
+        out_ref[:, own_at : own_at + rows, :] = own_ref[:, 0:rows, :]
+        ids = own_ref[:, rows:, :].astype(F32) + got_ref[:, rows:, :].astype(F32)
+        out_ref[:, 2 * rows :, :] = ids.astype(BF)
+        turn = jnp.where(iota((IDS, LANES), 0) < 6, ids[0], turn_ref[...].astype(F32))
+        out_ref[0, 2 * rows :, :] = turn.astype(BF)
+        copy.wait()
+
+    @pl.when(core == 0)
     def _():
-        out_ref[:, 0:rows, :] = own_ref[:, 0:rows, :]
-        out_ref[:, rows : 2 * rows, :] = got_ref[:, 0:rows, :]
-
-    @pl.when(jnp.logical_not(first))
+        merge(0, rows)
+
+    @pl.when(core == 1)
     def _():
-        out_ref[:, 0:rows, :] = got_ref[:, 0:rows, :]
-        out_ref[:, rows : 2 * rows, :] = own_ref[:, 0:rows, :]
-
-    ids = own_ref[:, rows:, :].astype(F32) + got_ref[:, rows:, :].astype(F32)
-    out_ref[:, 2 * rows :, :] = ids.astype(BF)
-    turn = jnp.where(iota((IDS, LANES), 0) < 6, ids[0], turn_ref[...].astype(F32))
-    out_ref[0, 2 * rows :, :] = turn.astype(BF)
+        merge(rows, 0)
 
 
 def update_kernel(cap, shards, recv_ref, table_ref, state_ref, out_ref):
@@ -245,14 +253,23 @@
     for _ in range(TURNS):
         ring = [(2 * i + 1, 2 * ((i + 1) % chips) + 1) for i in range(chips)]
         turn = lax.ppermute(turn, ("yx", "core"), ring)
+    placed = pl.pallas_call(
+        place_kernel,
+        out_shape=jax.ShapeDtypeStruct(own.shape, BF),
+        in_specs=[VMEM],
+        out_specs=VMEM,
+        compiler_params=PARAMS,
+        name="place",
+    )(own)
     send = pl.pallas_call(
         merge_kernel,
         out_shape=jax.ShapeDtypeStruct((chips, 4 * cap + IDS, LANES), BF),
         in_specs=[VMEM, VMEM, VMEM],
         out_specs=VMEM,
+        scratch_shapes=[pltpu.SemaphoreType.DMA],
         compiler_params=PARAMS,
         name="merge",
-    )(own, got, turn)
+    )(placed, got, turn)
     received = lax.all_to_all(send, "yx", split_axis=0, concat_axis=0, tiled=True)
     updated = pl.pallas_call(
         lambda *refs: update_kernel(cap, replicas, *refs),

time: 131 us -> 130 us (level)
  transfers between devices with their start and end apart: 4 -> 4, of which waited for: 3 -> 2; matrix products, arithmetic and copies ran while one was open for 0% -> 0% of each run, Pallas kernels for 0% -> 0%
where the time goes in v7:
time: 130 us
  blocking collectives  60.8 us (47%)
  waiting for transfers between devices  29.7 us (23%)
  starting transfers between devices  25 us (19%)
  Pallas kernels  11.3 us (9%)
  local copies, waits for them, and re-layouts  2.15 us (2%)
    all_to_all x1, blocking collectives, shards_fn(): lax.all_to_all(updated, 'rep', split_axis=0, concat_axis=0, tiled=True)  33.6 us
    all_to_all x1, waiting for transfers between devices, shards_fn(): lax.all_to_all(send, 'yx', split_axis=0, concat_axis=0, tiled=True)  28.3 us
    all_to_all x1, blocking collectives, shards_fn(): lax.all_to_all(copies, 'rep', split_axis=0, concat_axis=0, tiled=True)  27.2 us
    all_to_all x1, starting transfers between devices, shards_fn(): lax.all_to_all(send, 'yx', split_axis=0, concat_axis=0, tiled=True)  14.1 us
    ppermute x2, starting transfers between devices, shards_fn(): turn = lax.ppermute(turn, ('yx', 'core'), ring)  8.34 us
    pallas_call x1, Pallas kernels, shards_fn(): pl.pallas_call(lambda *refs: pack_kernel(owners, cap, rows_dev, *refs), o...  5.18 us
    pallas_call x1, Pallas kernels, shards_fn(): pl.pallas_call(lambda *refs: update_kernel(cap, replicas, *refs), out_sha...  4.13 us
  transfers between devices with their start and end apart: 4, of which 2 were waited for; matrix products, arithmetic and copies ran while one was open for 0% of the time, Pallas kernels for 0%

profile of v7, /device:TPU:15, one launch (start us, length us, event | category | flops | bytes accessed | tf_op | source)
XLA Modules:
  0.0 129.7 jit_solution(17106817524527731464)
XLA Ops:
  0.6 5.2 %pack.1 = (bf16[32,104,128]{2,1,0:T(8,128)(2,1)}, bf16[32,104,128]{2,1,0:T(8,128)(2,1)}, bf16[8,128]{1,0:T(8,128)(2,1)}) custom-call(s32[8]{0:T(128)} %refs_0_.1, s32[16,128]{1,0:T(8,128)} %bitcast.14, s32[16,128]{1,0:T(8,128)} %bitcast.15, bf16[1024,256]{1,0:T(8,128)(2,1)} %bitcast.13), custom_call_target="tpu_custom_call" | custom-call | tf_op jit(solution)/shard_map/pack/pallas_call | solution.py:233
  5.8 2.6 %collective-permute-start = (bf16[32,104,128]{2,1,0:T(8,128)(2,1)}, bf16[32,104,128]{2,1,0:T(8,128)(2,1)S(1)}, u32[]{:S(2)}, u32[]{:S(2)}) collective-permute-start(bf16[32,104,128]{2,1,0:T(8,128)(2,1)} %get-tuple-element.8), channel_id=1, source_target_pairs={{0,1},{1,0},{2,3},{3,2},{4,5},{5,4},{6,7},{7,6},{8,9},{9,8},{10,11... | collective-permute-start | bytes 2555912 | tf_op jit(solution)/shard_map/ppermute | solution.py:252
  8.4 3.1 %collective-permute-start.1 = (bf16[8,128]{1,0:T(8,128)(2,1)}, bf16[8,128]{1,0:T(8,128)(2,1)S(1)}, u32[]{:S(2)}, u32[]{:S(2)}) collective-permute-start(bf16[8,128]{1,0:T(8,128)(2,1)} %get-tuple-element.9), channel_id=1, source_target_pairs={{1,3},{3,5},{5,7},{7,9},{9,11},{11,13},{13,15},{15,17},{17,19},{19... | collective-permute-start | bytes 6152 | tf_op jit(solution)/shard_map/ppermute | solution.py:255
  11.5 1.4 %collective-permute-done.1 = bf16[8,128]{1,0:T(8,128)(2,1)S(1)} collective-permute-done((bf16[8,128]{1,0:T(8,128)(2,1)}, bf16[8,128]{1,0:T(8,128)(2,1)S(1)}, u32[]{:S(2)}, u32[]{:S(2)}) %collective-permute-start.1) | collective-permute-done | bytes 2080 | tf_op jit(solution)/shard_map/ppermute | solution.py:255
  12.9 5.2 %collective-permute-start.2 = (bf16[8,128]{1,0:T(8,128)(2,1)S(1)}, bf16[8,128]{1,0:T(8,128)(2,1)S(1)}, u32[]{:S(2)}, u32[]{:S(2)}) collective-permute-start(bf16[8,128]{1,0:T(8,128)(2,1)S(1)} %collective-permute-done.1), channel_id=1, source_target_pairs={{1,3},{3,5},{5,7},{7,9},{9,11},{11,13},{13,15},{15,17},{17,19},{19... | collective-permute-start | bytes 6152 | tf_op jit(solution)/shard_map/ppermute | solution.py:255
  18.2 0.0 copy-start.1
  18.2 1.1 copy-done.1
  19.3 0.1 place.1.own_ref
  19.4 0.0 collective-permute-done.2.turn_ref
  19.4 0.0 collective-permute-done.got_ref
  19.4 1.3 %merge.1 = bf16[32,200,128]{2,1,0:T(8,128)(2,1)} custom-call(bf16[32,104,128]{2,1,0:T(8,128)(2,1)S(1)} %place.1.own_ref, bf16[32,104,128]{2,1,0:T(8,128)(2,1)S(1)} %collective-permute-done.got_ref, bf16[8,128]{1,0:T(8,128)(2,1)S(1)} %collective-permute-done.2.turn_ref), custom_call_target="tpu_custom_call" | custom-call | tf_op jit(solution)/shard_map/merge/pallas_call | solution.py:264
  20.7 0.0 copy-start.2
  20.8 0.0 copy-start
  20.8 14.1 %all-to-all-start = ((bf16[32,200,128]{2,1,0:T(8,128)(2,1)}), bf16[32,200,128]{2,1,0:T(8,128)(2,1)S(1)}, u32[]{:S(2)}, u32[]{:S(2)}) async-start(bf16[32,200,128]{2,1,0:T(8,128)(2,1)} %merge.1), calls=%async_computation | async-start | bytes 3276800 | tf_op jit(solution)/shard_map/all_to_all | solution.py:273
  34.8 0.0 copy-done.2
  34.9 28.3 %all-to-all-done.refs_0_ = bf16[32,200,128]{2,1,0:T(8,128)(2,1)S(1)} async-done(((bf16[32,200,128]{2,1,0:T(8,128)(2,1)}), bf16[32,200,128]{2,1,0:T(8,128)(2,1)S(1)}, u32[]{:S(2)}, u32[]{:S(2)}) %all-to-all-start) | async-done | bytes 1638432 | tf_op jit(solution)/shard_map/all_to_all | solution.py:273
  63.2 0.0 copy-done
  63.2 4.1 %update.1 = bf16[8,272,256]{2,1,0:T(8,128)(2,1)S(1)} custom-call(bf16[32,200,128]{2,1,0:T(8,128)(2,1)S(1)} %all-to-all-done.refs_0_, bf16[2048,256]{1,0:T(8,128)(2,1)S(1)} %bitcast.11, f32[16,128]{1,0:T(8,128)S(1)} %reshape.26.refs_2_), custom_call_target="tpu_custom_call" | custom-call | tf_op jit(solution)/shard_map/update/pallas_call | solution.py:274
  67.3 33.6 %all_to_all.15.got_ref = bf16[8,272,256]{2,1,0:T(8,128)(2,1)S(1)} all-to-all(bf16[8,272,256]{2,1,0:T(8,128)(2,1)S(1)} %update.1), channel_id=1, replica_groups=mesh['rep'=8,'yx'=32,'core'=2] {'rep'}, dimensions={0} | all-to-all | bytes 2228224 | tf_op jit(solution)/shard_map/all_to_all | solution.py:282
  100.9 0.6 average.1
  101.5 27.2 %all_to_all.16 = bf16[8,256,256]{2,1,0:T(8,128)(2,1)S(1)} all-to-all(bf16[8,256,256]{2,1,0:T(8,128)(2,1)S(1)} %get-tuple-element.10), channel_id=1, replica_groups=mesh['rep'=8,'yx'=32,'core'=2] {'rep'}, dimensions={0} | all-to-all | bytes 2097152 | tf_op jit(solution)/shard_map/all_to_all | solution.py:294
  128.7 1.0 copy.9
  (1 shorter events, 0.0 us)
Async XLA Ops:
  5.8 13.6 %collective-permute-start = (bf16[32,104,128]{2,1,0:T(8,128)(2,1)}, bf16[32,104,128]{2,1,0:T(8,128)(2,1)S(1)}, u32[]{:S(2)}, u32[]{:S(2)}) collective-permute-start(bf16[32,104,128]{2,1,0:T(8,128)(2,1)} %get-tuple-element.8), channel_id=1, source_target_pairs={{0,1},{1,0},{2,3},{3,2},{4,5},{5,4},{6,7},{7,6},{8,9},{9,8},{10,11... | collective-permute-start | bytes 2555912 | tf_op jit(solution)/shard_map/ppermute | solution.py:252
  8.4 4.5 %collective-permute-start.1 = (bf16[8,128]{1,0:T(8,128)(2,1)}, bf16[8,128]{1,0:T(8,128)(2,1)S(1)}, u32[]{:S(2)}, u32[]{:S(2)}) collective-permute-start(bf16[8,128]{1,0:T(8,128)(2,1)} %get-tuple-element.9), channel_id=1, source_target_pairs={{1,3},{3,5},{5,7},{7,9},{9,11},{11,13},{13,15},{15,17},{17,19},{19... | collective-permute-start | bytes 6152 | tf_op jit(solution)/shard_map/ppermute | solution.py:255
  12.9 6.4 %collective-permute-start.2 = (bf16[8,128]{1,0:T(8,128)(2,1)S(1)}, bf16[8,128]{1,0:T(8,128)(2,1)S(1)}, u32[]{:S(2)}, u32[]{:S(2)}) collective-permute-start(bf16[8,128]{1,0:T(8,128)(2,1)S(1)} %collective-permute-done.1), channel_id=1, source_target_pairs={{1,3},{3,5},{5,7},{7,9},{9,11},{11,13},{13,15},{15,17},{17,19},{19... | collective-permute-start | bytes 6152 | tf_op jit(solution)/shard_map/ppermute | solution.py:255
  18.2 1.2 copy-start.1
  20.7 14.1 %copy-start.2 = (f32[2,1024]{1,0:T(2,128)S(1)}, f32[2,1024]{1,0:T(2,128)}, u32[]{:S(2)}) copy-start(f32[2,1024]{1,0:T(2,128)} %param.11) | copy-start | bytes 24580
  20.8 42.4 %copy-start = (bf16[2,1024,256]{2,1,0:T(8,128)(2,1)S(1)}, bf16[2,1024,256]{2,1,0:T(8,128)(2,1)}, u32[]{:S(2)}) copy-start(bf16[2,1024,256]{2,1,0:T(8,128)(2,1)} %param.10) | copy-start | bytes 3145732
  20.8 42.4 %all-to-all-start = ((bf16[32,200,128]{2,1,0:T(8,128)(2,1)}), bf16[32,200,128]{2,1,0:T(8,128)(2,1)S(1)}, u32[]{:S(2)}, u32[]{:S(2)}) async-start(bf16[32,200,128]{2,1,0:T(8,128)(2,1)} %merge.1), calls=%async_computation | async-start | bytes 3276800 | tf_op jit(solution)/shard_map/all_to_all | solution.py:273

commit v8 on v7

--- a/solution.py
+++ b/solution.py
@@ -8,7 +8,7 @@
 BF = jnp.bfloat16
 F32 = jnp.float32
 LANES = 128
-TURNS = 2
+TURNS = 3
 IDS = 8
 
 
@@ -251,8 +251,8 @@
     )(feature_table, owner, local, pooled_grad.reshape(samples * features, embed))
     got = lax.ppermute(other, "core", [(0, 1), (1, 0)])
     for _ in range(TURNS):
-        ring = [(2 * i + 1, 2 * ((i + 1) % chips) + 1) for i in range(chips)]
-        turn = lax.ppermute(turn, ("yx", "core"), ring)
+        neighbours = [(2 * i + 1, 2 * (i ^ 1) + 1) for i in range(chips)]
+        turn = lax.ppermute(turn, ("yx", "core"), neighbours)
     placed = pl.pallas_call(
         place_kernel,
         out_shape=jax.ShapeDtypeStruct(own.shape, BF),

time: 130 us -> 131 us (level)
  the two profiles are of different devices: /device:TPU:15 before, /device:TPU:5 now
where the time goes in v8:
time: 131 us
  blocking collectives  60.9 us (46%)
  waiting for transfers between devices  35 us (27%)
  starting transfers between devices  20.8 us (16%)
  Pallas kernels  11.3 us (9%)
  local copies, waits for them, and re-layouts  2.15 us (2%)
    all_to_all x1, blocking collectives, shards_fn(): lax.all_to_all(updated, 'rep', split_axis=0, concat_axis=0, tiled=True)  33.7 us
    all_to_all x1, waiting for transfers between devices, shards_fn(): lax.all_to_all(send, 'yx', split_axis=0, concat_axis=0, tiled=True)  31.5 us
    all_to_all x1, blocking collectives, shards_fn(): lax.all_to_all(copies, 'rep', split_axis=0, concat_axis=0, tiled=True)  27.2 us
    all_to_all x1, starting transfers between devices, shards_fn(): lax.all_to_all(send, 'yx', split_axis=0, concat_axis=0, tiled=True)  9.81 us
    ppermute x3, starting transfers between devices, shards_fn(): turn = lax.ppermute(turn, ('yx', 'core'), neighbours)  8.46 us
    pallas_call x1, Pallas kernels, shards_fn(): pl.pallas_call(lambda *refs: pack_kernel(owners, cap, rows_dev, *refs), o...  5.19 us
    pallas_call x1, Pallas kernels, shards_fn(): pl.pallas_call(lambda *refs: update_kernel(cap, replicas, *refs), out_sha...  4.13 us
    ppermute x3, waiting for transfers between devices, shards_fn(): turn = lax.ppermute(turn, ('yx', 'core'), neighbours)  3.48 us
  transfers between devices with their start and end apart: 5, of which 4 were waited for; matrix products, arithmetic and copies ran while one was open for 0% of the time, Pallas kernels for 0%

profile of v8, /device:TPU:5, one launch (start us, length us, event | category | flops | bytes accessed | tf_op | source)
XLA Modules:
  0.0 131.0 jit_solution(11540631715650093793)
XLA Ops:
  0.6 5.2 %pack.1 = (bf16[32,104,128]{2,1,0:T(8,128)(2,1)}, bf16[32,104,128]{2,1,0:T(8,128)(2,1)}, bf16[8,128]{1,0:T(8,128)(2,1)}) custom-call(s32[8]{0:T(128)} %refs_0_.1, s32[16,128]{1,0:T(8,128)} %bitcast.14, s32[16,128]{1,0:T(8,128)} %bitcast.15, bf16[1024,256]{1,0:T(8,128)(2,1)} %bitcast.13), custom_call_target="tpu_custom_call" | custom-call | tf_op jit(solution)/shard_map/pack/pallas_call | solution.py:233
  5.8 2.6 %collective-permute-start = (bf16[32,104,128]{2,1,0:T(8,128)(2,1)}, bf16[32,104,128]{2,1,0:T(8,128)(2,1)S(1)}, u32[]{:S(2)}, u32[]{:S(2)}) collective-permute-start(bf16[32,104,128]{2,1,0:T(8,128)(2,1)} %get-tuple-element.8), channel_id=1, source_target_pairs={{0,1},{1,0},{2,3},{3,2},{4,5},{5,4},{6,7},{7,6},{8,9},{9,8},{10,11... | collective-permute-start | bytes 2555912 | tf_op jit(solution)/shard_map/ppermute | solution.py:252
  8.4 2.8 %collective-permute-start.1 = (bf16[8,128]{1,0:T(8,128)(2,1)}, bf16[8,128]{1,0:T(8,128)(2,1)S(1)}, u32[]{:S(2)}, u32[]{:S(2)}) collective-permute-start(bf16[8,128]{1,0:T(8,128)(2,1)} %get-tuple-element.9), channel_id=1, source_target_pairs={{1,3},{3,1},{5,7},{7,5},{9,11},{11,9},{13,15},{15,13},{17,19},{19,... | collective-permute-start | bytes 6152 | tf_op jit(solution)/shard_map/ppermute | solution.py:255
  11.3 1.7 %collective-permute-done.1 = bf16[8,128]{1,0:T(8,128)(2,1)S(1)} collective-permute-done((bf16[8,128]{1,0:T(8,128)(2,1)}, bf16[8,128]{1,0:T(8,128)(2,1)S(1)}, u32[]{:S(2)}, u32[]{:S(2)}) %collective-permute-start.1) | collective-permute-done | bytes 2080 | tf_op jit(solution)/shard_map/ppermute | solution.py:255
  13.0 2.8 %collective-permute-start.2 = (bf16[8,128]{1,0:T(8,128)(2,1)S(1)}, bf16[8,128]{1,0:T(8,128)(2,1)S(1)}, u32[]{:S(2)}, u32[]{:S(2)}) collective-permute-start(bf16[8,128]{1,0:T(8,128)(2,1)S(1)} %collective-permute-done.1), channel_id=1, source_target_pairs={{1,3},{3,1},{5,7},{7,5},{9,11},{11,9},{13,15},{15,13},{17,19},{19,... | collective-permute-start | bytes 6152 | tf_op jit(solution)/shard_map/ppermute | solution.py:255
  15.8 1.5 %collective-permute-done.2 = bf16[8,128]{1,0:T(8,128)(2,1)S(1)} collective-permute-done((bf16[8,128]{1,0:T(8,128)(2,1)S(1)}, bf16[8,128]{1,0:T(8,128)(2,1)S(1)}, u32[]{:S(2)}, u32[]{:S(2)}) %collective-permute-start.2) | collective-permute-done | bytes 2080 | tf_op jit(solution)/shard_map/ppermute | solution.py:255
  17.3 2.8 %collective-permute-start.3 = (bf16[8,128]{1,0:T(8,128)(2,1)S(1)}, bf16[8,128]{1,0:T(8,128)(2,1)S(1)}, u32[]{:S(2)}, u32[]{:S(2)}) collective-permute-start(bf16[8,128]{1,0:T(8,128)(2,1)S(1)} %collective-permute-done.2), channel_id=1, source_target_pairs={{1,3},{3,1},{5,7},{7,5},{9,11},{11,9},{13,15},{15,13},{17,19},{19,... | collective-permute-start | bytes 6152 | tf_op jit(solution)/shard_map/ppermute | solution.py:255
  20.1 0.0 copy-start.1
  20.1 1.1 copy-done.1
  21.3 0.1 place.1.own_ref
  21.3 0.3 collective-permute-done.3.turn_ref
  21.6 0.0 collective-permute-done.got_ref
  21.6 1.3 %merge.1 = bf16[32,200,128]{2,1,0:T(8,128)(2,1)} custom-call(bf16[32,104,128]{2,1,0:T(8,128)(2,1)S(1)} %place.1.own_ref, bf16[32,104,128]{2,1,0:T(8,128)(2,1)S(1)} %collective-permute-done.got_ref, bf16[8,128]{1,0:T(8,128)(2,1)S(1)} %collective-permute-done.3.turn_ref), custom_call_target="tpu_custom_call" | custom-call | tf_op jit(solution)/shard_map/merge/pallas_call | solution.py:264
  22.9 0.0 copy-start.2
  22.9 0.0 copy-start
  23.0 9.8 %all-to-all-start = ((bf16[32,200,128]{2,1,0:T(8,128)(2,1)}), bf16[32,200,128]{2,1,0:T(8,128)(2,1)S(1)}, u32[]{:S(2)}, u32[]{:S(2)}) async-start(bf16[32,200,128]{2,1,0:T(8,128)(2,1)} %merge.1), calls=%async_computation | async-start | bytes 3276800 | tf_op jit(solution)/shard_map/all_to_all | solution.py:273
  32.8 0.0 copy-done.2
  32.8 31.5 %all-to-all-done.refs_0_ = bf16[32,200,128]{2,1,0:T(8,128)(2,1)S(1)} async-done(((bf16[32,200,128]{2,1,0:T(8,128)(2,1)}), bf16[32,200,128]{2,1,0:T(8,128)(2,1)S(1)}, u32[]{:S(2)}, u32[]{:S(2)}) %all-to-all-start) | async-done | bytes 1638432 | tf_op jit(solution)/shard_map/all_to_all | solution.py:273
  64.3 0.0 copy-done
  64.3 4.1 %update.1 = bf16[8,272,256]{2,1,0:T(8,128)(2,1)S(1)} custom-call(bf16[32,200,128]{2,1,0:T(8,128)(2,1)S(1)} %all-to-all-done.refs_0_, bf16[2048,256]{1,0:T(8,128)(2,1)S(1)} %bitcast.11, f32[16,128]{1,0:T(8,128)S(1)} %reshape.26.refs_2_), custom_call_target="tpu_custom_call" | custom-call | tf_op jit(solution)/shard_map/update/pallas_call | solution.py:274
  68.5 33.7 %all_to_all.15.got_ref = bf16[8,272,256]{2,1,0:T(8,128)(2,1)S(1)} all-to-all(bf16[8,272,256]{2,1,0:T(8,128)(2,1)S(1)} %update.1), channel_id=1, replica_groups=mesh['rep'=8,'yx'=32,'core'=2] {'rep'}, dimensions={0} | all-to-all | bytes 2228224 | tf_op jit(solution)/shard_map/all_to_all | solution.py:282
  102.2 0.6 average.1
  102.8 27.2 %all_to_all.16 = bf16[8,256,256]{2,1,0:T(8,128)(2,1)S(1)} all-to-all(bf16[8,256,256]{2,1,0:T(8,128)(2,1)S(1)} %get-tuple-element.10), channel_id=1, replica_groups=mesh['rep'=8,'yx'=32,'core'=2] {'rep'}, dimensions={0} | all-to-all | bytes 2097152 | tf_op jit(solution)/shard_map/all_to_all | solution.py:294
  130.0 1.0 copy.9
  (1 shorter events, 0.0 us)
Async XLA Ops:
  5.8 15.8 %collective-permute-start = (bf16[32,104,128]{2,1,0:T(8,128)(2,1)}, bf16[32,104,128]{2,1,0:T(8,128)(2,1)S(1)}, u32[]{:S(2)}, u32[]{:S(2)}) collective-permute-start(bf16[32,104,128]{2,1,0:T(8,128)(2,1)} %get-tuple-element.8), channel_id=1, source_target_pairs={{0,1},{1,0},{2,3},{3,2},{4,5},{5,4},{6,7},{7,6},{8,9},{9,8},{10,11... | collective-permute-start | bytes 2555912 | tf_op jit(solution)/shard_map/ppermute | solution.py:252
  8.4 4.5 %collective-permute-start.1 = (bf16[8,128]{1,0:T(8,128)(2,1)}, bf16[8,128]{1,0:T(8,128)(2,1)S(1)}, u32[]{:S(2)}, u32[]{:S(2)}) collective-permute-start(bf16[8,128]{1,0:T(8,128)(2,1)} %get-tuple-element.9), channel_id=1, source_target_pairs={{1,3},{3,1},{5,7},{7,5},{9,11},{11,9},{13,15},{15,13},{17,19},{19,... | collective-permute-start | bytes 6152 | tf_op jit(solution)/shard_map/ppermute | solution.py:255
  13.0 4.3 %collective-permute-start.2 = (bf16[8,128]{1,0:T(8,128)(2,1)S(1)}, bf16[8,128]{1,0:T(8,128)(2,1)S(1)}, u32[]{:S(2)}, u32[]{:S(2)}) collective-permute-start(bf16[8,128]{1,0:T(8,128)(2,1)S(1)} %collective-permute-done.1), channel_id=1, source_target_pairs={{1,3},{3,1},{5,7},{7,5},{9,11},{11,9},{13,15},{15,13},{17,19},{19,... | collective-permute-start | bytes 6152 | tf_op jit(solution)/shard_map/ppermute | solution.py:255
  17.3 4.3 %collective-permute-start.3 = (bf16[8,128]{1,0:T(8,128)(2,1)S(1)}, bf16[8,128]{1,0:T(8,128)(2,1)S(1)}, u32[]{:S(2)}, u32[]{:S(2)}) collective-permute-start(bf16[8,128]{1,0:T(8,128)(2,1)S(1)} %collective-permute-done.2), channel_id=1, source_target_pairs={{1,3},{3,1},{5,7},{7,5},{9,11},{11,9},{13,15},{15,13},{17,19},{19,... | collective-permute-start | bytes 6152 | tf_op jit(solution)/shard_map/ppermute | solution.py:255
  20.1 1.2 copy-start.1
  22.9 9.8 %copy-start.2 = (f32[2,1024]{1,0:T(2,128)S(1)}, f32[2,1024]{1,0:T(2,128)}, u32[]{:S(2)}) copy-start(f32[2,1024]{1,0:T(2,128)} %param.11) | copy-start | bytes 24580
  22.9 41.4 %copy-start = (bf16[2,1024,256]{2,1,0:T(8,128)(2,1)S(1)}, bf16[2,1024,256]{2,1,0:T(8,128)(2,1)}, u32[]{:S(2)}) copy-start(bf16[2,1024,256]{2,1,0:T(8,128)(2,1)} %param.10) | copy-start | bytes 3145732
  23.0 41.4 %all-to-all-start = ((bf16[32,200,128]{2,1,0:T(8,128)(2,1)}), bf16[32,200,128]{2,1,0:T(8,128)(2,1)S(1)}, u32[]{:S(2)}, u32[]{:S(2)}) async-start(bf16[32,200,128]{2,1,0:T(8,128)(2,1)} %merge.1), calls=%async_computation | async-start | bytes 3276800 | tf_op jit(solution)/shard_map/all_to_all | solution.py:273

commit v9 on v8

--- a/solution.py
+++ b/solution.py
@@ -8,7 +8,7 @@
 BF = jnp.bfloat16
 F32 = jnp.float32
 LANES = 128
-TURNS = 3
+STEPS = ("next", "next", "near")
 IDS = 8
 
 
@@ -250,9 +250,9 @@
         name="pack",
     )(feature_table, owner, local, pooled_grad.reshape(samples * features, embed))
     got = lax.ppermute(other, "core", [(0, 1), (1, 0)])
-    for _ in range(TURNS):
-        neighbours = [(2 * i + 1, 2 * (i ^ 1) + 1) for i in range(chips)]
-        turn = lax.ppermute(turn, ("yx", "core"), neighbours)
+    for step in STEPS:
+        to = [(i + 1) % chips if step == "next" else i ^ 1 for i in range(chips)]
+        turn = lax.ppermute(turn, ("yx", "core"), [(2 * i + 1, 2 * to[i] + 1) for i in range(chips)])
     placed = pl.pallas_call(
         place_kernel,
         out_shape=jax.ShapeDtypeStruct(own.shape, BF),

time: 131 us -> 123 us (0.939)
  the two profiles are of different devices: /device:TPU:5 before, /device:TPU:1 now
where the time goes in v9:
time: 123 us; the launch traced here: 122 us
  blocking collectives  50.9 us (41%)
  waiting for transfers between devices  38.7 us (31%)
  starting transfers between devices  18.6 us (15%)
  Pallas kernels  11.3 us (9%)
  local copies, waits for them, and re-layouts  2.15 us (2%)
    all_to_all x1, blocking collectives, shards_fn(): lax.all_to_all(updated, 'rep', split_axis=0, concat_axis=0, tiled=True)  30.6 us
    all_to_all x1, waiting for transfers between devices, shards_fn(): lax.all_to_all(send, 'yx', split_axis=0, concat_axis=0, tiled=True)  25.6 us
    all_to_all x1, blocking collectives, shards_fn(): lax.all_to_all(copies, 'rep', split_axis=0, concat_axis=0, tiled=True)  20.3 us
    ppermute x3, waiting for transfers between devices, shards_fn(): lax.ppermute(turn, ('yx', 'core'), [(2 * i + 1, 2 * to[i] + 1) for i in r...  13.1 us
    ppermute x1, starting transfers between devices, shards_fn(): got = lax.ppermute(other, 'core', [(0, 1), (1, 0)])  8.79 us
    ppermute x3, starting transfers between devices, shards_fn(): lax.ppermute(turn, ('yx', 'core'), [(2 * i + 1, 2 * to[i] + 1) for i in r...  5.74 us
    pallas_call x1, Pallas kernels, shards_fn(): pl.pallas_call(lambda *refs: pack_kernel(owners, cap, rows_dev, *refs), o...  5.19 us
    pallas_call x1, Pallas kernels, shards_fn(): pl.pallas_call(lambda *refs: update_kernel(cap, replicas, *refs), out_sha...  4.13 us
  transfers between devices with their start and end apart: 5, of which 4 were waited for; matrix products, arithmetic and copies ran while one was open for 0% of the time, Pallas kernels for 0%

profile of v9, /device:TPU:1, one launch (start us, length us, event | category | flops | bytes accessed | tf_op | source)
XLA Modules:
  0.0 122.4 jit_solution(6306189236910002152)
XLA Ops:
  0.6 5.2 %pack.1 = (bf16[32,104,128]{2,1,0:T(8,128)(2,1)}, bf16[32,104,128]{2,1,0:T(8,128)(2,1)}, bf16[8,128]{1,0:T(8,128)(2,1)}) custom-call(s32[8]{0:T(128)} %refs_0_.1, s32[16,128]{1,0:T(8,128)} %bitcast.14, s32[16,128]{1,0:T(8,128)} %bitcast.15, bf16[1024,256]{1,0:T(8,128)(2,1)} %bitcast.13), custom_call_target="tpu_custom_call" | custom-call | tf_op jit(solution)/shard_map/pack/pallas_call | solution.py:233
  5.8 8.8 %collective-permute-start = (bf16[32,104,128]{2,1,0:T(8,128)(2,1)}, bf16[32,104,128]{2,1,0:T(8,128)(2,1)S(1)}, u32[]{:S(2)}, u32[]{:S(2)}) collective-permute-start(bf16[32,104,128]{2,1,0:T(8,128)(2,1)} %get-tuple-element.8), channel_id=1, source_target_pairs={{0,1},{1,0},{2,3},{3,2},{4,5},{5,4},{6,7},{7,6},{8,9},{9,8},{10,11... | collective-permute-start | bytes 2555912 | tf_op jit(solution)/shard_map/ppermute | solution.py:252
  14.6 1.9 %collective-permute-start.1 = (bf16[8,128]{1,0:T(8,128)(2,1)}, bf16[8,128]{1,0:T(8,128)(2,1)S(1)}, u32[]{:S(2)}, u32[]{:S(2)}) collective-permute-start(bf16[8,128]{1,0:T(8,128)(2,1)} %get-tuple-element.9), channel_id=1, source_target_pairs={{1,3},{3,5},{5,7},{7,9},{9,11},{11,13},{13,15},{15,17},{17,19},{19... | collective-permute-start | bytes 6152 | tf_op jit(solution)/shard_map/ppermute | solution.py:255
  16.6 5.9 %collective-permute-done.1 = bf16[8,128]{1,0:T(8,128)(2,1)S(1)} collective-permute-done((bf16[8,128]{1,0:T(8,128)(2,1)}, bf16[8,128]{1,0:T(8,128)(2,1)S(1)}, u32[]{:S(2)}, u32[]{:S(2)}) %collective-permute-start.1) | collective-permute-done | bytes 2080 | tf_op jit(solution)/shard_map/ppermute | solution.py:255
  22.5 1.9 %collective-permute-start.2 = (bf16[8,128]{1,0:T(8,128)(2,1)S(1)}, bf16[8,128]{1,0:T(8,128)(2,1)S(1)}, u32[]{:S(2)}, u32[]{:S(2)}) collective-permute-start(bf16[8,128]{1,0:T(8,128)(2,1)S(1)} %collective-permute-done.1), channel_id=1, source_target_pairs={{1,3},{3,5},{5,7},{7,9},{9,11},{11,13},{13,15},{15,17},{17,19},{19... | collective-permute-start | bytes 6152 | tf_op jit(solution)/shard_map/ppermute | solution.py:255
  24.4 5.7 %collective-permute-done.2 = bf16[8,128]{1,0:T(8,128)(2,1)S(1)} collective-permute-done((bf16[8,128]{1,0:T(8,128)(2,1)S(1)}, bf16[8,128]{1,0:T(8,128)(2,1)S(1)}, u32[]{:S(2)}, u32[]{:S(2)}) %collective-permute-start.2) | collective-permute-done | bytes 2080 | tf_op jit(solution)/shard_map/ppermute | solution.py:255
  30.1 1.9 %collective-permute-start.3 = (bf16[8,128]{1,0:T(8,128)(2,1)S(1)}, bf16[8,128]{1,0:T(8,128)(2,1)S(1)}, u32[]{:S(2)}, u32[]{:S(2)}) collective-permute-start(bf16[8,128]{1,0:T(8,128)(2,1)S(1)} %collective-permute-done.2), channel_id=1, source_target_pairs={{1,3},{3,1},{5,7},{7,5},{9,11},{11,9},{13,15},{15,13},{17,19},{19,... | collective-permute-start | bytes 6152 | tf_op jit(solution)/shard_map/ppermute | solution.py:255
  32.0 0.0 copy-start.1
  32.1 1.1 copy-done.1
  33.2 0.1 place.1.own_ref
  33.3 1.5 %collective-permute-done.3.turn_ref = bf16[8,128]{1,0:T(8,128)(2,1)S(1)} collective-permute-done((bf16[8,128]{1,0:T(8,128)(2,1)S(1)}, bf16[8,128]{1,0:T(8,128)(2,1)S(1)}, u32[]{:S(2)}, u32[]{:S(2)}) %collective-permute-start.3) | collective-permute-done | bytes 2080 | tf_op jit(solution)/shard_map/ppermute | solution.py:255
  34.7 0.0 collective-permute-done.got_ref
  34.7 1.3 %merge.1 = bf16[32,200,128]{2,1,0:T(8,128)(2,1)} custom-call(bf16[32,104,128]{2,1,0:T(8,128)(2,1)S(1)} %place.1.own_ref, bf16[32,104,128]{2,1,0:T(8,128)(2,1)S(1)} %collective-permute-done.got_ref, bf16[8,128]{1,0:T(8,128)(2,1)S(1)} %collective-permute-done.3.turn_ref), custom_call_target="tpu_custom_call" | custom-call | tf_op jit(solution)/shard_map/merge/pallas_call | solution.py:264
  36.1 0.0 copy-start.2
  36.1 0.0 copy-start
  36.1 4.1 %all-to-all-start = ((bf16[32,200,128]{2,1,0:T(8,128)(2,1)}), bf16[32,200,128]{2,1,0:T(8,128)(2,1)S(1)}, u32[]{:S(2)}, u32[]{:S(2)}) async-start(bf16[32,200,128]{2,1,0:T(8,128)(2,1)} %merge.1), calls=%async_computation | async-start | bytes 3276800 | tf_op jit(solution)/shard_map/all_to_all | solution.py:273
  40.2 0.0 copy-done.2
  40.2 25.6 %all-to-all-done.refs_0_ = bf16[32,200,128]{2,1,0:T(8,128)(2,1)S(1)} async-done(((bf16[32,200,128]{2,1,0:T(8,128)(2,1)}), bf16[32,200,128]{2,1,0:T(8,128)(2,1)S(1)}, u32[]{:S(2)}, u32[]{:S(2)}) %all-to-all-start) | async-done | bytes 1638432 | tf_op jit(solution)/shard_map/all_to_all | solution.py:273
  65.8 0.0 copy-done
  65.8 4.1 %update.1 = bf16[8,272,256]{2,1,0:T(8,128)(2,1)S(1)} custom-call(bf16[32,200,128]{2,1,0:T(8,128)(2,1)S(1)} %all-to-all-done.refs_0_, bf16[2048,256]{1,0:T(8,128)(2,1)S(1)} %bitcast.11, f32[16,128]{1,0:T(8,128)S(1)} %reshape.26.refs_2_), custom_call_target="tpu_custom_call" | custom-call | tf_op jit(solution)/shard_map/update/pallas_call | solution.py:274
  70.0 30.6 %all_to_all.15.got_ref = bf16[8,272,256]{2,1,0:T(8,128)(2,1)S(1)} all-to-all(bf16[8,272,256]{2,1,0:T(8,128)(2,1)S(1)} %update.1), channel_id=1, replica_groups=mesh['rep'=8,'yx'=32,'core'=2] {'rep'}, dimensions={0} | all-to-all | bytes 2228224 | tf_op jit(solution)/shard_map/all_to_all | solution.py:282
  100.5 0.6 average.1
  101.2 20.3 %all_to_all.16 = bf16[8,256,256]{2,1,0:T(8,128)(2,1)S(1)} all-to-all(bf16[8,256,256]{2,1,0:T(8,128)(2,1)S(1)} %get-tuple-element.10), channel_id=1, replica_groups=mesh['rep'=8,'yx'=32,'core'=2] {'rep'}, dimensions={0} | all-to-all | bytes 2097152 | tf_op jit(solution)/shard_map/all_to_all | solution.py:294
  121.5 1.0 copy.9
  (1 shorter events, 0.0 us)
Async XLA Ops:
  5.8 28.9 %collective-permute-start = (bf16[32,104,128]{2,1,0:T(8,128)(2,1)}, bf16[32,104,128]{2,1,0:T(8,128)(2,1)S(1)}, u32[]{:S(2)}, u32[]{:S(2)}) collective-permute-start(bf16[32,104,128]{2,1,0:T(8,128)(2,1)} %get-tuple-element.8), channel_id=1, source_target_pairs={{0,1},{1,0},{2,3},{3,2},{4,5},{5,4},{6,7},{7,6},{8,9},{9,8},{10,11... | collective-permute-start | bytes 2555912 | tf_op jit(solution)/shard_map/ppermute | solution.py:252
  14.6 7.9 %collective-permute-start.1 = (bf16[8,128]{1,0:T(8,128)(2,1)}, bf16[8,128]{1,0:T(8,128)(2,1)S(1)}, u32[]{:S(2)}, u32[]{:S(2)}) collective-permute-start(bf16[8,128]{1,0:T(8,128)(2,1)} %get-tuple-element.9), channel_id=1, source_target_pairs={{1,3},{3,5},{5,7},{7,9},{9,11},{11,13},{13,15},{15,17},{17,19},{19... | collective-permute-start | bytes 6152 | tf_op jit(solution)/shard_map/ppermute | solution.py:255
  22.5 7.6 %collective-permute-start.2 = (bf16[8,128]{1,0:T(8,128)(2,1)S(1)}, bf16[8,128]{1,0:T(8,128)(2,1)S(1)}, u32[]{:S(2)}, u32[]{:S(2)}) collective-permute-start(bf16[8,128]{1,0:T(8,128)(2,1)S(1)} %collective-permute-done.1), channel_id=1, source_target_pairs={{1,3},{3,5},{5,7},{7,9},{9,11},{11,13},{13,15},{15,17},{17,19},{19... | collective-permute-start | bytes 6152 | tf_op jit(solution)/shard_map/ppermute | solution.py:255
  30.1 4.6 %collective-permute-start.3 = (bf16[8,128]{1,0:T(8,128)(2,1)S(1)}, bf16[8,128]{1,0:T(8,128)(2,1)S(1)}, u32[]{:S(2)}, u32[]{:S(2)}) collective-permute-start(bf16[8,128]{1,0:T(8,128)(2,1)S(1)} %collective-permute-done.2), channel_id=1, source_target_pairs={{1,3},{3,1},{5,7},{7,5},{9,11},{11,9},{13,15},{15,13},{17,19},{19,... | collective-permute-start | bytes 6152 | tf_op jit(solution)/shard_map/ppermute | solution.py:255
  32.0 1.2 copy-start.1
  36.1 4.2 %copy-start.2 = (f32[2,1024]{1,0:T(2,128)S(1)}, f32[2,1024]{1,0:T(2,128)}, u32[]{:S(2)}) copy-start(f32[2,1024]{1,0:T(2,128)} %param.11) | copy-start | bytes 24580
  36.1 29.8 %copy-start = (bf16[2,1024,256]{2,1,0:T(8,128)(2,1)S(1)}, bf16[2,1024,256]{2,1,0:T(8,128)(2,1)}, u32[]{:S(2)}) copy-start(bf16[2,1024,256]{2,1,0:T(8,128)(2,1)} %param.10) | copy-start | bytes 3145732
  36.1 29.7 %all-to-all-start = ((bf16[32,200,128]{2,1,0:T(8,128)(2,1)}), bf16[32,200,128]{2,1,0:T(8,128)(2,1)S(1)}, u32[]{:S(2)}, u32[]{:S(2)}) async-start(bf16[32,200,128]{2,1,0:T(8,128)(2,1)} %merge.1), calls=%async_computation | async-start | bytes 3276800 | tf_op jit(solution)/shard_map/all_to_all | solution.py:273

commit v10 on v9

--- a/solution.py
+++ b/solution.py
@@ -8,7 +8,7 @@
 BF = jnp.bfloat16
 F32 = jnp.float32
 LANES = 128
-STEPS = ("next", "next", "near")
+STEPS = ("next", "next", "near", "near")
 IDS = 8
 
 

time: 123 us -> 127 us (1.033)
  starting transfers between devices: 18.6 us -> 20.6 us
    ppermute x3 -> x4, waiting for transfers between devices: 13.1 us -> 16 us  [shards_fn(): lax.ppermute(turn, ('yx', 'core'), [(2 * i + 1, 2 * to[i] + 1) for i in r...]
    ppermute x3 -> x4, starting transfers between devices: 5.74 us -> 7.65 us  [shards_fn(): lax.ppermute(turn, ('yx', 'core'), [(2 * i + 1, 2 * to[i] + 1) for i in r...]
    all_to_all x1, waiting for transfers between devices: 25.6 us -> 23.7 us  [shards_fn(): lax.all_to_all(send, 'yx', split_axis=0, concat_axis=0, tiled=True)]
    all_to_all x1, blocking collectives: 20.3 us -> 21.7 us  [shards_fn(): lax.all_to_all(copies, 'rep', split_axis=0, concat_axis=0, tiled=True)]
  transfers between devices with their start and end apart: 5 -> 6, of which waited for: 4 -> 5; matrix products, arithmetic and copies ran while one was open for 0% -> 0% of each run, Pallas kernels for 0% -> 0%
where the time goes in v10:
time: 127 us
  blocking collectives  52 us (41%)
  waiting for transfers between devices  39.7 us (31%)
  starting transfers between devices  20.6 us (16%)
  Pallas kernels  11.3 us (9%)
  local copies, waits for them, and re-layouts  2.15 us (2%)
    all_to_all x1, blocking collectives, shards_fn(): lax.all_to_all(updated, 'rep', split_axis=0, concat_axis=0, tiled=True)  30.3 us
    all_to_all x1, waiting for transfers between devices, shards_fn(): lax.all_to_all(send, 'yx', split_axis=0, concat_axis=0, tiled=True)  23.7 us
    all_to_all x1, blocking collectives, shards_fn(): lax.all_to_all(copies, 'rep', split_axis=0, concat_axis=0, tiled=True)  21.7 us
    ppermute x4, waiting for transfers between devices, shards_fn(): lax.ppermute(turn, ('yx', 'core'), [(2 * i + 1, 2 * to[i] + 1) for i in r...  16 us
    ppermute x1, starting transfers between devices, shards_fn(): got = lax.ppermute(other, 'core', [(0, 1), (1, 0)])  8.79 us
    ppermute x4, starting transfers between devices, shards_fn(): lax.ppermute(turn, ('yx', 'core'), [(2 * i + 1, 2 * to[i] + 1) for i in r...  7.65 us
    pallas_call x1, Pallas kernels, shards_fn(): pl.pallas_call(lambda *refs: pack_kernel(owners, cap, rows_dev, *refs), o...  5.19 us
    pallas_call x1, Pallas kernels, shards_fn(): pl.pallas_call(lambda *refs: update_kernel(cap, replicas, *refs), out_sha...  4.13 us
  transfers between devices with their start and end apart: 6, of which 5 were waited for; matrix products, arithmetic and copies ran while one was open for 0% of the time, Pallas kernels for 0%

profile of v10, /device:TPU:1, one launch (start us, length us, event | category | flops | bytes accessed | tf_op | source)
XLA Modules:
  0.0 126.5 jit_solution(16904152023583273263)
XLA Ops:
  0.6 5.2 %pack.1 = (bf16[32,104,128]{2,1,0:T(8,128)(2,1)}, bf16[32,104,128]{2,1,0:T(8,128)(2,1)}, bf16[8,128]{1,0:T(8,128)(2,1)}) custom-call(s32[8]{0:T(128)} %refs_0_.1, s32[16,128]{1,0:T(8,128)} %bitcast.14, s32[16,128]{1,0:T(8,128)} %bitcast.15, bf16[1024,256]{1,0:T(8,128)(2,1)} %bitcast.13), custom_call_target="tpu_custom_call" | custom-call | tf_op jit(solution)/shard_map/pack/pallas_call | solution.py:233
  5.8 8.8 %collective-permute-start = (bf16[32,104,128]{2,1,0:T(8,128)(2,1)}, bf16[32,104,128]{2,1,0:T(8,128)(2,1)S(1)}, u32[]{:S(2)}, u32[]{:S(2)}) collective-permute-start(bf16[32,104,128]{2,1,0:T(8,128)(2,1)} %get-tuple-element.8), channel_id=1, source_target_pairs={{0,1},{1,0},{2,3},{3,2},{4,5},{5,4},{6,7},{7,6},{8,9},{9,8},{10,11... | collective-permute-start | bytes 2555912 | tf_op jit(solution)/shard_map/ppermute | solution.py:252
  14.6 1.9 %collective-permute-start.1 = (bf16[8,128]{1,0:T(8,128)(2,1)}, bf16[8,128]{1,0:T(8,128)(2,1)S(1)}, u32[]{:S(2)}, u32[]{:S(2)}) collective-permute-start(bf16[8,128]{1,0:T(8,128)(2,1)} %get-tuple-element.9), channel_id=1, source_target_pairs={{1,3},{3,5},{5,7},{7,9},{9,11},{11,13},{13,15},{15,17},{17,19},{19... | collective-permute-start | bytes 6152 | tf_op jit(solution)/shard_map/ppermute | solution.py:255
  16.5 5.9 %collective-permute-done.1 = bf16[8,128]{1,0:T(8,128)(2,1)S(1)} collective-permute-done((bf16[8,128]{1,0:T(8,128)(2,1)}, bf16[8,128]{1,0:T(8,128)(2,1)S(1)}, u32[]{:S(2)}, u32[]{:S(2)}) %collective-permute-start.1) | collective-permute-done | bytes 2080 | tf_op jit(solution)/shard_map/ppermute | solution.py:255
  22.5 1.9 %collective-permute-start.2 = (bf16[8,128]{1,0:T(8,128)(2,1)S(1)}, bf16[8,128]{1,0:T(8,128)(2,1)S(1)}, u32[]{:S(2)}, u32[]{:S(2)}) collective-permute-start(bf16[8,128]{1,0:T(8,128)(2,1)S(1)} %collective-permute-done.1), channel_id=1, source_target_pairs={{1,3},{3,5},{5,7},{7,9},{9,11},{11,13},{13,15},{15,17},{17,19},{19... | collective-permute-start | bytes 6152 | tf_op jit(solution)/shard_map/ppermute | solution.py:255
  24.4 5.7 %collective-permute-done.2 = bf16[8,128]{1,0:T(8,128)(2,1)S(1)} collective-permute-done((bf16[8,128]{1,0:T(8,128)(2,1)S(1)}, bf16[8,128]{1,0:T(8,128)(2,1)S(1)}, u32[]{:S(2)}, u32[]{:S(2)}) %collective-permute-start.2) | collective-permute-done | bytes 2080 | tf_op jit(solution)/shard_map/ppermute | solution.py:255
  30.1 1.9 %collective-permute-start.3 = (bf16[8,128]{1,0:T(8,128)(2,1)S(1)}, bf16[8,128]{1,0:T(8,128)(2,1)S(1)}, u32[]{:S(2)}, u32[]{:S(2)}) collective-permute-start(bf16[8,128]{1,0:T(8,128)(2,1)S(1)} %collective-permute-done.2), channel_id=1, source_target_pairs={{1,3},{3,1},{5,7},{7,5},{9,11},{11,9},{13,15},{15,13},{17,19},{19,... | collective-permute-start | bytes 6152 | tf_op jit(solution)/shard_map/ppermute | solution.py:255
  32.0 2.7 %collective-permute-done.3 = bf16[8,128]{1,0:T(8,128)(2,1)S(1)} collective-permute-done((bf16[8,128]{1,0:T(8,128)(2,1)S(1)}, bf16[8,128]{1,0:T(8,128)(2,1)S(1)}, u32[]{:S(2)}, u32[]{:S(2)}) %collective-permute-start.3) | collective-permute-done | bytes 2080 | tf_op jit(solution)/shard_map/ppermute | solution.py:255
  34.7 1.9 %collective-permute-start.4 = (bf16[8,128]{1,0:T(8,128)(2,1)S(1)}, bf16[8,128]{1,0:T(8,128)(2,1)S(1)}, u32[]{:S(2)}, u32[]{:S(2)}) collective-permute-start(bf16[8,128]{1,0:T(8,128)(2,1)S(1)} %collective-permute-done.3), channel_id=1, source_target_pairs={{1,3},{3,1},{5,7},{7,5},{9,11},{11,9},{13,15},{15,13},{17,19},{19,... | collective-permute-start | bytes 6152 | tf_op jit(solution)/shard_map/ppermute | solution.py:255
  36.6 0.0 copy-start.1
  36.7 1.1 copy-done.1
  37.8 0.1 place.1.own_ref
  37.9 1.7 %collective-permute-done.4.turn_ref = bf16[8,128]{1,0:T(8,128)(2,1)S(1)} collective-permute-done((bf16[8,128]{1,0:T(8,128)(2,1)S(1)}, bf16[8,128]{1,0:T(8,128)(2,1)S(1)}, u32[]{:S(2)}, u32[]{:S(2)}) %collective-permute-start.4) | collective-permute-done | bytes 2080 | tf_op jit(solution)/shard_map/ppermute | solution.py:255
  39.5 0.0 collective-permute-done.got_ref
  39.6 1.3 %merge.1 = bf16[32,200,128]{2,1,0:T(8,128)(2,1)} custom-call(bf16[32,104,128]{2,1,0:T(8,128)(2,1)S(1)} %place.1.own_ref, bf16[32,104,128]{2,1,0:T(8,128)(2,1)S(1)} %collective-permute-done.got_ref, bf16[8,128]{1,0:T(8,128)(2,1)S(1)} %collective-permute-done.4.turn_ref), custom_call_target="tpu_custom_call" | custom-call | tf_op jit(solution)/shard_map/merge/pallas_call | solution.py:264
  40.9 0.0 copy-start.2
  40.9 0.0 copy-start
  40.9 4.1 %all-to-all-start = ((bf16[32,200,128]{2,1,0:T(8,128)(2,1)}), bf16[32,200,128]{2,1,0:T(8,128)(2,1)S(1)}, u32[]{:S(2)}, u32[]{:S(2)}) async-start(bf16[32,200,128]{2,1,0:T(8,128)(2,1)} %merge.1), calls=%async_computation | async-start | bytes 3276800 | tf_op jit(solution)/shard_map/all_to_all | solution.py:273
  45.1 23.7 %all-to-all-done.refs_0_ = bf16[32,200,128]{2,1,0:T(8,128)(2,1)S(1)} async-done(((bf16[32,200,128]{2,1,0:T(8,128)(2,1)}), bf16[32,200,128]{2,1,0:T(8,128)(2,1)S(1)}, u32[]{:S(2)}, u32[]{:S(2)}) %all-to-all-start) | async-done | bytes 1638432 | tf_op jit(solution)/shard_map/all_to_all | solution.py:273
  68.8 4.1 %update.1 = bf16[8,272,256]{2,1,0:T(8,128)(2,1)S(1)} custom-call(bf16[32,200,128]{2,1,0:T(8,128)(2,1)S(1)} %all-to-all-done.refs_0_, bf16[2048,256]{1,0:T(8,128)(2,1)S(1)} %bitcast.11, f32[16,128]{1,0:T(8,128)S(1)} %reshape.26.refs_2_), custom_call_target="tpu_custom_call" | custom-call | tf_op jit(solution)/shard_map/update/pallas_call | solution.py:274
  72.9 30.3 %all_to_all.15.got_ref = bf16[8,272,256]{2,1,0:T(8,128)(2,1)S(1)} all-to-all(bf16[8,272,256]{2,1,0:T(8,128)(2,1)S(1)} %update.1), channel_id=1, replica_groups=mesh['rep'=8,'yx'=32,'core'=2] {'rep'}, dimensions={0} | all-to-all | bytes 2228224 | tf_op jit(solution)/shard_map/all_to_all | solution.py:282
  103.2 0.6 average.1
  103.8 21.7 %all_to_all.16 = bf16[8,256,256]{2,1,0:T(8,128)(2,1)S(1)} all-to-all(bf16[8,256,256]{2,1,0:T(8,128)(2,1)S(1)} %get-tuple-element.10), channel_id=1, replica_groups=mesh['rep'=8,'yx'=32,'core'=2] {'rep'}, dimensions={0} | all-to-all | bytes 2097152 | tf_op jit(solution)/shard_map/all_to_all | solution.py:294
  125.5 1.0 copy.9
  (3 shorter events, 0.0 us)
Async XLA Ops:
  5.8 33.7 %collective-permute-start = (bf16[32,104,128]{2,1,0:T(8,128)(2,1)}, bf16[32,104,128]{2,1,0:T(8,128)(2,1)S(1)}, u32[]{:S(2)}, u32[]{:S(2)}) collective-permute-start(bf16[32,104,128]{2,1,0:T(8,128)(2,1)} %get-tuple-element.8), channel_id=1, source_target_pairs={{0,1},{1,0},{2,3},{3,2},{4,5},{5,4},{6,7},{7,6},{8,9},{9,8},{10,11... | collective-permute-start | bytes 2555912 | tf_op jit(solution)/shard_map/ppermute | solution.py:252
  14.6 7.9 %collective-permute-start.1 = (bf16[8,128]{1,0:T(8,128)(2,1)}, bf16[8,128]{1,0:T(8,128)(2,1)S(1)}, u32[]{:S(2)}, u32[]{:S(2)}) collective-permute-start(bf16[8,128]{1,0:T(8,128)(2,1)} %get-tuple-element.9), channel_id=1, source_target_pairs={{1,3},{3,5},{5,7},{7,9},{9,11},{11,13},{13,15},{15,17},{17,19},{19... | collective-permute-start | bytes 6152 | tf_op jit(solution)/shard_map/ppermute | solution.py:255
  22.5 7.6 %collective-permute-start.2 = (bf16[8,128]{1,0:T(8,128)(2,1)S(1)}, bf16[8,128]{1,0:T(8,128)(2,1)S(1)}, u32[]{:S(2)}, u32[]{:S(2)}) collective-permute-start(bf16[8,128]{1,0:T(8,128)(2,1)S(1)} %collective-permute-done.1), channel_id=1, source_target_pairs={{1,3},{3,5},{5,7},{7,9},{9,11},{11,13},{13,15},{15,17},{17,19},{19... | collective-permute-start | bytes 6152 | tf_op jit(solution)/shard_map/ppermute | solution.py:255
  30.1 4.6 %collective-permute-start.3 = (bf16[8,128]{1,0:T(8,128)(2,1)S(1)}, bf16[8,128]{1,0:T(8,128)(2,1)S(1)}, u32[]{:S(2)}, u32[]{:S(2)}) collective-permute-start(bf16[8,128]{1,0:T(8,128)(2,1)S(1)} %collective-permute-done.2), channel_id=1, source_target_pairs={{1,3},{3,1},{5,7},{7,5},{9,11},{11,9},{13,15},{15,13},{17,19},{19,... | collective-permute-start | bytes 6152 | tf_op jit(solution)/shard_map/ppermute | solution.py:255
  34.7 4.8 %collective-permute-start.4 = (bf16[8,128]{1,0:T(8,128)(2,1)S(1)}, bf16[8,128]{1,0:T(8,128)(2,1)S(1)}, u32[]{:S(2)}, u32[]{:S(2)}) collective-permute-start(bf16[8,128]{1,0:T(8,128)(2,1)S(1)} %collective-permute-done.3), channel_id=1, source_target_pairs={{1,3},{3,1},{5,7},{7,5},{9,11},{11,9},{13,15},{15,13},{17,19},{19,... | collective-permute-start | bytes 6152 | tf_op jit(solution)/shard_map/ppermute | solution.py:255
  36.6 1.2 copy-start.1
  40.9 4.2 %copy-start.2 = (f32[2,1024]{1,0:T(2,128)S(1)}, f32[2,1024]{1,0:T(2,128)}, u32[]{:S(2)}) copy-start(f32[2,1024]{1,0:T(2,128)} %param.11) | copy-start | bytes 24580
  40.9 27.9 %copy-start = (bf16[2,1024,256]{2,1,0:T(8,128)(2,1)S(1)}, bf16[2,1024,256]{2,1,0:T(8,128)(2,1)}, u32[]{:S(2)}) copy-start(bf16[2,1024,256]{2,1,0:T(8,128)(2,1)} %param.10) | copy-start | bytes 3145732
  40.9 27.8 %all-to-all-start = ((bf16[32,200,128]{2,1,0:T(8,128)(2,1)}), bf16[32,200,128]{2,1,0:T(8,128)(2,1)S(1)}, u32[]{:S(2)}, u32[]{:S(2)}) async-start(bf16[32,200,128]{2,1,0:T(8,128)(2,1)} %merge.1), calls=%async_computation | async-start | bytes 3276800 | tf_op jit(solution)/shard_map/all_to_all | solution.py:273

commit v11 on v9

--- a/solution.py
+++ b/solution.py
@@ -252,7 +252,7 @@
     got = lax.ppermute(other, "core", [(0, 1), (1, 0)])
     for step in STEPS:
         to = [(i + 1) % chips if step == "next" else i ^ 1 for i in range(chips)]
-        turn = lax.ppermute(turn, ("yx", "core"), [(2 * i + 1, 2 * to[i] + 1) for i in range(chips)])
+        turn = lax.ppermute(turn, ("yx", "core"), [(2 * i, 2 * to[i]) for i in range(chips)])
     placed = pl.pallas_call(
         place_kernel,
         out_shape=jax.ShapeDtypeStruct(own.shape, BF),

time: 123 us -> 133 us (1.081)
  the two profiles are of different devices: /device:TPU:1 before, /device:TPU:4 now
where the time goes in v11:
time: 133 us; the launch traced here: 132 us
  blocking collectives  59.3 us (45%)
  waiting for transfers between devices  34.2 us (26%)
  starting transfers between devices  24.5 us (18%)
  Pallas kernels  11.3 us (8%)
  local copies, waits for them, and re-layouts  2.15 us (2%)
    all_to_all x1, blocking collectives, shards_fn(): lax.all_to_all(updated, 'rep', split_axis=0, concat_axis=0, tiled=True)  38 us
    all_to_all x1, waiting for transfers between devices, shards_fn(): lax.all_to_all(send, 'yx', split_axis=0, concat_axis=0, tiled=True)  24.6 us
    all_to_all x1, blocking collectives, shards_fn(): lax.all_to_all(copies, 'rep', split_axis=0, concat_axis=0, tiled=True)  21.3 us
    all_to_all x1, starting transfers between devices, shards_fn(): lax.all_to_all(send, 'yx', split_axis=0, concat_axis=0, tiled=True)  14.3 us
    ppermute x3, waiting for transfers between devices, shards_fn(): lax.ppermute(turn, ('yx', 'core'), [(2 * i, 2 * to[i]) for i in range(chi...  9.6 us
    ppermute x3, starting transfers between devices, shards_fn(): lax.ppermute(turn, ('yx', 'core'), [(2 * i, 2 * to[i]) for i in range(chi...  8.2 us
    pallas_call x1, Pallas kernels, shards_fn(): pl.pallas_call(lambda *refs: pack_kernel(owners, cap, rows_dev, *refs), o...  5.19 us
    pallas_call x1, Pallas kernels, shards_fn(): pl.pallas_call(lambda *refs: update_kernel(cap, replicas, *refs), out_sha...  4.13 us
  transfers between devices with their start and end apart: 5, of which 4 were waited for; matrix products, arithmetic and copies ran while one was open for 0% of the time, Pallas kernels for 0%

profile of v11, /device:TPU:4, one launch (start us, length us, event | category | flops | bytes accessed | tf_op | source)
XLA Modules:
  0.0 132.2 jit_solution(18321356795282533845)
XLA Ops:
  0.6 5.2 %pack.1 = (bf16[32,104,128]{2,1,0:T(8,128)(2,1)}, bf16[32,104,128]{2,1,0:T(8,128)(2,1)}, bf16[8,128]{1,0:T(8,128)(2,1)}) custom-call(s32[8]{0:T(128)} %refs_0_.1, s32[16,128]{1,0:T(8,128)} %bitcast.14, s32[16,128]{1,0:T(8,128)} %bitcast.15, bf16[1024,256]{1,0:T(8,128)(2,1)} %bitcast.13), custom_call_target="tpu_custom_call" | custom-call | tf_op jit(solution)/shard_map/pack/pallas_call | solution.py:233
  5.8 1.9 %collective-permute-start = (bf16[32,104,128]{2,1,0:T(8,128)(2,1)}, bf16[32,104,128]{2,1,0:T(8,128)(2,1)S(1)}, u32[]{:S(2)}, u32[]{:S(2)}) collective-permute-start(bf16[32,104,128]{2,1,0:T(8,128)(2,1)} %get-tuple-element.8), channel_id=1, source_target_pairs={{0,1},{1,0},{2,3},{3,2},{4,5},{5,4},{6,7},{7,6},{8,9},{9,8},{10,11... | collective-permute-start | bytes 2555912 | tf_op jit(solution)/shard_map/ppermute | solution.py:252
  7.8 3.1 %collective-permute-start.1 = (bf16[8,128]{1,0:T(8,128)(2,1)}, bf16[8,128]{1,0:T(8,128)(2,1)S(1)}, u32[]{:S(2)}, u32[]{:S(2)}) collective-permute-start(bf16[8,128]{1,0:T(8,128)(2,1)} %get-tuple-element.9), channel_id=1, source_target_pairs={{0,2},{2,4},{4,6},{6,8},{8,10},{10,12},{12,14},{14,16},{16,18},{18... | collective-permute-start | bytes 6152 | tf_op jit(solution)/shard_map/ppermute | solution.py:255
  10.9 2.6 %collective-permute-done.1 = bf16[8,128]{1,0:T(8,128)(2,1)S(1)} collective-permute-done((bf16[8,128]{1,0:T(8,128)(2,1)}, bf16[8,128]{1,0:T(8,128)(2,1)S(1)}, u32[]{:S(2)}, u32[]{:S(2)}) %collective-permute-start.1) | collective-permute-done | bytes 2080 | tf_op jit(solution)/shard_map/ppermute | solution.py:255
  13.4 3.1 %collective-permute-start.2 = (bf16[8,128]{1,0:T(8,128)(2,1)S(1)}, bf16[8,128]{1,0:T(8,128)(2,1)S(1)}, u32[]{:S(2)}, u32[]{:S(2)}) collective-permute-start(bf16[8,128]{1,0:T(8,128)(2,1)S(1)} %collective-permute-done.1), channel_id=1, source_target_pairs={{0,2},{2,4},{4,6},{6,8},{8,10},{10,12},{12,14},{14,16},{16,18},{18... | collective-permute-start | bytes 6152 | tf_op jit(solution)/shard_map/ppermute | solution.py:255
  16.5 4.8 %collective-permute-done.2 = bf16[8,128]{1,0:T(8,128)(2,1)S(1)} collective-permute-done((bf16[8,128]{1,0:T(8,128)(2,1)S(1)}, bf16[8,128]{1,0:T(8,128)(2,1)S(1)}, u32[]{:S(2)}, u32[]{:S(2)}) %collective-permute-start.2) | collective-permute-done | bytes 2080 | tf_op jit(solution)/shard_map/ppermute | solution.py:255
  21.3 2.0 %collective-permute-start.3 = (bf16[8,128]{1,0:T(8,128)(2,1)S(1)}, bf16[8,128]{1,0:T(8,128)(2,1)S(1)}, u32[]{:S(2)}, u32[]{:S(2)}) collective-permute-start(bf16[8,128]{1,0:T(8,128)(2,1)S(1)} %collective-permute-done.2), channel_id=1, source_target_pairs={{0,2},{2,0},{4,6},{6,4},{8,10},{10,8},{12,14},{14,12},{16,18},{18,... | collective-permute-start | bytes 6152 | tf_op jit(solution)/shard_map/ppermute | solution.py:255
  23.3 0.0 copy-start.1
  23.4 1.1 copy-done.1
  24.5 0.1 place.1.own_ref
  24.6 2.2 %collective-permute-done.3.turn_ref = bf16[8,128]{1,0:T(8,128)(2,1)S(1)} collective-permute-done((bf16[8,128]{1,0:T(8,128)(2,1)S(1)}, bf16[8,128]{1,0:T(8,128)(2,1)S(1)}, u32[]{:S(2)}, u32[]{:S(2)}) %collective-permute-start.3) | collective-permute-done | bytes 2080 | tf_op jit(solution)/shard_map/ppermute | solution.py:255
  26.8 0.0 collective-permute-done.got_ref
  26.8 1.3 %merge.1 = bf16[32,200,128]{2,1,0:T(8,128)(2,1)} custom-call(bf16[32,104,128]{2,1,0:T(8,128)(2,1)S(1)} %place.1.own_ref, bf16[32,104,128]{2,1,0:T(8,128)(2,1)S(1)} %collective-permute-done.got_ref, bf16[8,128]{1,0:T(8,128)(2,1)S(1)} %collective-permute-done.3.turn_ref), custom_call_target="tpu_custom_call" | custom-call | tf_op jit(solution)/shard_map/merge/pallas_call | solution.py:264
  28.1 0.0 copy-start.2
  28.1 0.0 copy-start
  28.2 14.3 %all-to-all-start = ((bf16[32,200,128]{2,1,0:T(8,128)(2,1)}), bf16[32,200,128]{2,1,0:T(8,128)(2,1)S(1)}, u32[]{:S(2)}, u32[]{:S(2)}) async-start(bf16[32,200,128]{2,1,0:T(8,128)(2,1)} %merge.1), calls=%async_computation | async-start | bytes 3276800 | tf_op jit(solution)/shard_map/all_to_all | solution.py:273
  42.5 0.0 copy-done.2
  42.5 24.6 %all-to-all-done.refs_0_ = bf16[32,200,128]{2,1,0:T(8,128)(2,1)S(1)} async-done(((bf16[32,200,128]{2,1,0:T(8,128)(2,1)}), bf16[32,200,128]{2,1,0:T(8,128)(2,1)S(1)}, u32[]{:S(2)}, u32[]{:S(2)}) %all-to-all-start) | async-done | bytes 1638432 | tf_op jit(solution)/shard_map/all_to_all | solution.py:273
  67.1 0.0 copy-done
  67.2 4.1 %update.1 = bf16[8,272,256]{2,1,0:T(8,128)(2,1)S(1)} custom-call(bf16[32,200,128]{2,1,0:T(8,128)(2,1)S(1)} %all-to-all-done.refs_0_, bf16[2048,256]{1,0:T(8,128)(2,1)S(1)} %bitcast.11, f32[16,128]{1,0:T(8,128)S(1)} %reshape.26.refs_2_), custom_call_target="tpu_custom_call" | custom-call | tf_op jit(solution)/shard_map/update/pallas_call | solution.py:274
  71.3 38.0 %all_to_all.15.got_ref = bf16[8,272,256]{2,1,0:T(8,128)(2,1)S(1)} all-to-all(bf16[8,272,256]{2,1,0:T(8,128)(2,1)S(1)} %update.1), channel_id=1, replica_groups=mesh['rep'=8,'yx'=32,'core'=2] {'rep'}, dimensions={0} | all-to-all | bytes 2228224 | tf_op jit(solution)/shard_map/all_to_all | solution.py:282
  109.3 0.6 average.1
  109.9 21.3 %all_to_all.16 = bf16[8,256,256]{2,1,0:T(8,128)(2,1)S(1)} all-to-all(bf16[8,256,256]{2,1,0:T(8,128)(2,1)S(1)} %get-tuple-element.10), channel_id=1, replica_groups=mesh['rep'=8,'yx'=32,'core'=2] {'rep'}, dimensions={0} | all-to-all | bytes 2097152 | tf_op jit(solution)/shard_map/all_to_all | solution.py:294
  131.3 1.0 copy.9
  (1 shorter events, 0.0 us)
Async XLA Ops:
  5.8 21.0 %collective-permute-start = (bf16[32,104,128]{2,1,0:T(8,128)(2,1)}, bf16[32,104,128]{2,1,0:T(8,128)(2,1)S(1)}, u32[]{:S(2)}, u32[]{:S(2)}) collective-permute-start(bf16[32,104,128]{2,1,0:T(8,128)(2,1)} %get-tuple-element.8), channel_id=1, source_target_pairs={{0,1},{1,0},{2,3},{3,2},{4,5},{5,4},{6,7},{7,6},{8,9},{9,8},{10,11... | collective-permute-start | bytes 2555912 | tf_op jit(solution)/shard_map/ppermute | solution.py:252
  7.8 5.7 %collective-permute-start.1 = (bf16[8,128]{1,0:T(8,128)(2,1)}, bf16[8,128]{1,0:T(8,128)(2,1)S(1)}, u32[]{:S(2)}, u32[]{:S(2)}) collective-permute-start(bf16[8,128]{1,0:T(8,128)(2,1)} %get-tuple-element.9), channel_id=1, source_target_pairs={{0,2},{2,4},{4,6},{6,8},{8,10},{10,12},{12,14},{14,16},{16,18},{18... | collective-permute-start | bytes 6152 | tf_op jit(solution)/shard_map/ppermute | solution.py:255
  13.4 7.9 %collective-permute-start.2 = (bf16[8,128]{1,0:T(8,128)(2,1)S(1)}, bf16[8,128]{1,0:T(8,128)(2,1)S(1)}, u32[]{:S(2)}, u32[]{:S(2)}) collective-permute-start(bf16[8,128]{1,0:T(8,128)(2,1)S(1)} %collective-permute-done.1), channel_id=1, source_target_pairs={{0,2},{2,4},{4,6},{6,8},{8,10},{10,12},{12,14},{14,16},{16,18},{18... | collective-permute-start | bytes 6152 | tf_op jit(solution)/shard_map/ppermute | solution.py:255
  21.3 5.5 %collective-permute-start.3 = (bf16[8,128]{1,0:T(8,128)(2,1)S(1)}, bf16[8,128]{1,0:T(8,128)(2,1)S(1)}, u32[]{:S(2)}, u32[]{:S(2)}) collective-permute-start(bf16[8,128]{1,0:T(8,128)(2,1)S(1)} %collective-permute-done.2), channel_id=1, source_target_pairs={{0,2},{2,0},{4,6},{6,4},{8,10},{10,8},{12,14},{14,12},{16,18},{18,... | collective-permute-start | bytes 6152 | tf_op jit(solution)/shard_map/ppermute | solution.py:255
  23.3 1.2 copy-start.1
  28.1 14.4 %copy-start.2 = (f32[2,1024]{1,0:T(2,128)S(1)}, f32[2,1024]{1,0:T(2,128)}, u32[]{:S(2)}) copy-start(f32[2,1024]{1,0:T(2,128)} %param.11) | copy-start | bytes 24580
  28.1 39.0 %copy-start = (bf16[2,1024,256]{2,1,0:T(8,128)(2,1)S(1)}, bf16[2,1024,256]{2,1,0:T(8,128)(2,1)}, u32[]{:S(2)}) copy-start(bf16[2,1024,256]{2,1,0:T(8,128)(2,1)} %param.10) | copy-start | bytes 3145732
  28.2 39.0 %all-to-all-start = ((bf16[32,200,128]{2,1,0:T(8,128)(2,1)}), bf16[32,200,128]{2,1,0:T(8,128)(2,1)S(1)}, u32[]{:S(2)}, u32[]{:S(2)}) async-start(bf16[32,200,128]{2,1,0:T(8,128)(2,1)} %merge.1), calls=%async_computation | async-start | bytes 3276800 | tf_op jit(solution)/shard_map/all_to_all | solution.py:273

commit v12 on v11

--- a/solution.py
+++ b/solution.py
@@ -8,7 +8,7 @@
 BF = jnp.bfloat16
 F32 = jnp.float32
 LANES = 128
-STEPS = ("next", "next", "near")
+STEPS = ("next", "next")
 IDS = 8
 
 

time: 133 us -> 127 us (0.955)
  the two profiles are of different devices: /device:TPU:4 before, /device:TPU:16 now
where the time goes in v12:
time: 127 us
  blocking collectives  57.6 us (45%)
  waiting for transfers between devices  35.6 us (28%)
  starting transfers between devices  19.3 us (15%)
  Pallas kernels  11.3 us (9%)
  local copies, waits for them, and re-layouts  2.15 us (2%)
    all_to_all x1, blocking collectives, shards_fn(): lax.all_to_all(updated, 'rep', split_axis=0, concat_axis=0, tiled=True)  34 us
    all_to_all x1, waiting for transfers between devices, shards_fn(): lax.all_to_all(send, 'yx', split_axis=0, concat_axis=0, tiled=True)  26.8 us
    all_to_all x1, blocking collectives, shards_fn(): lax.all_to_all(copies, 'rep', split_axis=0, concat_axis=0, tiled=True)  23.6 us
    all_to_all x1, starting transfers between devices, shards_fn(): lax.all_to_all(send, 'yx', split_axis=0, concat_axis=0, tiled=True)  12.1 us
    ppermute x2, waiting for transfers between devices, shards_fn(): lax.ppermute(turn, ('yx', 'core'), [(2 * i, 2 * to[i]) for i in range(chi...  8.83 us
    ppermute x2, starting transfers between devices, shards_fn(): lax.ppermute(turn, ('yx', 'core'), [(2 * i, 2 * to[i]) for i in range(chi...  5.31 us
    pallas_call x1, Pallas kernels, shards_fn(): pl.pallas_call(lambda *refs: pack_kernel(owners, cap, rows_dev, *refs), o...  5.17 us
    pallas_call x1, Pallas kernels, shards_fn(): pl.pallas_call(lambda *refs: update_kernel(cap, replicas, *refs), out_sha...  4.13 us
  transfers between devices with their start and end apart: 4, of which 3 were waited for; matrix products, arithmetic and copies ran while one was open for 0% of the time, Pallas kernels for 0%

profile of v12, /device:TPU:16, one launch (start us, length us, event | category | flops | bytes accessed | tf_op | source)
XLA Modules:
  0.0 126.7 jit_solution(13619055209169085315)
XLA Ops:
  0.6 5.2 %pack.1 = (bf16[32,104,128]{2,1,0:T(8,128)(2,1)}, bf16[32,104,128]{2,1,0:T(8,128)(2,1)}, bf16[8,128]{1,0:T(8,128)(2,1)}) custom-call(s32[8]{0:T(128)} %refs_0_.1, s32[16,128]{1,0:T(8,128)} %bitcast.14, s32[16,128]{1,0:T(8,128)} %bitcast.15, bf16[1024,256]{1,0:T(8,128)(2,1)} %bitcast.13), custom_call_target="tpu_custom_call" | custom-call | tf_op jit(solution)/shard_map/pack/pallas_call | solution.py:233
  5.8 1.9 %collective-permute-start = (bf16[32,104,128]{2,1,0:T(8,128)(2,1)}, bf16[32,104,128]{2,1,0:T(8,128)(2,1)S(1)}, u32[]{:S(2)}, u32[]{:S(2)}) collective-permute-start(bf16[32,104,128]{2,1,0:T(8,128)(2,1)} %get-tuple-element.8), channel_id=1, source_target_pairs={{0,1},{1,0},{2,3},{3,2},{4,5},{5,4},{6,7},{7,6},{8,9},{9,8},{10,11... | collective-permute-start | bytes 2555912 | tf_op jit(solution)/shard_map/ppermute | solution.py:252
  7.7 3.4 %collective-permute-start.1 = (bf16[8,128]{1,0:T(8,128)(2,1)}, bf16[8,128]{1,0:T(8,128)(2,1)S(1)}, u32[]{:S(2)}, u32[]{:S(2)}) collective-permute-start(bf16[8,128]{1,0:T(8,128)(2,1)} %get-tuple-element.9), channel_id=1, source_target_pairs={{0,2},{2,4},{4,6},{6,8},{8,10},{10,12},{12,14},{14,16},{16,18},{18... | collective-permute-start | bytes 6152 | tf_op jit(solution)/shard_map/ppermute | solution.py:255
  11.1 4.4 %collective-permute-done.1 = bf16[8,128]{1,0:T(8,128)(2,1)S(1)} collective-permute-done((bf16[8,128]{1,0:T(8,128)(2,1)}, bf16[8,128]{1,0:T(8,128)(2,1)S(1)}, u32[]{:S(2)}, u32[]{:S(2)}) %collective-permute-start.1) | collective-permute-done | bytes 2080 | tf_op jit(solution)/shard_map/ppermute | solution.py:255
  15.5 1.9 %collective-permute-start.2 = (bf16[8,128]{1,0:T(8,128)(2,1)S(1)}, bf16[8,128]{1,0:T(8,128)(2,1)S(1)}, u32[]{:S(2)}, u32[]{:S(2)}) collective-permute-start(bf16[8,128]{1,0:T(8,128)(2,1)S(1)} %collective-permute-done.1), channel_id=1, source_target_pairs={{0,2},{2,4},{4,6},{6,8},{8,10},{10,12},{12,14},{14,16},{16,18},{18... | collective-permute-start | bytes 6152 | tf_op jit(solution)/shard_map/ppermute | solution.py:255
  17.5 0.0 copy-start.1
  17.5 1.1 copy-done.1
  18.6 0.1 place.1.own_ref
  18.7 4.4 %collective-permute-done.2.turn_ref = bf16[8,128]{1,0:T(8,128)(2,1)S(1)} collective-permute-done((bf16[8,128]{1,0:T(8,128)(2,1)S(1)}, bf16[8,128]{1,0:T(8,128)(2,1)S(1)}, u32[]{:S(2)}, u32[]{:S(2)}) %collective-permute-start.2) | collective-permute-done | bytes 2080 | tf_op jit(solution)/shard_map/ppermute | solution.py:255
  23.1 0.0 collective-permute-done.got_ref
  23.1 1.3 %merge.1 = bf16[32,200,128]{2,1,0:T(8,128)(2,1)} custom-call(bf16[32,104,128]{2,1,0:T(8,128)(2,1)S(1)} %place.1.own_ref, bf16[32,104,128]{2,1,0:T(8,128)(2,1)S(1)} %collective-permute-done.got_ref, bf16[8,128]{1,0:T(8,128)(2,1)S(1)} %collective-permute-done.2.turn_ref), custom_call_target="tpu_custom_call" | custom-call | tf_op jit(solution)/shard_map/merge/pallas_call | solution.py:264
  24.4 0.0 copy-start.2
  24.5 0.0 copy-start
  24.5 12.1 %all-to-all-start = ((bf16[32,200,128]{2,1,0:T(8,128)(2,1)}), bf16[32,200,128]{2,1,0:T(8,128)(2,1)S(1)}, u32[]{:S(2)}, u32[]{:S(2)}) async-start(bf16[32,200,128]{2,1,0:T(8,128)(2,1)} %merge.1), calls=%async_computation | async-start | bytes 3276800 | tf_op jit(solution)/shard_map/all_to_all | solution.py:273
  36.5 0.0 copy-done.2
  36.6 26.8 %all-to-all-done.refs_0_ = bf16[32,200,128]{2,1,0:T(8,128)(2,1)S(1)} async-done(((bf16[32,200,128]{2,1,0:T(8,128)(2,1)}), bf16[32,200,128]{2,1,0:T(8,128)(2,1)S(1)}, u32[]{:S(2)}, u32[]{:S(2)}) %all-to-all-start) | async-done | bytes 1638432 | tf_op jit(solution)/shard_map/all_to_all | solution.py:273
  63.3 0.0 copy-done
  63.3 4.1 %update.1 = bf16[8,272,256]{2,1,0:T(8,128)(2,1)S(1)} custom-call(bf16[32,200,128]{2,1,0:T(8,128)(2,1)S(1)} %all-to-all-done.refs_0_, bf16[2048,256]{1,0:T(8,128)(2,1)S(1)} %bitcast.11, f32[16,128]{1,0:T(8,128)S(1)} %reshape.26.refs_2_), custom_call_target="tpu_custom_call" | custom-call | tf_op jit(solution)/shard_map/update/pallas_call | solution.py:274
  67.5 34.0 %all_to_all.15.got_ref = bf16[8,272,256]{2,1,0:T(8,128)(2,1)S(1)} all-to-all(bf16[8,272,256]{2,1,0:T(8,128)(2,1)S(1)} %update.1), channel_id=1, replica_groups=mesh['rep'=8,'yx'=32,'core'=2] {'rep'}, dimensions={0} | all-to-all | bytes 2228224 | tf_op jit(solution)/shard_map/all_to_all | solution.py:282
  101.4 0.6 average.1
  102.1 23.6 %all_to_all.16 = bf16[8,256,256]{2,1,0:T(8,128)(2,1)S(1)} all-to-all(bf16[8,256,256]{2,1,0:T(8,128)(2,1)S(1)} %get-tuple-element.10), channel_id=1, replica_groups=mesh['rep'=8,'yx'=32,'core'=2] {'rep'}, dimensions={0} | all-to-all | bytes 2097152 | tf_op jit(solution)/shard_map/all_to_all | solution.py:294
  125.7 1.0 copy.9
  (1 shorter events, 0.0 us)
Async XLA Ops:
  5.8 17.3 %collective-permute-start = (bf16[32,104,128]{2,1,0:T(8,128)(2,1)}, bf16[32,104,128]{2,1,0:T(8,128)(2,1)S(1)}, u32[]{:S(2)}, u32[]{:S(2)}) collective-permute-start(bf16[32,104,128]{2,1,0:T(8,128)(2,1)} %get-tuple-element.8), channel_id=1, source_target_pairs={{0,1},{1,0},{2,3},{3,2},{4,5},{5,4},{6,7},{7,6},{8,9},{9,8},{10,11... | collective-permute-start | bytes 2555912 | tf_op jit(solution)/shard_map/ppermute | solution.py:252
  7.7 7.8 %collective-permute-start.1 = (bf16[8,128]{1,0:T(8,128)(2,1)}, bf16[8,128]{1,0:T(8,128)(2,1)S(1)}, u32[]{:S(2)}, u32[]{:S(2)}) collective-permute-start(bf16[8,128]{1,0:T(8,128)(2,1)} %get-tuple-element.9), channel_id=1, source_target_pairs={{0,2},{2,4},{4,6},{6,8},{8,10},{10,12},{12,14},{14,16},{16,18},{18... | collective-permute-start | bytes 6152 | tf_op jit(solution)/shard_map/ppermute | solution.py:255
  15.5 7.6 %collective-permute-start.2 = (bf16[8,128]{1,0:T(8,128)(2,1)S(1)}, bf16[8,128]{1,0:T(8,128)(2,1)S(1)}, u32[]{:S(2)}, u32[]{:S(2)}) collective-permute-start(bf16[8,128]{1,0:T(8,128)(2,1)S(1)} %collective-permute-done.1), channel_id=1, source_target_pairs={{0,2},{2,4},{4,6},{6,8},{8,10},{10,12},{12,14},{14,16},{16,18},{18... | collective-permute-start | bytes 6152 | tf_op jit(solution)/shard_map/ppermute | solution.py:255
  17.5 1.2 copy-start.1
  24.4 12.1 %copy-start.2 = (f32[2,1024]{1,0:T(2,128)S(1)}, f32[2,1024]{1,0:T(2,128)}, u32[]{:S(2)}) copy-start(f32[2,1024]{1,0:T(2,128)} %param.11) | copy-start | bytes 24580
  24.5 38.9 %copy-start = (bf16[2,1024,256]{2,1,0:T(8,128)(2,1)S(1)}, bf16[2,1024,256]{2,1,0:T(8,128)(2,1)}, u32[]{:S(2)}) copy-start(bf16[2,1024,256]{2,1,0:T(8,128)(2,1)} %param.10) | copy-start | bytes 3145732
  24.5 38.8 %all-to-all-start = ((bf16[32,200,128]{2,1,0:T(8,128)(2,1)}), bf16[32,200,128]{2,1,0:T(8,128)(2,1)S(1)}, u32[]{:S(2)}, u32[]{:S(2)}) async-start(bf16[32,200,128]{2,1,0:T(8,128)(2,1)} %merge.1), calls=%async_computation | async-start | bytes 3276800 | tf_op jit(solution)/shard_map/all_to_all | solution.py:273

commit v13 on v12

--- a/solution.py
+++ b/solution.py
@@ -8,7 +8,7 @@
 BF = jnp.bfloat16
 F32 = jnp.float32
 LANES = 128
-STEPS = ("next", "next")
+STEPS = ("next", "near")
 IDS = 8
 
 

time: 127 us -> 125 us (0.984)
  blocking collectives: 57.6 us -> 56 us
  starting transfers between devices: 19.3 us -> 18 us
    all_to_all x1, waiting for transfers between devices: 26.8 us -> 30.1 us  [shards_fn(): lax.all_to_all(send, 'yx', split_axis=0, concat_axis=0, tiled=True)]
    ppermute x2, waiting for transfers between devices: 8.83 us -> 6.72 us  [shards_fn(): lax.ppermute(turn, ('yx', 'core'), [(2 * i, 2 * to[i]) for i in range(chi...]
where the time goes in v13:
time: 125 us
  blocking collectives  56 us (45%)
  waiting for transfers between devices  36.8 us (29%)
  starting transfers between devices  18 us (14%)
  Pallas kernels  11.3 us (9%)
  local copies, waits for them, and re-layouts  2.15 us (2%)
    all_to_all x1, blocking collectives, shards_fn(): lax.all_to_all(updated, 'rep', split_axis=0, concat_axis=0, tiled=True)  32.7 us
    all_to_all x1, waiting for transfers between devices, shards_fn(): lax.all_to_all(send, 'yx', split_axis=0, concat_axis=0, tiled=True)  30.1 us
    all_to_all x1, blocking collectives, shards_fn(): lax.all_to_all(copies, 'rep', split_axis=0, concat_axis=0, tiled=True)  23.3 us
    all_to_all x1, starting transfers between devices, shards_fn(): lax.all_to_all(send, 'yx', split_axis=0, concat_axis=0, tiled=True)  10.8 us
    ppermute x2, waiting for transfers between devices, shards_fn(): lax.ppermute(turn, ('yx', 'core'), [(2 * i, 2 * to[i]) for i in range(chi...  6.72 us
    ppermute x2, starting transfers between devices, shards_fn(): lax.ppermute(turn, ('yx', 'core'), [(2 * i, 2 * to[i]) for i in range(chi...  5.31 us
    pallas_call x1, Pallas kernels, shards_fn(): pl.pallas_call(lambda *refs: pack_kernel(owners, cap, rows_dev, *refs), o...  5.17 us
    pallas_call x1, Pallas kernels, shards_fn(): pl.pallas_call(lambda *refs: update_kernel(cap, replicas, *refs), out_sha...  4.13 us
  transfers between devices with their start and end apart: 4, of which 3 were waited for; matrix products, arithmetic and copies ran while one was open for 0% of the time, Pallas kernels for 0%

profile of v13, /device:TPU:16, one launch (start us, length us, event | category | flops | bytes accessed | tf_op | source)
XLA Modules:
  0.0 125.1 jit_solution(5037359168385042752)
XLA Ops:
  0.6 5.2 %pack.1 = (bf16[32,104,128]{2,1,0:T(8,128)(2,1)}, bf16[32,104,128]{2,1,0:T(8,128)(2,1)}, bf16[8,128]{1,0:T(8,128)(2,1)}) custom-call(s32[8]{0:T(128)} %refs_0_.1, s32[16,128]{1,0:T(8,128)} %bitcast.14, s32[16,128]{1,0:T(8,128)} %bitcast.15, bf16[1024,256]{1,0:T(8,128)(2,1)} %bitcast.13), custom_call_target="tpu_custom_call" | custom-call | tf_op jit(solution)/shard_map/pack/pallas_call | solution.py:233
  5.8 1.9 %collective-permute-start = (bf16[32,104,128]{2,1,0:T(8,128)(2,1)}, bf16[32,104,128]{2,1,0:T(8,128)(2,1)S(1)}, u32[]{:S(2)}, u32[]{:S(2)}) collective-permute-start(bf16[32,104,128]{2,1,0:T(8,128)(2,1)} %get-tuple-element.8), channel_id=1, source_target_pairs={{0,1},{1,0},{2,3},{3,2},{4,5},{5,4},{6,7},{7,6},{8,9},{9,8},{10,11... | collective-permute-start | bytes 2555912 | tf_op jit(solution)/shard_map/ppermute | solution.py:252
  7.7 3.4 %collective-permute-start.1 = (bf16[8,128]{1,0:T(8,128)(2,1)}, bf16[8,128]{1,0:T(8,128)(2,1)S(1)}, u32[]{:S(2)}, u32[]{:S(2)}) collective-permute-start(bf16[8,128]{1,0:T(8,128)(2,1)} %get-tuple-element.9), channel_id=1, source_target_pairs={{0,2},{2,4},{4,6},{6,8},{8,10},{10,12},{12,14},{14,16},{16,18},{18... | collective-permute-start | bytes 6152 | tf_op jit(solution)/shard_map/ppermute | solution.py:255
  11.1 4.4 %collective-permute-done.1 = bf16[8,128]{1,0:T(8,128)(2,1)S(1)} collective-permute-done((bf16[8,128]{1,0:T(8,128)(2,1)}, bf16[8,128]{1,0:T(8,128)(2,1)S(1)}, u32[]{:S(2)}, u32[]{:S(2)}) %collective-permute-start.1) | collective-permute-done | bytes 2080 | tf_op jit(solution)/shard_map/ppermute | solution.py:255
  15.5 1.9 %collective-permute-start.2 = (bf16[8,128]{1,0:T(8,128)(2,1)S(1)}, bf16[8,128]{1,0:T(8,128)(2,1)S(1)}, u32[]{:S(2)}, u32[]{:S(2)}) collective-permute-start(bf16[8,128]{1,0:T(8,128)(2,1)S(1)} %collective-permute-done.1), channel_id=1, source_target_pairs={{0,2},{2,0},{4,6},{6,4},{8,10},{10,8},{12,14},{14,12},{16,18},{18,... | collective-permute-start | bytes 6152 | tf_op jit(solution)/shard_map/ppermute | solution.py:255
  17.5 0.0 copy-start.1
  17.5 1.1 copy-done.1
  18.6 0.1 place.1.own_ref
  18.7 2.3 %collective-permute-done.2.turn_ref = bf16[8,128]{1,0:T(8,128)(2,1)S(1)} collective-permute-done((bf16[8,128]{1,0:T(8,128)(2,1)S(1)}, bf16[8,128]{1,0:T(8,128)(2,1)S(1)}, u32[]{:S(2)}, u32[]{:S(2)}) %collective-permute-start.2) | collective-permute-done | bytes 2080 | tf_op jit(solution)/shard_map/ppermute | solution.py:255
  21.0 0.0 collective-permute-done.got_ref
  21.0 1.3 %merge.1 = bf16[32,200,128]{2,1,0:T(8,128)(2,1)} custom-call(bf16[32,104,128]{2,1,0:T(8,128)(2,1)S(1)} %place.1.own_ref, bf16[32,104,128]{2,1,0:T(8,128)(2,1)S(1)} %collective-permute-done.got_ref, bf16[8,128]{1,0:T(8,128)(2,1)S(1)} %collective-permute-done.2.turn_ref), custom_call_target="tpu_custom_call" | custom-call | tf_op jit(solution)/shard_map/merge/pallas_call | solution.py:264
  22.3 0.0 copy-start.2
  22.3 0.0 copy-start
  22.4 10.8 %all-to-all-start = ((bf16[32,200,128]{2,1,0:T(8,128)(2,1)}), bf16[32,200,128]{2,1,0:T(8,128)(2,1)S(1)}, u32[]{:S(2)}, u32[]{:S(2)}) async-start(bf16[32,200,128]{2,1,0:T(8,128)(2,1)} %merge.1), calls=%async_computation | async-start | bytes 3276800 | tf_op jit(solution)/shard_map/all_to_all | solution.py:273
  33.2 0.0 copy-done.2
  33.2 30.1 %all-to-all-done.refs_0_ = bf16[32,200,128]{2,1,0:T(8,128)(2,1)S(1)} async-done(((bf16[32,200,128]{2,1,0:T(8,128)(2,1)}), bf16[32,200,128]{2,1,0:T(8,128)(2,1)S(1)}, u32[]{:S(2)}, u32[]{:S(2)}) %all-to-all-start) | async-done | bytes 1638432 | tf_op jit(solution)/shard_map/all_to_all | solution.py:273
  63.3 0.0 copy-done
  63.3 4.1 %update.1 = bf16[8,272,256]{2,1,0:T(8,128)(2,1)S(1)} custom-call(bf16[32,200,128]{2,1,0:T(8,128)(2,1)S(1)} %all-to-all-done.refs_0_, bf16[2048,256]{1,0:T(8,128)(2,1)S(1)} %bitcast.11, f32[16,128]{1,0:T(8,128)S(1)} %reshape.26.refs_2_), custom_call_target="tpu_custom_call" | custom-call | tf_op jit(solution)/shard_map/update/pallas_call | solution.py:274
  67.4 32.7 %all_to_all.15.got_ref = bf16[8,272,256]{2,1,0:T(8,128)(2,1)S(1)} all-to-all(bf16[8,272,256]{2,1,0:T(8,128)(2,1)S(1)} %update.1), channel_id=1, replica_groups=mesh['rep'=8,'yx'=32,'core'=2] {'rep'}, dimensions={0} | all-to-all | bytes 2228224 | tf_op jit(solution)/shard_map/all_to_all | solution.py:282
  100.2 0.6 average.1
  100.8 23.3 %all_to_all.16 = bf16[8,256,256]{2,1,0:T(8,128)(2,1)S(1)} all-to-all(bf16[8,256,256]{2,1,0:T(8,128)(2,1)S(1)} %get-tuple-element.10), channel_id=1, replica_groups=mesh['rep'=8,'yx'=32,'core'=2] {'rep'}, dimensions={0} | all-to-all | bytes 2097152 | tf_op jit(solution)/shard_map/all_to_all | solution.py:294
  124.1 1.0 copy.9
  (1 shorter events, 0.0 us)
Async XLA Ops:
  5.8 15.2 %collective-permute-start = (bf16[32,104,128]{2,1,0:T(8,128)(2,1)}, bf16[32,104,128]{2,1,0:T(8,128)(2,1)S(1)}, u32[]{:S(2)}, u32[]{:S(2)}) collective-permute-start(bf16[32,104,128]{2,1,0:T(8,128)(2,1)} %get-tuple-element.8), channel_id=1, source_target_pairs={{0,1},{1,0},{2,3},{3,2},{4,5},{5,4},{6,7},{7,6},{8,9},{9,8},{10,11... | collective-permute-start | bytes 2555912 | tf_op jit(solution)/shard_map/ppermute | solution.py:252
  7.7 7.8 %collective-permute-start.1 = (bf16[8,128]{1,0:T(8,128)(2,1)}, bf16[8,128]{1,0:T(8,128)(2,1)S(1)}, u32[]{:S(2)}, u32[]{:S(2)}) collective-permute-start(bf16[8,128]{1,0:T(8,128)(2,1)} %get-tuple-element.9), channel_id=1, source_target_pairs={{0,2},{2,4},{4,6},{6,8},{8,10},{10,12},{12,14},{14,16},{16,18},{18... | collective-permute-start | bytes 6152 | tf_op jit(solution)/shard_map/ppermute | solution.py:255
  15.5 5.5 %collective-permute-start.2 = (bf16[8,128]{1,0:T(8,128)(2,1)S(1)}, bf16[8,128]{1,0:T(8,128)(2,1)S(1)}, u32[]{:S(2)}, u32[]{:S(2)}) collective-permute-start(bf16[8,128]{1,0:T(8,128)(2,1)S(1)} %collective-permute-done.1), channel_id=1, source_target_pairs={{0,2},{2,0},{4,6},{6,4},{8,10},{10,8},{12,14},{14,12},{16,18},{18,... | collective-permute-start | bytes 6152 | tf_op jit(solution)/shard_map/ppermute | solution.py:255
  17.5 1.2 copy-start.1
  22.3 10.8 %copy-start.2 = (f32[2,1024]{1,0:T(2,128)S(1)}, f32[2,1024]{1,0:T(2,128)}, u32[]{:S(2)}) copy-start(f32[2,1024]{1,0:T(2,128)} %param.11) | copy-start | bytes 24580
  22.3 40.9 %copy-start = (bf16[2,1024,256]{2,1,0:T(8,128)(2,1)S(1)}, bf16[2,1024,256]{2,1,0:T(8,128)(2,1)}, u32[]{:S(2)}) copy-start(bf16[2,1024,256]{2,1,0:T(8,128)(2,1)} %param.10) | copy-start | bytes 3145732
  22.4 40.9 %all-to-all-start = ((bf16[32,200,128]{2,1,0:T(8,128)(2,1)}), bf16[32,200,128]{2,1,0:T(8,128)(2,1)S(1)}, u32[]{:S(2)}, u32[]{:S(2)}) async-start(bf16[32,200,128]{2,1,0:T(8,128)(2,1)} %merge.1), calls=%async_computation | async-start | bytes 3276800 | tf_op jit(solution)/shard_map/all_to_all | solution.py:273
